TPU v7x, 512 devices: a whole 4x8x8 slice. The times are simulated.
512 devices in a mesh: grp: 2 (over core), kv: 8 (over z), srv: 32 (over x, y).
Axes of the slice: x: 4, y: 8, z: 8, core: 2. Of those that a mesh axis runs over, the one named last changes fastest.
Arguments:
- queries: bfloat16 [8192, 8, 1024], P('srv', 'kv', 'grp'), may hold values from -120 to 120
- keys: bfloat16 [8192, 8, 128], P('srv', 'kv'), may hold values from -5 to 5
- values: bfloat16 [8192, 8, 128], P('srv', 'kv'), may hold values from -6 to 6
- lengths: int32 [16], replicated, may hold values from 1 to 1024, 8192 in all
- output_projection_weight: bfloat16 [8, 1024, 8192], P('kv', 'grp', 'srv'), may hold values from -0.0625 to 0.0625
Outputs:
- projected: bfloat16 [8192, 8192], P('srv', ('grp', 'kv'))
Inputs may be any that keep to these rules, and one draw needn't show every extreme that they name: The 16 lengths sum to 8192; the longest document has exactly 1024 tokens.
All inputs are finite; a program needn't handle non-finite values.
Results may differ from a plain program's by a relative error of at most 0.017.
Values may be sent and summed in bfloat16 or wider, within the bound.
No kernel may reach another device: no remote copies, remote signals or barrier semaphores. Data moves between devices by JAX's collectives and lax.ppermute only.
A program may use at most 64 MiB of HBM per device.

v0:
```python
import math

import jax
import jax.numpy as jnp
from jax import lax
from jax.sharding import PartitionSpec as P

REACH = 4


def from_behind(block, axis, distance):
    devices = range(lax.axis_size(axis))
    route = [(i - distance, i) for i in devices if i - distance in devices]
    return lax.ppermute(block, axis, route)


def sum_by_axis(array, axes, dim):
    if not axes:
        return array
    nearer = lax.psum_scatter(array, axes[0], scatter_dimension=dim, tiled=True)
    return sum_by_axis(nearer, axes[1:], dim)


def doc_starts(lengths, position):
    starts = jnp.cumsum(lengths) - lengths
    chosen = jnp.where(starts[None, :] <= position[:, None], starts[None, :], 0)
    return jnp.max(chosen, axis=1)


def attend(queries, window_keys, window_values, query_pos, key_pos, lengths):
    token_count = queries.shape[0]
    groups = queries.shape[1]
    head_size = window_keys.shape[2]
    heads = queries.shape[2] // head_size
    split_output = queries.reshape(token_count, groups, heads, head_size)
    scores = jnp.einsum(
        "tjhd,wjd->jhtw", split_output, window_keys, preferred_element_type=jnp.float32
    )
    scores = scores * (1.0 / math.sqrt(head_size))
    first_key = doc_starts(lengths, query_pos)
    allowed = (key_pos[None, :] >= first_key[:, None]) & (key_pos[None, :] <= query_pos[:, None])
    scores = jnp.where(allowed[None, None], scores, -jnp.inf)
    peak = jnp.max(scores, axis=3, keepdims=True)
    weights = jnp.exp(scores - peak)
    total = jnp.sum(weights, axis=3)
    numer = jnp.einsum(
        "jhtw,wjd->tjhd",
        weights.astype(jnp.bfloat16),
        window_values,
        preferred_element_type=jnp.float32,
    )
    final_output = numer / jnp.transpose(total, (2, 0, 1))[..., None]
    return final_output.astype(jnp.bfloat16).reshape(token_count, groups * heads * head_size)


def on_device(queries, keys, values, lengths, output_projection_weight):
    token_count = queries.shape[0]
    shard = lax.axis_index("srv")
    stacked = jnp.stack([keys, values])
    arrived = [stacked]
    for distance in range(1, REACH + 1):
        arrived.append(from_behind(stacked, "srv", distance))
    window = jnp.concatenate(arrived[::-1], axis=1)
    query_pos = shard * token_count + jnp.arange(token_count, dtype=jnp.int32)
    key_pos = (shard - REACH) * token_count + jnp.arange(window.shape[1], dtype=jnp.int32)
    attention_output = attend(queries, window[0], window[1], query_pos, key_pos, lengths)
    inner = attention_output.shape[1]
    piece = lax.all_gather(output_projection_weight, "srv", axis=2, tiled=True)
    partial_sum = jnp.dot(
        attention_output, piece.reshape(inner, piece.shape[2]), preferred_element_type=jnp.float32
    )
    summed = sum_by_axis(partial_sum.astype(jnp.bfloat16), ("grp", "kv"), 1).astype(jnp.float32)
    return summed.astype(jnp.bfloat16)


def solution(mesh):
    placed = (
        P("srv", "kv", "grp"),
        P("srv", "kv", None),
        P("srv", "kv", None),
        P(),
        P("kv", "grp", "srv"),
    )
    return jax.shard_map(
        on_device, mesh=mesh, in_specs=placed, out_specs=P("srv", ("grp", "kv")), check_vma=False
    )
```

profile of v0, /device:TPU:6, one launch (start us, length us, event | category | flops | bytes accessed | tf_op | source)
XLA Modules:
  0.0 212.5 jit_solution(3647171846262931791)
XLA Ops:
  6.5 0.0 all-gather.2.cloned.1.call-start
  6.5 0.7 all-gather.2.cloned.1.call-update
  7.3 0.0 reduce-scatter.3.cloned.1.call-start
  7.3 0.9 pad_maximum_fusion
  8.2 7.7 %collective-permute-start = (bf16[2,256,1,128]{3,1,2,0:T(8,128)(2,1)S(1)}, bf16[2,256,1,128]{3,1,2,0:T(8,128)(2,1)S(1)}, u32[]{:S(2)}, u32[]{:S(2)}) collective-permute-start(bf16[2,256,1,128]{3,1,2,0:T(8,128)(2,1)S(1)} %pad_maximum_fusion), channel_id=1, source_target_pairs={{0,4},{1,5},{2,6},{3,7},{4,8},{5,9},{6,10},{7,11},{8,12},{9,13},{1... | collective-permute-start | bytes 393224 | tf_op jit(solution)/shard_map/ppermute | solution.py:14
  15.9 2.8 %collective-permute-start.1 = (bf16[2,256,1,128]{3,1,2,0:T(8,128)(2,1)S(1)}, bf16[2,256,1,128]{3,1,2,0:T(8,128)(2,1)S(1)}, u32[]{:S(2)}, u32[]{:S(2)}) collective-permute-start(bf16[2,256,1,128]{3,1,2,0:T(8,128)(2,1)S(1)} %pad_maximum_fusion), channel_id=1, source_target_pairs={{0,3},{1,4},{2,5},{3,6},{4,7},{5,8},{6,9},{7,10},{8,11},{9,12},{10... | collective-permute-start | bytes 393224 | tf_op jit(solution)/shard_map/ppermute | solution.py:14
  18.8 1.9 collective-permute-start.2
  20.7 2.5 %collective-permute-start.3 = (bf16[2,256,1,128]{3,1,2,0:T(8,128)(2,1)S(1)}, bf16[2,256,1,128]{3,1,2,0:T(8,128)(2,1)S(1)}, u32[]{:S(2)}, u32[]{:S(2)}) collective-permute-start(bf16[2,256,1,128]{3,1,2,0:T(8,128)(2,1)S(1)} %pad_maximum_fusion), channel_id=1, source_target_pairs={{0,1},{1,2},{2,3},{3,4},{4,5},{5,6},{6,7},{7,8},{8,9},{9,10},{10,1... | collective-permute-start | bytes 393224 | tf_op jit(solution)/shard_map/ppermute | solution.py:14
  23.2 0.7 copy.14
  23.9 0.1 reduce.2
  24.1 0.7 sub.15
  24.7 0.1 select_reduce_fusion
  24.8 0.3 compare_and_fusion
  25.1 1.0 reshape.130
  26.2 0.0 collective-permute-done
  26.2 8.5 %collective-permute-done.1 = bf16[2,256,1,128]{3,1,2,0:T(8,128)(2,1)S(1)} collective-permute-done((bf16[2,256,1,128]{3,1,2,0:T(8,128)(2,1)S(1)}, bf16[2,256,1,128]{3,1,2,0:T(8,128)(2,1)S(1)}, u32[]{:S(2)}, u32[]{:S(2)}) %collective-permute-start.1) | collective-permute-done | bytes 131104 | tf_op jit(solution)/shard_map/ppermute | solution.py:14
  34.7 0.0 collective-permute-done.2
  34.7 6.6 %collective-permute-done.3 = bf16[2,256,1,128]{3,1,2,0:T(8,128)(2,1)S(1)} collective-permute-done((bf16[2,256,1,128]{3,1,2,0:T(8,128)(2,1)S(1)}, bf16[2,256,1,128]{3,1,2,0:T(8,128)(2,1)S(1)}, u32[]{:S(2)}, u32[]{:S(2)}) %collective-permute-start.3) | collective-permute-done | bytes 131104 | tf_op jit(solution)/shard_map/ppermute | solution.py:14
  41.4 0.9 constant_dynamic-update-slice_fusion
  42.3 1.0 fusion.17
  43.3 0.7 fusion.1
  44.0 1.0 fusion.13
  45.0 83.1 %all-gather.2.cloned.1.call-done = bf16[1,512,8192]{2,1,0:T(8,128)(2,1)} async-done(((bf16[1,512,256]{2,1,0:T(8,128)(2,1)}), bf16[1,512,8192]{2,1,0:T(8,128)(2,1)}) %all-gather.2.cloned.1.call-update) | async-done | bytes 8388624 | tf_op jit(solution)/shard_map/all_gather | solution.py:68
  128.1 7.7 %convolution_convert_fusion = bf16[256,8192]{1,0:T(8,128)(2,1)} fusion(bf16[256,512]{0,1:T(8,128)(2,1)S(1)} %bitcast.48, bf16[1,512,8192]{2,1,0:T(8,128)(2,1)} %all-gather.2.cloned.1.call-done), kind=kOutput, calls=%fused_computation | convolution fusion | flops 2149580800 | bytes 12845056 | tf_op jit(solution)/shard_map/dot_general | solution.py:69
  135.8 0.0 reduce-scatter.3.cloned.1.call-update
  135.8 0.0 reduce-scatter.5.cloned.1.call-start
  135.9 19.8 %reduce-scatter.3.cloned.1.call-done = bf16[256,4096]{1,0:T(8,128)(2,1)} async-done(((bf16[256,8192]{1,0:T(8,128)(2,1)}), bf16[256,4096]{1,0:T(8,128)(2,1)}) %reduce-scatter.3.cloned.1.call-update) | async-done | bytes 2097168 | tf_op jit(solution)/shard_map/reduce_scatter | solution.py:20
  155.7 0.0 reduce-scatter.5.cloned.1.call-update
  155.7 50.3 %reduce-scatter.5.cloned.1.call-done = bf16[256,512]{1,0:T(8,128)(2,1)} async-done(((bf16[256,4096]{1,0:T(8,128)(2,1)}), bf16[256,512]{1,0:T(8,128)(2,1)}) %reduce-scatter.5.cloned.1.call-update) | async-done | bytes 262160 | tf_op jit(solution)/shard_map/reduce_scatter | solution.py:20
  (7 shorter events, 0.1 us)
Async XLA Ops:
  6.5 121.5 %all-gather.2.cloned.1.call-start = ((), (), s32[]{:S(2)}) async-start(), calls=%async_computation.2 | async-start | bytes 8650752 | tf_op jit(solution)/shard_map/all_gather | solution.py:68
  7.3 148.4 %reduce-scatter.3.cloned.1.call-start = ((), (), s32[]{:S(2)}) async-start(), calls=%async_computation.3 | async-start | bytes 6291456 | tf_op jit(solution)/shard_map/reduce_scatter | solution.py:20
  8.2 18.0 %collective-permute-start = (bf16[2,256,1,128]{3,1,2,0:T(8,128)(2,1)S(1)}, bf16[2,256,1,128]{3,1,2,0:T(8,128)(2,1)S(1)}, u32[]{:S(2)}, u32[]{:S(2)}) collective-permute-start(bf16[2,256,1,128]{3,1,2,0:T(8,128)(2,1)S(1)} %pad_maximum_fusion), channel_id=1, source_target_pairs={{0,4},{1,5},{2,6},{3,7},{4,8},{5,9},{6,10},{7,11},{8,12},{9,13},{1... | collective-permute-start | bytes 393224 | tf_op jit(solution)/shard_map/ppermute | solution.py:14
  15.9 18.7 %collective-permute-start.1 = (bf16[2,256,1,128]{3,1,2,0:T(8,128)(2,1)S(1)}, bf16[2,256,1,128]{3,1,2,0:T(8,128)(2,1)S(1)}, u32[]{:S(2)}, u32[]{:S(2)}) collective-permute-start(bf16[2,256,1,128]{3,1,2,0:T(8,128)(2,1)S(1)} %pad_maximum_fusion), channel_id=1, source_target_pairs={{0,3},{1,4},{2,5},{3,6},{4,7},{5,8},{6,9},{7,10},{8,11},{9,12},{10... | collective-permute-start | bytes 393224 | tf_op jit(solution)/shard_map/ppermute | solution.py:14
  18.8 16.0 %collective-permute-start.2 = (bf16[2,256,1,128]{3,1,2,0:T(8,128)(2,1)S(1)}, bf16[2,256,1,128]{3,1,2,0:T(8,128)(2,1)S(1)}, u32[]{:S(2)}, u32[]{:S(2)}) collective-permute-start(bf16[2,256,1,128]{3,1,2,0:T(8,128)(2,1)S(1)} %pad_maximum_fusion), channel_id=1, source_target_pairs={{0,2},{1,3},{2,4},{3,5},{4,6},{5,7},{6,8},{7,9},{8,10},{9,11},{10,... | collective-permute-start | bytes 393224 | tf_op jit(solution)/shard_map/ppermute | solution.py:14
  20.7 20.7 %collective-permute-start.3 = (bf16[2,256,1,128]{3,1,2,0:T(8,128)(2,1)S(1)}, bf16[2,256,1,128]{3,1,2,0:T(8,128)(2,1)S(1)}, u32[]{:S(2)}, u32[]{:S(2)}) collective-permute-start(bf16[2,256,1,128]{3,1,2,0:T(8,128)(2,1)S(1)} %pad_maximum_fusion), channel_id=1, source_target_pairs={{0,1},{1,2},{2,3},{3,4},{4,5},{5,6},{6,7},{7,8},{8,9},{9,10},{10,1... | collective-permute-start | bytes 393224 | tf_op jit(solution)/shard_map/ppermute | solution.py:14
  135.8 70.1 %reduce-scatter.5.cloned.1.call-start = ((), (), s32[]{:S(2)}) async-start(), calls=%async_computation.4 | async-start | bytes 2359296 | tf_op jit(solution)/shard_map/reduce_scatter | solution.py:20
Sparse Core Ops, SparseCore 0:
  10.4 117.6 all-gather.1
  135.9 19.7 reduce-scatter.2
  158.8 47.1 reduce-scatter.4
where the time goes:
time: 213 us; the launch traced here: 212 us
  waiting for transfers between devices  169 us (79%)
  starting transfers between devices  15 us (7%)
  between operations  13.2 us (6%)
  matrix products  9.71 us (5%)
  other arithmetic  3.71 us (2%)
    all_gather x1, waiting for transfers between devices, on_device(): piece = lax.all_gather(output_projection_weight, 'srv', axis=2, tiled=True)  83.1 us
    reduce_scatter x2, waiting for transfers between devices, sum_by_axis(): nearer = lax.psum_scatter(array, axes[0], scatter_dimension=dim, tiled=True)  70.1 us
    ppermute x4, waiting for transfers between devices, from_behind(): return lax.ppermute(block, axis, route)  15.1 us
    ppermute x4, starting transfers between devices, from_behind(): return lax.ppermute(block, axis, route)  14.9 us
    dot_general x1, matrix products, on_device(): jnp.dot(attention_output, piece.reshape(inner, piece.shape[2]), preferred...  7.73 us
  transfers between devices with their start and end apart: 7, of which 5 were waited for; matrix products, arithmetic and copies ran while one was open for 4% of the time, Pallas kernels for 0%

commit v1 on v0

v1 whole, which is shorter than its diff:
```python
import functools
import math

import jax
import jax.numpy as jnp
from jax import lax
from jax.experimental import pallas as pl
from jax.experimental.pallas import tpu as pltpu
from jax.sharding import PartitionSpec as P

REACH = 4
ALL = ("grp", "kv", "srv")


def doc_starts(lengths, position):
    count = lengths.shape[0]
    before = jnp.arange(count)[None, :] < jnp.arange(count)[:, None]
    starts = jnp.sum(jnp.where(before, lengths[None, :], 0), axis=1)
    chosen = jnp.where(starts[None, :] <= position[:, None], starts[None, :], 0)
    return jnp.max(chosen, axis=1)


def attend(queries, window_keys, window_values, query_pos, key_pos, lengths):
    token_count = queries.shape[0]
    head_size = window_keys.shape[1]
    heads = queries.shape[1] // head_size
    split = queries.reshape(token_count, heads, head_size)
    scores = jnp.einsum("thd,wd->htw", split, window_keys, preferred_element_type=jnp.float32)
    scores = scores * (1.0 / math.sqrt(head_size))
    first_key = doc_starts(lengths, query_pos)
    allowed = (key_pos[None, :] >= first_key[:, None]) & (key_pos[None, :] <= query_pos[:, None])
    scores = jnp.where(allowed[None], scores, -jnp.inf)
    peak = jnp.max(scores, axis=2, keepdims=True)
    weights = jnp.exp(scores - peak)
    total = jnp.sum(weights, axis=2)
    numer = jnp.einsum(
        "htw,wd->thd", weights.astype(jnp.bfloat16), window_values, preferred_element_type=jnp.float32
    )
    result = numer / jnp.transpose(total, (1, 0))[..., None]
    return result.astype(jnp.bfloat16).reshape(token_count, heads * head_size)


def window_of(stacked, core, n_srv):
    def fetch(near):
        route = []
        for c in range(2):
            distance = near + 2 * c
            route += [(c * n_srv + i - distance, c * n_srv + i) for i in range(distance, n_srv)]
        return lax.ppermute(stacked, ("grp", "srv"), route)

    mine = jnp.concatenate([fetch(1), fetch(2)], axis=1)
    other = lax.ppermute(mine, "grp", [(0, 1), (1, 0)])
    window = jnp.concatenate([mine, other, stacked], axis=1)
    behind = jnp.stack([1 + 2 * core, 2 + 2 * core, 3 - 2 * core, 4 - 2 * core, 0 * core])
    return window, behind


def product_kernel(steps, left_ref, right_ref, out_ref, total_ref):
    step = pl.program_id(0)

    @pl.when(step == 0)
    def _():
        total_ref[...] = jnp.zeros_like(total_ref)

    left = left_ref[0]
    width = right_ref.shape[3]
    for half in range(right_ref.shape[0]):
        total_ref[:, half * width : (half + 1) * width] += jnp.dot(
            left, right_ref[half, 0], preferred_element_type=jnp.float32
        )

    @pl.when(step == steps - 1)
    def _():
        out_ref[...] = total_ref[...].astype(out_ref.dtype)


def product(left, right):
    steps, tokens, depth = left.shape
    halves, _, _, width = right.shape
    return pl.pallas_call(
        functools.partial(product_kernel, steps),
        grid=(steps,),
        out_shape=jax.ShapeDtypeStruct((tokens, halves * width), jnp.bfloat16),
        in_specs=[
            pl.BlockSpec((1, tokens, depth), lambda s: (s, 0, 0)),
            pl.BlockSpec((halves, 1, depth, width), lambda s: (0, s, 0, 0)),
        ],
        out_specs=pl.BlockSpec((tokens, halves * width), lambda s: (0, 0)),
        scratch_shapes=[pltpu.VMEM((tokens, halves * width), jnp.float32)],
        compiler_params=pltpu.CompilerParams(vmem_limit_bytes=58 * 2**20),
        cost_estimate=pl.CostEstimate(
            flops=2 * steps * tokens * depth * halves * width,
            bytes_accessed=2 * (left.size + right.size + tokens * halves * width),
            transcendentals=0,
        ),
    )(left, right)


def solution(mesh):
    n_grp, n_kv, n_srv = mesh.shape["grp"], mesh.shape["kv"], mesh.shape["srv"]
    blocks = n_grp * n_kv
    halves = n_srv // blocks

    to_owner = []
    for c in range(n_grp):
        for z in range(n_kv):
            for s in range(n_srv):
                owner = s // halves
                place = (s % halves) * blocks + c * n_kv + z
                to_owner.append(((c * n_kv + z) * n_srv + s, owner * n_srv + place))

    def on_device(queries, keys, values, lengths, weight):
        tokens = queries.shape[0]
        core = lax.axis_index("grp")
        shard = lax.axis_index("srv")
        weight = lax.ppermute(weight[0], ALL, to_owner)
        columns = lax.all_gather(weight, "srv", axis=0, tiled=True)
        columns = columns.reshape(halves, blocks, weight.shape[0], weight.shape[1])

        window, behind = window_of(jnp.stack([keys[:, 0], values[:, 0]]), core, n_srv)
        query_pos = shard * tokens + jnp.arange(tokens, dtype=jnp.int32)
        key_pos = ((shard - behind) * tokens)[:, None] + jnp.arange(tokens, dtype=jnp.int32)[None, :]
        heads = attend(queries[:, 0], window[0], window[1], query_pos, key_pos.reshape(-1), lengths)
        along = lax.all_to_all(jnp.broadcast_to(heads, (n_kv,) + heads.shape), "kv", 0, 0)
        both = lax.all_to_all(jnp.broadcast_to(along, (n_grp,) + along.shape), "grp", 0, 0)
        return product(both.reshape(blocks, tokens, heads.shape[1]), columns)

    placed = (P("srv", "kv", "grp"), P("srv", "kv", None), P("srv", "kv", None), P(), P("kv", "grp", "srv"))
    return jax.shard_map(
        on_device, mesh=mesh, in_specs=placed, out_specs=P("srv", ("grp", "kv")), check_vma=False
    )
```

time: 213 us -> 177 us (0.83)
  waiting for transfers between devices: 169 us -> 34.2 us
  blocking collectives: 0 us -> 73.3 us
  starting transfers between devices: 15 us -> 32.1 us
  Pallas kernels: 0 us -> 13 us
  matrix products: 9.71 us -> 1.98 us
    all_to_all x0 -> x2, blocking collectives: none -> 73.3 us  [the longest x1 65.1 us: on_device(): lax.all_to_all(jnp.broadcast_to(heads, (n_kv,) + heads.shape), 'kv', 0, 0)]
    all_gather x1, waiting for transfers between devices: 83.1 us -> 10.2 us  [on_device(): columns = lax.all_gather(weight, 'srv', axis=0, tiled=True)]
    reduce_scatter x2 -> x0, waiting for transfers between devices: 70.1 us -> none  [sum_by_axis(): nearer = lax.psum_scatter(array, axes[0], scatter_dimension=dim, tiled=True)]
    ppermute x4, starting transfers between devices: 14.9 us -> 32.1 us  [the longest x2 18.9 us: fetch(): return lax.ppermute(stacked, ('grp', 'srv'), route)]
    pallas_call x0 -> x1, Pallas kernels: none -> 13 us  [product(): pl.pallas_call(functools.partial(product_kernel, steps), grid=(steps,), o...]
    ppermute x4, waiting for transfers between devices: 15.1 us -> 24 us  [the longest x1 12.2 us: on_device(): weight = lax.ppermute(weight[0], ALL, to_owner)]
    dot_general x3 -> x2, matrix products: 9.71 us -> 1.98 us  [the longest x1 1.02 us: attend(): jnp.einsum('htw,wd->thd', weights.astype(jnp.bfloat16), window_values, pr...]
  transfers between devices with their start and end apart: 7 -> 5, of which waited for: 5 -> 5; matrix products, arithmetic and copies ran while one was open for 4% -> 4% of each run, Pallas kernels for 0% -> 0%
where the time goes in v1:
time: 177 us; the launch traced here: 174 us
  blocking collectives  73.3 us (41%)
  waiting for transfers between devices  34.2 us (19%)
  starting transfers between devices  32.1 us (18%)
  between operations  13.5 us (8%)
  Pallas kernels  13 us (7%)
  other arithmetic  3.78 us (2%)
  local copies, waits for them, and re-layouts  2.59 us (1%)
  matrix products  1.98 us (1%)
    all_to_all x1, blocking collectives, on_device(): lax.all_to_all(jnp.broadcast_to(heads, (n_kv,) + heads.shape), 'kv', 0, 0)  65.1 us
    ppermute x2, starting transfers between devices, fetch(): return lax.ppermute(stacked, ('grp', 'srv'), route)  18.9 us
    pallas_call x1, Pallas kernels, product(): pl.pallas_call(functools.partial(product_kernel, steps), grid=(steps,), o...  13 us
    ppermute x1, waiting for transfers between devices, on_device(): weight = lax.ppermute(weight[0], ALL, to_owner)  12.2 us
    ppermute x2, waiting for transfers between devices, fetch(): return lax.ppermute(stacked, ('grp', 'srv'), route)  11 us
    ppermute x1, starting transfers between devices, on_device(): weight = lax.ppermute(weight[0], ALL, to_owner)  10.3 us
    all_gather x1, waiting for transfers between devices, on_device(): columns = lax.all_gather(weight, 'srv', axis=0, tiled=True)  10.2 us
    all_to_all x1, blocking collectives, on_device(): lax.all_to_all(jnp.broadcast_to(along, (n_grp,) + along.shape), 'grp', 0, 0)  8.21 us
  transfers between devices with their start and end apart: 5, of which 5 were waited for; matrix products, arithmetic and copies ran while one was open for 4% of the time, Pallas kernels for 0%

profile of v1, /device:TPU:6, one launch (start us, length us, event | category | flops | bytes accessed | tf_op | source)
XLA Modules:
  0.0 174.4 jit_solution(10475711817543206971)
XLA Ops:
  6.5 0.0 all-gather.2.cloned.1.call-start
  6.5 10.3 %collective-permute-start.3 = (bf16[512,256]{1,0:T(8,128)(2,1)}, bf16[512,256]{1,0:T(8,128)(2,1)S(1)}, u32[]{:S(2)}, u32[]{:S(2)}) collective-permute-start(bf16[512,256]{1,0:T(8,128)(2,1)} %bitcast.40), channel_id=1, source_target_pairs={{0,0},{1,16},{2,32},{3,48},{4,64},{5,80},{6,96},{7,112},{8,128},{9... | collective-permute-start | bytes 786440 | tf_op jit(solution)/shard_map/ppermute | solution.py:116
  16.8 12.2 %collective-permute-done.3 = bf16[512,256]{1,0:T(8,128)(2,1)S(1)} collective-permute-done((bf16[512,256]{1,0:T(8,128)(2,1)}, bf16[512,256]{1,0:T(8,128)(2,1)S(1)}, u32[]{:S(2)}, u32[]{:S(2)}) %collective-permute-start.3) | collective-permute-done | bytes 262176 | tf_op jit(solution)/shard_map/ppermute | solution.py:116
  29.0 0.0 copy-start
  29.0 0.7 copy-done
  29.7 0.0 all-gather.2.cloned.1.call-update
  29.7 0.9 pad_maximum_fusion.1
  30.6 2.0 %collective-permute-start = (bf16[2,256,128]{2,1,0:T(8,128)(2,1)S(1)}, bf16[2,256,128]{2,1,0:T(8,128)(2,1)S(1)}, u32[]{:S(2)}, u32[]{:S(2)}) collective-permute-start(bf16[2,256,128]{2,1,0:T(8,128)(2,1)S(1)} %pad_maximum_fusion.1), channel_id=1, source_target_pairs={{0,1},{1,2},{2,3},{3,4},{4,5},{5,6},{6,7},{7,8},{8,9},{9,10},{10,1... | collective-permute-start | bytes 393224 | tf_op jit(solution)/shard_map/ppermute | solution.py:49
  32.6 17.0 %collective-permute-start.1 = (bf16[2,256,128]{2,1,0:T(8,128)(2,1)S(1)}, bf16[2,256,128]{2,1,0:T(8,128)(2,1)S(1)}, u32[]{:S(2)}, u32[]{:S(2)}) collective-permute-start(bf16[2,256,128]{2,1,0:T(8,128)(2,1)S(1)} %pad_maximum_fusion.1), channel_id=1, source_target_pairs={{0,2},{1,3},{2,4},{3,5},{4,6},{5,7},{6,8},{7,9},{8,10},{9,11},{10,... | collective-permute-start | bytes 393224 | tf_op jit(solution)/shard_map/ppermute | solution.py:49
  49.6 0.1 stack.23
  49.7 0.8 select_reduce_fusion.1
  50.5 0.1 iota_add_fusion
  50.5 1.0 reshape_squeeze.3
  51.6 0.1 select_reduce_fusion
  51.6 7.3 %collective-permute-done = bf16[2,256,128]{2,1,0:T(8,128)(2,1)S(1)} collective-permute-done((bf16[2,256,128]{2,1,0:T(8,128)(2,1)S(1)}, bf16[2,256,128]{2,1,0:T(8,128)(2,1)S(1)}, u32[]{:S(2)}, u32[]{:S(2)}) %collective-permute-start) | collective-permute-done | bytes 131104 | tf_op jit(solution)/shard_map/ppermute | solution.py:49
  58.9 3.7 %collective-permute-done.1 = bf16[2,256,128]{2,1,0:T(8,128)(2,1)S(1)} collective-permute-done((bf16[2,256,128]{2,1,0:T(8,128)(2,1)S(1)}, bf16[2,256,128]{2,1,0:T(8,128)(2,1)S(1)}, u32[]{:S(2)}, u32[]{:S(2)}) %collective-permute-start.1) | collective-permute-done | bytes 131104 | tf_op jit(solution)/shard_map/ppermute | solution.py:49
  62.6 2.9 %collective-permute-start.2 = (bf16[2,512,128]{2,1,0:T(8,128)(2,1)S(1)}, bf16[2,512,128]{2,1,0:T(8,128)(2,1)S(1)}, u32[]{:S(2)}, u32[]{:S(2)}) collective-permute-start(bf16[2,512,128]{2,1,0:T(8,128)(2,1)S(1)} %pad_maximum_fusion), channel_id=1, source_target_pairs={{0,256},{256,0},{1,257},{257,1},{2,258},{258,2},{3,259},{259,3},{4... | collective-permute-start | bytes 786440 | tf_op jit(solution)/shard_map/ppermute | solution.py:52
  65.5 0.3 compare_and_fusion
  65.8 0.8 collective-permute-done.2
  66.6 0.9 maximum_maximum_fusion
  67.6 1.0 fusion.15
  68.5 0.7 fusion
  69.2 1.0 fusion.11
  70.3 0.1 copy.13
  70.4 0.2 broadcast_in_dim.58
  70.6 65.1 %all_to_all.10 = bf16[8,256,512]{2,1,0:T(8,128)(2,1)S(1)} all-to-all(bf16[8,256,512]{2,1,0:T(8,128)(2,1)S(1)} %broadcast_in_dim.58), channel_id=1, replica_groups=mesh['grp'=2,'kv'=8,'srv'=32] {'kv'}, dimensions={0} | all-to-all | bytes 4194304 | tf_op jit(solution)/shard_map/all_to_all | solution.py:124
  135.7 0.5 broadcast_in_dim.59
  136.2 8.2 %all_to_all.11 = bf16[2,8,256,512]{3,2,1,0:T(8,128)(2,1)} all-to-all(bf16[2,8,256,512]{3,2,1,0:T(8,128)(2,1)S(1)} %broadcast_in_dim.59), channel_id=1, replica_groups=mesh['grp'=2,'kv'=8,'srv'=32] {'grp'}, dimensions={0} | all-to-all | bytes 8388608 | tf_op jit(solution)/shard_map/all_to_all | solution.py:125
  144.4 10.2 %all-gather.2.cloned.1.call-done = bf16[16384,256]{1,0:T(8,128)(2,1)} async-done(((bf16[512,256]{1,0:T(8,128)(2,1)}), bf16[16384,256]{1,0:T(8,128)(2,1)}) %all-gather.2.cloned.1.call-update) | async-done | bytes 8388624 | tf_op jit(solution)/shard_map/all_gather | solution.py:117
  154.6 13.0 %shard_map.55 = bf16[256,512]{1,0:T(8,128)(2,1)} custom-call(bf16[16,256,512]{2,1,0:T(8,128)(2,1)} %bitcast.32, bf16[2,16,512,256]{3,2,1,0:T(8,128)(2,1)} %bitcast.33), custom_call_target="tpu_custom_call" | custom-call | flops 2147483648 | bytes 12845056 | tf_op jit(solution)/shard_map/pallas_call | solution.py:80
  (4 shorter events, 0.0 us)
Async XLA Ops:
  6.5 148.1 %all-gather.2.cloned.1.call-start = ((), (), s32[]{:S(2)}) async-start(), calls=%async_computation.2 | async-start | bytes 8650752 | tf_op jit(solution)/shard_map/all_gather | solution.py:117
  6.5 22.5 %collective-permute-start.3 = (bf16[512,256]{1,0:T(8,128)(2,1)}, bf16[512,256]{1,0:T(8,128)(2,1)S(1)}, u32[]{:S(2)}, u32[]{:S(2)}) collective-permute-start(bf16[512,256]{1,0:T(8,128)(2,1)} %bitcast.40), channel_id=1, source_target_pairs={{0,0},{1,16},{2,32},{3,48},{4,64},{5,80},{6,96},{7,112},{8,128},{9... | collective-permute-start | bytes 786440 | tf_op jit(solution)/shard_map/ppermute | solution.py:116
  29.0 0.7 copy-start
  30.6 28.3 %collective-permute-start = (bf16[2,256,128]{2,1,0:T(8,128)(2,1)S(1)}, bf16[2,256,128]{2,1,0:T(8,128)(2,1)S(1)}, u32[]{:S(2)}, u32[]{:S(2)}) collective-permute-start(bf16[2,256,128]{2,1,0:T(8,128)(2,1)S(1)} %pad_maximum_fusion.1), channel_id=1, source_target_pairs={{0,1},{1,2},{2,3},{3,4},{4,5},{5,6},{6,7},{7,8},{8,9},{9,10},{10,1... | collective-permute-start | bytes 393224 | tf_op jit(solution)/shard_map/ppermute | solution.py:49
  32.6 30.0 %collective-permute-start.1 = (bf16[2,256,128]{2,1,0:T(8,128)(2,1)S(1)}, bf16[2,256,128]{2,1,0:T(8,128)(2,1)S(1)}, u32[]{:S(2)}, u32[]{:S(2)}) collective-permute-start(bf16[2,256,128]{2,1,0:T(8,128)(2,1)S(1)} %pad_maximum_fusion.1), channel_id=1, source_target_pairs={{0,2},{1,3},{2,4},{3,5},{4,6},{5,7},{6,8},{7,9},{8,10},{9,11},{10,... | collective-permute-start | bytes 393224 | tf_op jit(solution)/shard_map/ppermute | solution.py:49
  62.6 4.0 %collective-permute-start.2 = (bf16[2,512,128]{2,1,0:T(8,128)(2,1)S(1)}, bf16[2,512,128]{2,1,0:T(8,128)(2,1)S(1)}, u32[]{:S(2)}, u32[]{:S(2)}) collective-permute-start(bf16[2,512,128]{2,1,0:T(8,128)(2,1)S(1)} %pad_maximum_fusion), channel_id=1, source_target_pairs={{0,256},{256,0},{1,257},{257,1},{2,258},{258,2},{3,259},{259,3},{4... | collective-permute-start | bytes 786440 | tf_op jit(solution)/shard_map/ppermute | solution.py:52
Sparse Core Ops, SparseCore 0:
  29.9 124.6 all-gather.1

commit v2 on v1

v2 whole, which is shorter than its diff:
```python
import math

import jax
import jax.numpy as jnp
from jax import lax
from jax.experimental import pallas as pl
from jax.experimental.pallas import tpu as pltpu
from jax.sharding import PartitionSpec as P

REACH = 4
ALL = ("grp", "kv", "sx", "sy")
SX = 4


def doc_starts(lengths, position):
    count = lengths.shape[0]
    before = jnp.arange(count)[None, :] < jnp.arange(count)[:, None]
    starts = jnp.sum(jnp.where(before, lengths[None, :], 0), axis=1)
    chosen = jnp.where(starts[None, :] <= position[:, None], starts[None, :], 0)
    return jnp.max(chosen, axis=1)


def attend(queries, window_keys, window_values, query_pos, key_pos, lengths):
    token_count = queries.shape[0]
    head_size = window_keys.shape[1]
    heads = queries.shape[1] // head_size
    split = queries.reshape(token_count, heads, head_size)
    scores = jnp.einsum("thd,wd->htw", split, window_keys, preferred_element_type=jnp.float32)
    scores = scores * (1.0 / math.sqrt(head_size))
    first_key = doc_starts(lengths, query_pos)
    allowed = (key_pos[None, :] >= first_key[:, None]) & (key_pos[None, :] <= query_pos[:, None])
    scores = jnp.where(allowed[None], scores, -jnp.inf)
    peak = jnp.max(scores, axis=2, keepdims=True)
    weights = jnp.exp(scores - peak)
    total = jnp.sum(weights, axis=2)
    numer = jnp.einsum(
        "htw,wd->thd", weights.astype(jnp.bfloat16), window_values, preferred_element_type=jnp.float32
    )
    result = numer / jnp.transpose(total, (1, 0))[..., None]
    return result.astype(jnp.bfloat16).reshape(token_count, heads * head_size)


def window_of(stacked, core, n_srv):
    def fetch(near):
        route = []
        for c in range(2):
            distance = near + 2 * c
            route += [(c * n_srv + i - distance, c * n_srv + i) for i in range(distance, n_srv)]
        return lax.ppermute(stacked, ("grp", "sx", "sy"), route)

    mine = jnp.concatenate([fetch(1), fetch(2)], axis=1)
    other = lax.ppermute(mine, "grp", [(0, 1), (1, 0)])
    window = jnp.concatenate([mine, other, stacked], axis=1)
    behind = jnp.stack([1 + 2 * core, 2 + 2 * core, 3 - 2 * core, 4 - 2 * core, 0 * core])
    return window, behind


def product_kernel(left_ref, right_ref, out_ref):
    right = jnp.concatenate([right_ref[0], right_ref[1]], axis=1)
    for block in range(left_ref.shape[0]):
        out_ref[0, block] = jnp.dot(
            left_ref[block], right, preferred_element_type=jnp.float32
        ).astype(out_ref.dtype)


def product(left, right):
    blocks, tokens, depth = left.shape
    pieces, _, width = right.shape
    tiles = pieces // 2
    return pl.pallas_call(
        product_kernel,
        grid=(tiles,),
        out_shape=jax.ShapeDtypeStruct((tiles, blocks, tokens, 2 * width), jnp.bfloat16),
        in_specs=[
            pl.BlockSpec((blocks, tokens, depth), lambda j: (0, 0, 0)),
            pl.BlockSpec((2, depth, width), lambda j: (j, 0, 0)),
        ],
        out_specs=pl.BlockSpec((1, blocks, tokens, 2 * width), lambda j: (j, 0, 0, 0)),
        compiler_params=pltpu.CompilerParams(vmem_limit_bytes=58 * 2**20),
        cost_estimate=pl.CostEstimate(
            flops=2 * blocks * tokens * depth * pieces * width,
            bytes_accessed=2 * (left.size + right.size + blocks * tokens * pieces * width),
            transcendentals=0,
        ),
    )(left, right)


def solution(mesh):
    n_grp, n_kv, n_srv = mesh.shape["grp"], mesh.shape["kv"], mesh.shape["srv"]
    sy = n_srv // SX
    fine = jax.sharding.Mesh(mesh.devices.reshape(n_grp, n_kv, SX, sy), ALL)
    tiles = n_grp * n_kv // SX

    to_owner = []
    for c in range(n_grp):
        for z in range(n_kv):
            for x in range(SX):
                j, to_x = divmod(z * n_grp + c, SX)
                owner = x * tiles + j
                for y in range(sy):
                    to_owner.append((((c * n_kv + z) * SX + x) * sy + y, (owner * SX + to_x) * sy + y))

    def on_device(queries, keys, values, lengths, weight):
        tokens = queries.shape[0]
        core = lax.axis_index("grp")
        shard = lax.axis_index("sx") * sy + lax.axis_index("sy")
        columns = lax.all_gather(weight[0], "sy", axis=0, tiled=True)
        columns = columns.reshape(sy, weight.shape[1], weight.shape[2])

        window, behind = window_of(jnp.stack([keys[:, 0], values[:, 0]]), core, n_srv)
        query_pos = shard * tokens + jnp.arange(tokens, dtype=jnp.int32)
        key_pos = ((shard - behind) * tokens)[:, None] + jnp.arange(tokens, dtype=jnp.int32)[None, :]
        heads = attend(queries[:, 0], window[0], window[1], query_pos, key_pos.reshape(-1), lengths)
        along = lax.all_to_all(jnp.broadcast_to(heads, (SX,) + heads.shape), "sx", 0, 0)
        partial = product(along, columns)
        partial = partial.reshape(n_kv * n_grp * tokens, partial.shape[3])
        summed = lax.psum_scatter(partial, "kv", scatter_dimension=0, tiled=True)
        summed = lax.all_to_all(summed.reshape(n_grp, tokens, summed.shape[1]), "grp", 0, 0)
        tile = jnp.sum(summed.astype(jnp.float32), axis=0).astype(jnp.bfloat16)
        return lax.ppermute(tile, ALL, to_owner)

    q = P(("sx", "sy"), "kv", "grp")
    k = P(("sx", "sy"), "kv", None)
    placed = (q, k, k, P(), P("kv", "grp", ("sx", "sy")))
    return jax.shard_map(
        on_device, mesh=fine, in_specs=placed, out_specs=P(("sx", "sy"), ("grp", "kv")), check_vma=False
    )
```

time: 177 us -> 163 us (0.921)
  the two profiles are of different devices: /device:TPU:6 before, /device:TPU:129 now
where the time goes in v2:
time: 163 us; the launch traced here: 162 us
  waiting for transfers between devices  93.3 us (57%)
  blocking collectives  26.7 us (16%)
  starting transfers between devices  15.1 us (9%)
  between operations  13.5 us (8%)
  Pallas kernels  5.99 us (4%)
  other arithmetic  3.87 us (2%)
  local copies, waits for them, and re-layouts  2.02 us (1%)
  matrix products  1.99 us (1%)
    reduce_scatter x1, waiting for transfers between devices, on_device(): summed = lax.psum_scatter(partial, 'kv', scatter_dimension=0, tiled=True)  59 us
    ppermute x1, waiting for transfers between devices, on_device(): return lax.ppermute(tile, ALL, to_owner)  28.1 us
    all_to_all x1, blocking collectives, on_device(): lax.all_to_all(jnp.broadcast_to(heads, (SX,) + heads.shape), 'sx', 0, 0)  20.9 us
    ppermute x2, starting transfers between devices, fetch(): return lax.ppermute(stacked, ('grp', 'sx', 'sy'), route)  9.99 us
    pallas_call x1, Pallas kernels, product(): pl.pallas_call(product_kernel, grid=(tiles,), out_shape=jax.ShapeDtypeStr...  5.99 us
    all_to_all x1, blocking collectives, on_device(): lax.all_to_all(summed.reshape(n_grp, tokens, summed.shape[1]), 'grp', 0, 0)  5.84 us
    ppermute x2, waiting for transfers between devices, fetch(): return lax.ppermute(stacked, ('grp', 'sx', 'sy'), route)  3.91 us
  transfers between devices with their start and end apart: 6, of which 5 were waited for; matrix products, arithmetic and copies ran while one was open for 4% of the time, Pallas kernels for 0%

profile of v2, /device:TPU:129, one launch (start us, length us, event | category | flops | bytes accessed | tf_op | source)
XLA Modules:
  0.0 162.5 jit_solution(13518558245084111305)
XLA Ops:
  6.5 0.0 all-gather.3.cloned.1.call-start
  6.5 0.7 all-gather.3.cloned.1.call-update
  7.3 0.0 reduce-scatter.2.cloned.1.call-start
  7.3 0.9 pad_maximum_fusion.1
  8.2 5.2 %collective-permute-start = (bf16[2,256,128]{2,1,0:T(8,128)(2,1)S(1)}, bf16[2,256,128]{2,1,0:T(8,128)(2,1)S(1)}, u32[]{:S(2)}, u32[]{:S(2)}) collective-permute-start(bf16[2,256,128]{2,1,0:T(8,128)(2,1)S(1)} %pad_maximum_fusion.1), channel_id=1, source_target_pairs={{0,1},{1,2},{2,3},{3,4},{4,5},{5,6},{6,7},{7,8},{8,9},{9,10},{10,1... | collective-permute-start | bytes 393224 | tf_op jit(solution)/shard_map/ppermute | solution.py:49
  13.4 4.8 %collective-permute-start.1 = (bf16[2,256,128]{2,1,0:T(8,128)(2,1)S(1)}, bf16[2,256,128]{2,1,0:T(8,128)(2,1)S(1)}, u32[]{:S(2)}, u32[]{:S(2)}) collective-permute-start(bf16[2,256,128]{2,1,0:T(8,128)(2,1)S(1)} %pad_maximum_fusion.1), channel_id=1, source_target_pairs={{0,2},{1,3},{2,4},{3,5},{4,6},{5,7},{6,8},{7,9},{8,10},{9,11},{10,... | collective-permute-start | bytes 393224 | tf_op jit(solution)/shard_map/ppermute | solution.py:49
  18.2 0.1 stack.23
  18.3 0.8 select_reduce_fusion.1
  19.1 0.1 iota_add_fusion
  19.1 1.0 reshape_squeeze.3
  20.2 0.1 select_reduce_fusion
  20.3 0.0 collective-permute-done
  20.3 3.9 %collective-permute-done.1 = bf16[2,256,128]{2,1,0:T(8,128)(2,1)S(1)} collective-permute-done((bf16[2,256,128]{2,1,0:T(8,128)(2,1)S(1)}, bf16[2,256,128]{2,1,0:T(8,128)(2,1)S(1)}, u32[]{:S(2)}, u32[]{:S(2)}) %collective-permute-start.1) | collective-permute-done | bytes 131104 | tf_op jit(solution)/shard_map/ppermute | solution.py:49
  24.2 1.9 %collective-permute-start.2 = (bf16[2,512,128]{2,1,0:T(8,128)(2,1)S(1)}, bf16[2,512,128]{2,1,0:T(8,128)(2,1)S(1)}, u32[]{:S(2)}, u32[]{:S(2)}) collective-permute-start(bf16[2,512,128]{2,1,0:T(8,128)(2,1)S(1)} %pad_maximum_fusion), channel_id=1, source_target_pairs={{0,256},{256,0},{1,257},{257,1},{2,258},{258,2},{3,259},{259,3},{4... | collective-permute-start | bytes 786440 | tf_op jit(solution)/shard_map/ppermute | solution.py:52
  26.1 0.3 compare_and_fusion
  26.4 1.2 collective-permute-done.2
  27.6 0.9 maximum_maximum_fusion
  28.5 1.0 fusion.15
  29.5 0.7 fusion
  30.2 1.0 fusion.11
  31.2 0.1 copy.13
  31.4 0.1 broadcast_in_dim.55
  31.5 20.9 %all_to_all.10.left_ref = bf16[4,256,512]{2,1,0:T(8,128)(2,1)} all-to-all(bf16[4,256,512]{2,1,0:T(8,128)(2,1)S(1)} %broadcast_in_dim.55), channel_id=1, replica_groups=mesh['grp'=2,'kv'=8,'sx'=4,'sy'=8] {'sx'}, dimensions={0} | all-to-all | bytes 2097152 | tf_op jit(solution)/shard_map/all_to_all | solution.py:114
  52.3 0.3 all-gather.3.cloned.1.call-done
  52.6 6.0 %shard_map.55 = bf16[4,4,256,512]{3,2,1,0:T(8,128)(2,1)} custom-call(bf16[4,256,512]{2,1,0:T(8,128)(2,1)} %all_to_all.10.left_ref, bf16[8,512,256]{2,1,0:T(8,128)(2,1)} %bitcast.40), custom_call_target="tpu_custom_call" | custom-call | flops 2147483648 | bytes 7340032 | tf_op jit(solution)/shard_map/pallas_call | solution.py:70
  58.6 0.0 reduce-scatter.2.cloned.1.call-update
  58.7 59.0 %reduce-scatter.2.cloned.1.call-done = bf16[512,512]{1,0:T(8,128)(2,1)} async-done(((bf16[4096,512]{1,0:T(8,128)(2,1)}), bf16[512,512]{1,0:T(8,128)(2,1)}) %reduce-scatter.2.cloned.1.call-update) | async-done | bytes 524304 | tf_op jit(solution)/shard_map/reduce_scatter | solution.py:117
  117.7 5.8 %all_to_all.11 = bf16[2,256,512]{2,1,0:T(8,128)(2,1)S(1)} all-to-all(bf16[2,256,512]{2,1,0:T(8,128)(2,1)} %bitcast.34), channel_id=1, replica_groups=mesh['grp'=2,'kv'=8,'sx'=4,'sy'=8] {'grp'}, dimensions={0} | all-to-all | bytes 1048576 | tf_op jit(solution)/shard_map/all_to_all | solution.py:118
  123.5 0.1 reduce_sum.32
  123.6 3.2 %collective-permute-start.3 = (bf16[256,512]{1,0:T(8,128)(2,1)S(1)}, bf16[256,512]{1,0:T(8,128)(2,1)S(1)}, u32[]{:S(2)}, u32[]{:S(2)}) collective-permute-start(bf16[256,512]{1,0:T(8,128)(2,1)S(1)} %reduce_sum.32), channel_id=1, source_target_pairs={{0,0},{1,1},{2,2},{3,3},{4,4},{5,5},{6,6},{7,7},{8,128},{9,129},{1... | collective-permute-start | bytes 786440 | tf_op jit(solution)/shard_map/ppermute | solution.py:120
  126.8 28.1 %collective-permute-done.3 = bf16[256,512]{1,0:T(8,128)(2,1)S(1)} collective-permute-done((bf16[256,512]{1,0:T(8,128)(2,1)S(1)}, bf16[256,512]{1,0:T(8,128)(2,1)S(1)}, u32[]{:S(2)}, u32[]{:S(2)}) %collective-permute-start.3) | collective-permute-done | bytes 262176 | tf_op jit(solution)/shard_map/ppermute | solution.py:120
  154.9 0.7 copy.22
  (4 shorter events, 0.0 us)
Async XLA Ops:
  6.5 46.1 %all-gather.3.cloned.1.call-start = ((), (), s32[]{:S(2)}) async-start(), calls=%async_computation.4 | async-start | bytes 2359296 | tf_op jit(solution)/shard_map/all_gather | solution.py:107
  7.3 110.4 %reduce-scatter.2.cloned.1.call-start = ((), (), s32[]{:S(2)}) async-start(), calls=%async_computation.3 | async-start | bytes 4718592 | tf_op jit(solution)/shard_map/reduce_scatter | solution.py:117
  8.2 12.1 %collective-permute-start = (bf16[2,256,128]{2,1,0:T(8,128)(2,1)S(1)}, bf16[2,256,128]{2,1,0:T(8,128)(2,1)S(1)}, u32[]{:S(2)}, u32[]{:S(2)}) collective-permute-start(bf16[2,256,128]{2,1,0:T(8,128)(2,1)S(1)} %pad_maximum_fusion.1), channel_id=1, source_target_pairs={{0,1},{1,2},{2,3},{3,4},{4,5},{5,6},{6,7},{7,8},{8,9},{9,10},{10,1... | collective-permute-start | bytes 393224 | tf_op jit(solution)/shard_map/ppermute | solution.py:49
  13.4 10.7 %collective-permute-start.1 = (bf16[2,256,128]{2,1,0:T(8,128)(2,1)S(1)}, bf16[2,256,128]{2,1,0:T(8,128)(2,1)S(1)}, u32[]{:S(2)}, u32[]{:S(2)}) collective-permute-start(bf16[2,256,128]{2,1,0:T(8,128)(2,1)S(1)} %pad_maximum_fusion.1), channel_id=1, source_target_pairs={{0,2},{1,3},{2,4},{3,5},{4,6},{5,7},{6,8},{7,9},{8,10},{9,11},{10,... | collective-permute-start | bytes 393224 | tf_op jit(solution)/shard_map/ppermute | solution.py:49
  24.2 3.4 %collective-permute-start.2 = (bf16[2,512,128]{2,1,0:T(8,128)(2,1)S(1)}, bf16[2,512,128]{2,1,0:T(8,128)(2,1)S(1)}, u32[]{:S(2)}, u32[]{:S(2)}) collective-permute-start(bf16[2,512,128]{2,1,0:T(8,128)(2,1)S(1)} %pad_maximum_fusion), channel_id=1, source_target_pairs={{0,256},{256,0},{1,257},{257,1},{2,258},{258,2},{3,259},{259,3},{4... | collective-permute-start | bytes 786440 | tf_op jit(solution)/shard_map/ppermute | solution.py:52
  123.6 31.3 %collective-permute-start.3 = (bf16[256,512]{1,0:T(8,128)(2,1)S(1)}, bf16[256,512]{1,0:T(8,128)(2,1)S(1)}, u32[]{:S(2)}, u32[]{:S(2)}) collective-permute-start(bf16[256,512]{1,0:T(8,128)(2,1)S(1)} %reduce_sum.32), channel_id=1, source_target_pairs={{0,0},{1,1},{2,2},{3,3},{4,4},{5,5},{6,6},{7,7},{8,128},{9,129},{1... | collective-permute-start | bytes 786440 | tf_op jit(solution)/shard_map/ppermute | solution.py:120
Sparse Core Ops, SparseCore 0:
  9.4 43.1 all-gather.2
  58.8 58.8 reduce-scatter.1

commit v3 on v2

v3 whole, which is shorter than its diff:
```python
import math

import jax
import jax.numpy as jnp
from jax import lax
from jax.experimental import pallas as pl
from jax.experimental.pallas import tpu as pltpu
from jax.sharding import PartitionSpec as P

REACH = 4
ALL = ("grp", "zh", "zl", "sx", "sy")
SX = 4
ZL = 2


def doc_starts(lengths, position):
    count = lengths.shape[0]
    before = jnp.arange(count)[None, :] < jnp.arange(count)[:, None]
    starts = jnp.sum(jnp.where(before, lengths[None, :], 0), axis=1)
    chosen = jnp.where(starts[None, :] <= position[:, None], starts[None, :], 0)
    return jnp.max(chosen, axis=1)


def attend(queries, window_keys, window_values, query_pos, key_pos, lengths):
    token_count = queries.shape[0]
    head_size = window_keys.shape[1]
    heads = queries.shape[1] // head_size
    split = queries.reshape(token_count, heads, head_size)
    scores = jnp.einsum("thd,wd->htw", split, window_keys, preferred_element_type=jnp.float32)
    scores = scores * (1.0 / math.sqrt(head_size))
    first_key = doc_starts(lengths, query_pos)
    allowed = (key_pos[None, :] >= first_key[:, None]) & (key_pos[None, :] <= query_pos[:, None])
    scores = jnp.where(allowed[None], scores, -jnp.inf)
    peak = jnp.max(scores, axis=2, keepdims=True)
    weights = jnp.exp(scores - peak)
    total = jnp.sum(weights, axis=2)
    numer = jnp.einsum(
        "htw,wd->thd", weights.astype(jnp.bfloat16), window_values, preferred_element_type=jnp.float32
    )
    result = numer / jnp.transpose(total, (1, 0))[..., None]
    return result.astype(jnp.bfloat16).reshape(token_count, heads * head_size)


def window_of(stacked, core, n_srv):
    def fetch(near):
        route = []
        for c in range(2):
            distance = near + 2 * c
            route += [(c * n_srv + i - distance, c * n_srv + i) for i in range(distance, n_srv)]
        return lax.ppermute(stacked, ("grp", "sx", "sy"), route)

    mine = jnp.concatenate([fetch(1), fetch(2)], axis=1)
    other = lax.ppermute(mine, "grp", [(0, 1), (1, 0)])
    window = jnp.concatenate([mine, other, stacked], axis=1)
    behind = jnp.stack([1 + 2 * core, 2 + 2 * core, 3 - 2 * core, 4 - 2 * core, 0 * core])
    return window, behind


def product_kernel(left_ref, right_ref, out_ref):
    cores, pairs = left_ref.shape[:2]
    left = jnp.concatenate([left_ref[c, z, 0] for z in range(pairs) for c in range(cores)], axis=1)
    halves, parts, depth, width = right_ref.shape
    for half in range(halves):
        out_ref[0, :, half * width : (half + 1) * width] = jnp.dot(
            left, right_ref[half].reshape(parts * depth, width), preferred_element_type=jnp.float32
        ).astype(out_ref.dtype)


def product(left, right):
    cores, pairs, blocks, tokens, depth = left.shape
    halves, parts, _, width = right.shape
    return pl.pallas_call(
        product_kernel,
        grid=(blocks,),
        out_shape=jax.ShapeDtypeStruct((blocks, tokens, halves * width), jnp.bfloat16),
        in_specs=[
            pl.BlockSpec((cores, pairs, 1, tokens, depth), lambda i: (0, 0, i, 0, 0)),
            pl.BlockSpec((halves, parts, depth, width), lambda i: (0, 0, 0, 0)),
        ],
        out_specs=pl.BlockSpec((1, tokens, halves * width), lambda i: (i, 0, 0)),
        compiler_params=pltpu.CompilerParams(vmem_limit_bytes=58 * 2**20),
        cost_estimate=pl.CostEstimate(
            flops=2 * left.size * halves * width,
            bytes_accessed=2 * (left.size + right.size + blocks * tokens * halves * width),
            transcendentals=0,
        ),
    )(left, right)


def solution(mesh):
    n_grp, n_kv, n_srv = mesh.shape["grp"], mesh.shape["kv"], mesh.shape["srv"]
    sy, zh = n_srv // SX, n_kv // ZL
    sizes = (n_grp, zh, ZL, SX, sy)
    fine = jax.sharding.Mesh(mesh.devices.reshape(sizes), ALL)

    def index(*place):
        total = 0
        for at, size in zip(place, sizes):
            total = total * size + at
        return total

    to_ring, to_owner = [], []
    for c in range(n_grp):
        for hi in range(zh):
            for lo in range(ZL):
                for x in range(SX):
                    for y in range(sy):
                        a, z = divmod((x * sy + y) // 2, n_kv)
                        g, w = divmod(z // 2, ZL)
                        ring = index(g, hi, w, 2 * a + z % 2, (y % 2) * 4 + lo * 2 + c)
                        to_ring.append((index(c, hi, lo, x, y), ring))
                        z = 2 * (c * ZL + lo) + x % 2
                        owner = index(x // 2, z // ZL, z % ZL, hi, y)
                        to_owner.append((index(c, hi, lo, x, y), owner))

    def on_device(queries, keys, values, lengths, weight):
        tokens = queries.shape[0]
        core = lax.axis_index("grp")
        shard = lax.axis_index("sx") * sy + lax.axis_index("sy")
        weight = lax.ppermute(weight[0], ALL, to_ring)
        columns = lax.all_gather(weight, "sy", axis=0, tiled=True)
        columns = columns.reshape(2, ZL * n_grp, weight.shape[0], weight.shape[1])

        window, behind = window_of(jnp.stack([keys[:, 0], values[:, 0]]), core, n_srv)
        query_pos = shard * tokens + jnp.arange(tokens, dtype=jnp.int32)
        key_pos = ((shard - behind) * tokens)[:, None] + jnp.arange(tokens, dtype=jnp.int32)[None, :]
        heads = attend(queries[:, 0], window[0], window[1], query_pos, key_pos.reshape(-1), lengths)
        along = lax.all_to_all(jnp.broadcast_to(heads, (ZL * SX,) + heads.shape), ("zl", "sx"), 0, 0)
        both = lax.all_to_all(jnp.broadcast_to(along, (n_grp,) + along.shape), "grp", 0, 0)
        partial = product(both.reshape((n_grp, ZL, SX) + heads.shape), columns)
        parts = lax.all_to_all(partial, "zh", 0, 0)
        tile = jnp.sum(parts.astype(jnp.float32), axis=0).astype(jnp.bfloat16)
        return lax.ppermute(tile, ALL, to_owner)

    q = P(("sx", "sy"), ("zh", "zl"), "grp")
    k = P(("sx", "sy"), ("zh", "zl"), None)
    placed = (q, k, k, P(), P(("zh", "zl"), "grp", ("sx", "sy")))
    return jax.shard_map(
        on_device, mesh=fine, in_specs=placed, out_specs=P(("sx", "sy"), ("grp", "zh", "zl")), check_vma=False
    )
```

time: 163 us -> 157 us (0.963)
  the two profiles are of different devices: /device:TPU:129 before, /device:TPU:6 now
where the time goes in v3:
time: 157 us; the launch traced here: 154 us
  waiting for transfers between devices  61.7 us (39%)
  blocking collectives  31.5 us (20%)
  starting transfers between devices  28.8 us (18%)
  between operations  13.5 us (9%)
  local copies, waits for them, and re-layouts  6.56 us (4%)
  Pallas kernels  6.21 us (4%)
  other arithmetic  4.03 us (3%)
  matrix products  1.99 us (1%)
    all_to_all x1, blocking collectives, on_device(): parts = lax.all_to_all(partial, 'zh', 0, 0)  31.5 us
    all_to_all x1, waiting for transfers between devices, on_device(): lax.all_to_all(jnp.broadcast_to(heads, (ZL * SX,) + heads.shape), ('zl',...  24.5 us
    all_gather x1, waiting for transfers between devices, on_device(): columns = lax.all_gather(weight, 'sy', axis=0, tiled=True)  19 us
    ppermute x1, waiting for transfers between devices, on_device(): return lax.ppermute(tile, ALL, to_owner)  13.4 us
    ppermute x2, starting transfers between devices, fetch(): return lax.ppermute(stacked, ('grp', 'sx', 'sy'), route)  7.98 us
    all_to_all x1, starting transfers between devices, on_device(): lax.all_to_all(jnp.broadcast_to(heads, (ZL * SX,) + heads.shape), ('zl',...  6.5 us
    pallas_call x1, Pallas kernels, product(): pl.pallas_call(product_kernel, grid=(blocks,), out_shape=jax.ShapeDtypeSt...  6.21 us
    all_to_all x1, starting transfers between devices, on_device(): lax.all_to_all(jnp.broadcast_to(along, (n_grp,) + along.shape), 'grp', 0, 0)  5.62 us
  transfers between devices with their start and end apart: 8, of which 5 were waited for; matrix products, arithmetic and copies ran while one was open for 7% of the time, Pallas kernels for 0%

profile of v3, /device:TPU:6, one launch (start us, length us, event | category | flops | bytes accessed | tf_op | source)
XLA Modules:
  0.0 154.2 jit_solution(13814818038434810807)
XLA Ops:
  6.5 0.9 pad_maximum_fusion.1
  7.4 3.5 %collective-permute-start = (bf16[2,256,128]{2,1,0:T(8,128)(2,1)S(1)}, bf16[2,256,128]{2,1,0:T(8,128)(2,1)S(1)}, u32[]{:S(2)}, u32[]{:S(2)}) collective-permute-start(bf16[2,256,128]{2,1,0:T(8,128)(2,1)S(1)} %pad_maximum_fusion.1), channel_id=1, source_target_pairs={{0,1},{1,2},{2,3},{3,4},{4,5},{5,6},{6,7},{7,8},{8,9},{9,10},{10,1... | collective-permute-start | bytes 393224 | tf_op jit(solution)/shard_map/ppermute | solution.py:50
  10.9 4.5 %collective-permute-start.1 = (bf16[2,256,128]{2,1,0:T(8,128)(2,1)S(1)}, bf16[2,256,128]{2,1,0:T(8,128)(2,1)S(1)}, u32[]{:S(2)}, u32[]{:S(2)}) collective-permute-start(bf16[2,256,128]{2,1,0:T(8,128)(2,1)S(1)} %pad_maximum_fusion.1), channel_id=1, source_target_pairs={{0,2},{1,3},{2,4},{3,5},{4,6},{5,7},{6,8},{7,9},{8,10},{9,11},{10,... | collective-permute-start | bytes 393224 | tf_op jit(solution)/shard_map/ppermute | solution.py:50
  15.4 4.2 %collective-permute-start.3 = (bf16[512,256]{1,0:T(8,128)(2,1)}, bf16[512,256]{1,0:T(8,128)(2,1)S(1)}, u32[]{:S(2)}, u32[]{:S(2)}) collective-permute-start(bf16[512,256]{1,0:T(8,128)(2,1)} %bitcast.39), channel_id=1, source_target_pairs={{0,0},{1,4},{2,8},{3,12},{4,32},{5,36},{6,40},{7,44},{8,256},{9,26... | collective-permute-start | bytes 786440 | tf_op jit(solution)/shard_map/ppermute | solution.py:120
  19.6 0.1 stack.23
  19.7 0.1 iota_add_fusion
  19.8 0.8 select_reduce_fusion.1
  20.6 1.0 reshape_squeeze.3
  21.6 0.1 select_reduce_fusion
  21.7 0.0 collective-permute-done
  21.7 3.9 %collective-permute-done.1 = bf16[2,256,128]{2,1,0:T(8,128)(2,1)S(1)} collective-permute-done((bf16[2,256,128]{2,1,0:T(8,128)(2,1)S(1)}, bf16[2,256,128]{2,1,0:T(8,128)(2,1)S(1)}, u32[]{:S(2)}, u32[]{:S(2)}) %collective-permute-start.1) | collective-permute-done | bytes 131104 | tf_op jit(solution)/shard_map/ppermute | solution.py:50
  25.6 2.6 %collective-permute-start.2 = (bf16[2,512,128]{2,1,0:T(8,128)(2,1)S(1)}, bf16[2,512,128]{2,1,0:T(8,128)(2,1)S(1)}, u32[]{:S(2)}, u32[]{:S(2)}) collective-permute-start(bf16[2,512,128]{2,1,0:T(8,128)(2,1)S(1)} %pad_maximum_fusion), channel_id=1, source_target_pairs={{0,256},{256,0},{1,257},{257,1},{2,258},{258,2},{3,259},{259,3},{4... | collective-permute-start | bytes 786440 | tf_op jit(solution)/shard_map/ppermute | solution.py:53
  28.2 0.3 compare_and_fusion
  28.5 0.8 collective-permute-done.2
  29.3 0.9 maximum_maximum_fusion
  30.2 1.0 fusion.15
  31.2 0.7 fusion
  31.9 1.0 fusion.11
  33.0 0.1 copy.13
  33.1 1.5 broadcast_in_dim.58
  34.6 6.5 %all-to-all-start = ((bf16[8,256,512]{2,1,0:T(8,128)(2,1)}), bf16[8,256,512]{2,1,0:T(8,128)(2,1)S(1)}, u32[]{:S(2)}, u32[]{:S(2)}) async-start(bf16[8,256,512]{2,1,0:T(8,128)(2,1)} %broadcast_in_dim.58), calls=%async_computation | async-start | bytes 4194304 | tf_op jit(solution)/shard_map/all_to_all | solution.py:128
  41.1 0.0 all-gather.2.cloned.1.call-start
  41.1 0.0 collective-permute-done.3
  41.1 0.0 copy-start
  41.2 0.7 copy-done
  41.8 0.0 all-gather.2.cloned.1.call-update
  41.9 24.5 %all-to-all-done = bf16[8,256,512]{2,1,0:T(8,128)(2,1)S(1)} async-done(((bf16[8,256,512]{2,1,0:T(8,128)(2,1)}), bf16[8,256,512]{2,1,0:T(8,128)(2,1)S(1)}, u32[]{:S(2)}, u32[]{:S(2)}) %all-to-all-start) | async-done | bytes 2097184 | tf_op jit(solution)/shard_map/all_to_all | solution.py:128
  66.3 2.4 %broadcast_in_dim.59 = bf16[2,8,256,512]{3,2,1,0:T(8,128)(2,1)} broadcast(bf16[8,256,512]{2,1,0:T(8,128)(2,1)S(1)} %all-to-all-done), dimensions={1,2,3} | broadcast | bytes 6291456 | tf_op jit(solution)/shard_map/broadcast_in_dim | solution.py:129
  68.7 5.6 %all-to-all-start.1 = ((bf16[2,8,256,512]{3,2,1,0:T(8,128)(2,1)}), bf16[2,8,256,512]{3,2,1,0:T(8,128)(2,1)}, u32[]{:S(2)}, u32[]{:S(2)}) async-start(bf16[2,8,256,512]{3,2,1,0:T(8,128)(2,1)} %broadcast_in_dim.59), calls=%async_computation.1 | async-start | bytes 8388608 | tf_op jit(solution)/shard_map/all_to_all | solution.py:129
  74.4 19.0 %all-gather.2.cloned.1.call-done = bf16[4096,256]{1,0:T(8,128)(2,1)} async-done(((bf16[512,256]{1,0:T(8,128)(2,1)}), bf16[4096,256]{1,0:T(8,128)(2,1)}) %all-gather.2.cloned.1.call-update) | async-done | bytes 2097168 | tf_op jit(solution)/shard_map/all_gather | solution.py:121
  93.4 0.0 all-to-all-done.1
  93.4 6.2 %shard_map.55 = bf16[4,256,512]{2,1,0:T(8,128)(2,1)} custom-call(bf16[2,2,4,256,512]{4,3,2,1,0:T(8,128)(2,1)} %bitcast.14.left_ref, bf16[2,4,512,256]{3,2,1,0:T(8,128)(2,1)} %bitcast.38), custom_call_target="tpu_custom_call" | custom-call | flops 2147483648 | bytes 7340032 | tf_op jit(solution)/shard_map/pallas_call | solution.py:72
  99.6 31.5 %all_to_all.15 = bf16[4,256,512]{2,1,0:T(8,128)(2,1)S(1)} all-to-all(bf16[4,256,512]{2,1,0:T(8,128)(2,1)} %shard_map.55), channel_id=1, replica_groups=mesh['grp'=2,'zh'=4,'zl'=2,'sx'=4,'sy'=8] {'zh'}, dimensions={0} | all-to-all | bytes 2097152 | tf_op jit(solution)/shard_map/all_to_all | solution.py:131
  131.1 0.2 reduce_sum.32
  131.3 1.9 %collective-permute-start.4 = (bf16[256,512]{1,0:T(8,128)(2,1)S(1)}, bf16[256,512]{1,0:T(8,128)(2,1)S(1)}, u32[]{:S(2)}, u32[]{:S(2)}) collective-permute-start(bf16[256,512]{1,0:T(8,128)(2,1)S(1)} %reduce_sum.32), channel_id=1, source_target_pairs={{0,0},{1,1},{2,2},{3,3},{4,4},{5,5},{6,6},{7,7},{8,32},{9,33},{10,... | collective-permute-start | bytes 786440 | tf_op jit(solution)/shard_map/ppermute | solution.py:133
  133.2 13.4 %collective-permute-done.4 = bf16[256,512]{1,0:T(8,128)(2,1)S(1)} collective-permute-done((bf16[256,512]{1,0:T(8,128)(2,1)S(1)}, bf16[256,512]{1,0:T(8,128)(2,1)S(1)}, u32[]{:S(2)}, u32[]{:S(2)}) %collective-permute-start.4) | collective-permute-done | bytes 262176 | tf_op jit(solution)/shard_map/ppermute | solution.py:133
  146.7 0.7 copy.22
  (4 shorter events, 0.0 us)
Async XLA Ops:
  7.4 14.3 %collective-permute-start = (bf16[2,256,128]{2,1,0:T(8,128)(2,1)S(1)}, bf16[2,256,128]{2,1,0:T(8,128)(2,1)S(1)}, u32[]{:S(2)}, u32[]{:S(2)}) collective-permute-start(bf16[2,256,128]{2,1,0:T(8,128)(2,1)S(1)} %pad_maximum_fusion.1), channel_id=1, source_target_pairs={{0,1},{1,2},{2,3},{3,4},{4,5},{5,6},{6,7},{7,8},{8,9},{9,10},{10,1... | collective-permute-start | bytes 393224 | tf_op jit(solution)/shard_map/ppermute | solution.py:50
  10.9 14.7 %collective-permute-start.1 = (bf16[2,256,128]{2,1,0:T(8,128)(2,1)S(1)}, bf16[2,256,128]{2,1,0:T(8,128)(2,1)S(1)}, u32[]{:S(2)}, u32[]{:S(2)}) collective-permute-start(bf16[2,256,128]{2,1,0:T(8,128)(2,1)S(1)} %pad_maximum_fusion.1), channel_id=1, source_target_pairs={{0,2},{1,3},{2,4},{3,5},{4,6},{5,7},{6,8},{7,9},{8,10},{9,11},{10,... | collective-permute-start | bytes 393224 | tf_op jit(solution)/shard_map/ppermute | solution.py:50
  15.4 25.7 %collective-permute-start.3 = (bf16[512,256]{1,0:T(8,128)(2,1)}, bf16[512,256]{1,0:T(8,128)(2,1)S(1)}, u32[]{:S(2)}, u32[]{:S(2)}) collective-permute-start(bf16[512,256]{1,0:T(8,128)(2,1)} %bitcast.39), channel_id=1, source_target_pairs={{0,0},{1,4},{2,8},{3,12},{4,32},{5,36},{6,40},{7,44},{8,256},{9,26... | collective-permute-start | bytes 786440 | tf_op jit(solution)/shard_map/ppermute | solution.py:120
  25.6 3.7 %collective-permute-start.2 = (bf16[2,512,128]{2,1,0:T(8,128)(2,1)S(1)}, bf16[2,512,128]{2,1,0:T(8,128)(2,1)S(1)}, u32[]{:S(2)}, u32[]{:S(2)}) collective-permute-start(bf16[2,512,128]{2,1,0:T(8,128)(2,1)S(1)} %pad_maximum_fusion), channel_id=1, source_target_pairs={{0,256},{256,0},{1,257},{257,1},{2,258},{258,2},{3,259},{259,3},{4... | collective-permute-start | bytes 786440 | tf_op jit(solution)/shard_map/ppermute | solution.py:53
  34.6 31.7 %all-to-all-start = ((bf16[8,256,512]{2,1,0:T(8,128)(2,1)}), bf16[8,256,512]{2,1,0:T(8,128)(2,1)S(1)}, u32[]{:S(2)}, u32[]{:S(2)}) async-start(bf16[8,256,512]{2,1,0:T(8,128)(2,1)} %broadcast_in_dim.58), calls=%async_computation | async-start | bytes 4194304 | tf_op jit(solution)/shard_map/all_to_all | solution.py:128
  41.1 52.3 %all-gather.2.cloned.1.call-start = ((), (), s32[]{:S(2)}) async-start(), calls=%async_computation.3 | async-start | bytes 2359296 | tf_op jit(solution)/shard_map/all_gather | solution.py:121
  41.1 0.7 copy-start
  68.7 24.7 %all-to-all-start.1 = ((bf16[2,8,256,512]{3,2,1,0:T(8,128)(2,1)}), bf16[2,8,256,512]{3,2,1,0:T(8,128)(2,1)}, u32[]{:S(2)}, u32[]{:S(2)}) async-start(bf16[2,8,256,512]{3,2,1,0:T(8,128)(2,1)} %broadcast_in_dim.59), calls=%async_computation.1 | async-start | bytes 8388608 | tf_op jit(solution)/shard_map/all_to_all | solution.py:129
  131.3 15.4 %collective-permute-start.4 = (bf16[256,512]{1,0:T(8,128)(2,1)S(1)}, bf16[256,512]{1,0:T(8,128)(2,1)S(1)}, u32[]{:S(2)}, u32[]{:S(2)}) collective-permute-start(bf16[256,512]{1,0:T(8,128)(2,1)S(1)} %reduce_sum.32), channel_id=1, source_target_pairs={{0,0},{1,1},{2,2},{3,3},{4,4},{5,5},{6,6},{7,7},{8,32},{9,33},{10,... | collective-permute-start | bytes 786440 | tf_op jit(solution)/shard_map/ppermute | solution.py:133
Sparse Core Ops, SparseCore 0:
  44.0 49.3 all-gather.1

commit v4 on v3

--- a/solution.py
+++ b/solution.py
@@ -41,24 +41,18 @@
     return result.astype(jnp.bfloat16).reshape(token_count, heads * head_size)
 
 
-def window_of(stacked, core, n_srv):
-    def fetch(near):
-        route = []
-        for c in range(2):
-            distance = near + 2 * c
-            route += [(c * n_srv + i - distance, c * n_srv + i) for i in range(distance, n_srv)]
-        return lax.ppermute(stacked, ("grp", "sx", "sy"), route)
-
-    mine = jnp.concatenate([fetch(1), fetch(2)], axis=1)
-    other = lax.ppermute(mine, "grp", [(0, 1), (1, 0)])
-    window = jnp.concatenate([mine, other, stacked], axis=1)
-    behind = jnp.stack([1 + 2 * core, 2 + 2 * core, 3 - 2 * core, 4 - 2 * core, 0 * core])
-    return window, behind
+def fetch_behind(stacked, near, n_srv):
+    route = []
+    for c in range(2):
+        distance = near + 2 * c
+        route += [(c * n_srv + i - distance, c * n_srv + i) for i in range(distance, n_srv)]
+    return lax.ppermute(stacked, ("grp", "sx", "sy"), route)
 
 
-def product_kernel(left_ref, right_ref, out_ref):
-    cores, pairs = left_ref.shape[:2]
-    left = jnp.concatenate([left_ref[c, z, 0] for z in range(pairs) for c in range(cores)], axis=1)
+def product_kernel(own_ref, other_ref, right_ref, out_ref):
+    left = jnp.concatenate(
+        [ref[z, 0] for z in range(own_ref.shape[0]) for ref in (own_ref, other_ref)], axis=1
+    )
     halves, parts, depth, width = right_ref.shape
     for half in range(halves):
         out_ref[0, :, half * width : (half + 1) * width] = jnp.dot(
@@ -66,25 +60,23 @@
         ).astype(out_ref.dtype)
 
 
-def product(left, right):
-    cores, pairs, blocks, tokens, depth = left.shape
+def product(own, other, right):
+    pairs, blocks, tokens, depth = own.shape
     halves, parts, _, width = right.shape
+    heads = pl.BlockSpec((pairs, 1, tokens, depth), lambda i: (0, i, 0, 0))
     return pl.pallas_call(
         product_kernel,
         grid=(blocks,),
         out_shape=jax.ShapeDtypeStruct((blocks, tokens, halves * width), jnp.bfloat16),
-        in_specs=[
-            pl.BlockSpec((cores, pairs, 1, tokens, depth), lambda i: (0, 0, i, 0, 0)),
-            pl.BlockSpec((halves, parts, depth, width), lambda i: (0, 0, 0, 0)),
-        ],
+        in_specs=[heads, heads, pl.BlockSpec((halves, parts, depth, width), lambda i: (0, 0, 0, 0))],
         out_specs=pl.BlockSpec((1, tokens, halves * width), lambda i: (i, 0, 0)),
         compiler_params=pltpu.CompilerParams(vmem_limit_bytes=58 * 2**20),
         cost_estimate=pl.CostEstimate(
-            flops=2 * left.size * halves * width,
-            bytes_accessed=2 * (left.size + right.size + blocks * tokens * halves * width),
+            flops=4 * own.size * halves * width,
+            bytes_accessed=2 * (2 * own.size + right.size + blocks * tokens * halves * width),
             transcendentals=0,
         ),
-    )(left, right)
+    )(own, other, right)
 
 
 def solution(mesh):
@@ -107,7 +99,7 @@
                     for y in range(sy):
                         a, z = divmod((x * sy + y) // 2, n_kv)
                         g, w = divmod(z // 2, ZL)
-                        ring = index(g, hi, w, 2 * a + z % 2, (y % 2) * 4 + lo * 2 + c)
+                        ring = index(g, hi, w, 2 * a + z % 2, (y % 2) * 4 + lo * 2 + (c ^ g))
                         to_ring.append((index(c, hi, lo, x, y), ring))
                         z = 2 * (c * ZL + lo) + x % 2
                         owner = index(x // 2, z // ZL, z % ZL, hi, y)
@@ -117,17 +109,29 @@
         tokens = queries.shape[0]
         core = lax.axis_index("grp")
         shard = lax.axis_index("sx") * sy + lax.axis_index("sy")
+        stacked = jnp.stack([keys[:, 0], values[:, 0]])
+        mine = jnp.concatenate([fetch_behind(stacked, 1, n_srv), fetch_behind(stacked, 2, n_srv)], axis=1)
         weight = lax.ppermute(weight[0], ALL, to_ring)
+        mine, weight = lax.optimization_barrier((mine, weight))
         columns = lax.all_gather(weight, "sy", axis=0, tiled=True)
         columns = columns.reshape(2, ZL * n_grp, weight.shape[0], weight.shape[1])
 
-        window, behind = window_of(jnp.stack([keys[:, 0], values[:, 0]]), core, n_srv)
-        query_pos = shard * tokens + jnp.arange(tokens, dtype=jnp.int32)
-        key_pos = ((shard - behind) * tokens)[:, None] + jnp.arange(tokens, dtype=jnp.int32)[None, :]
-        heads = attend(queries[:, 0], window[0], window[1], query_pos, key_pos.reshape(-1), lengths)
-        along = lax.all_to_all(jnp.broadcast_to(heads, (ZL * SX,) + heads.shape), ("zl", "sx"), 0, 0)
-        both = lax.all_to_all(jnp.broadcast_to(along, (n_grp,) + along.shape), "grp", 0, 0)
-        partial = product(both.reshape((n_grp, ZL, SX) + heads.shape), columns)
+        def gather_heads(queries, stacked, mine, lengths):
+            window = jnp.concatenate([mine, lax.ppermute(mine, "grp", [(0, 1), (1, 0)]), stacked], axis=1)
+            behind = jnp.stack([1 + 2 * core, 2 + 2 * core, 3 - 2 * core, 4 - 2 * core, 0 * core])
+            query_pos = shard * tokens + jnp.arange(tokens, dtype=jnp.int32)
+            key_pos = ((shard - behind) * tokens)[:, None] + jnp.arange(tokens, dtype=jnp.int32)[None, :]
+            heads = attend(queries, window[0], window[1], query_pos, key_pos.reshape(-1), lengths)
+            along = lax.all_to_all(jnp.broadcast_to(heads, (ZL * SX,) + heads.shape), ("zl", "sx"), 0, 0)
+            own = along.reshape((ZL, SX) + heads.shape)
+            return own, lax.ppermute(own, "grp", [(0, 1), (1, 0)])
+
+        def nothing(queries, stacked, mine, lengths):
+            empty = jnp.zeros((ZL, SX) + queries.shape, queries.dtype)
+            return empty, empty
+
+        own, other = lax.cond(lengths[0] > 0, gather_heads, nothing, queries[:, 0], stacked, mine, lengths)
+        partial = product(own, other, columns)
         parts = lax.all_to_all(partial, "zh", 0, 0)
         tile = jnp.sum(parts.astype(jnp.float32), axis=0).astype(jnp.bfloat16)
         return lax.ppermute(tile, ALL, to_owner)

time: 157 us -> 150 us (0.955)
  the two profiles are of different devices: /device:TPU:6 before, /device:TPU:4 now
where the time goes in v4:
time: 150 us; the launch traced here: 149 us
  blocking collectives  67.5 us (45%)
  waiting for transfers between devices  33.8 us (23%)
  starting transfers between devices  19.5 us (13%)
  between operations  14.1 us (9%)
  Pallas kernels  6.19 us (4%)
  other arithmetic  3.12 us (2%)
  local copies, waits for them, and re-layouts  2.96 us (2%)
  matrix products  1.96 us (1%)
    all_to_all x1, blocking collectives, on_device(): parts = lax.all_to_all(partial, 'zh', 0, 0)  36.4 us
    all_to_all x1, blocking collectives, gather_heads(): lax.all_to_all(jnp.broadcast_to(heads, (ZL * SX,) + heads.shape), ('zl',...  31.1 us
    ppermute x1, waiting for transfers between devices, on_device(): return lax.ppermute(tile, ALL, to_owner)  14.3 us
    ppermute x2, waiting for transfers between devices, fetch_behind(): return lax.ppermute(stacked, ('grp', 'sx', 'sy'), route)  13.9 us
    ppermute x2, starting transfers between devices, fetch_behind(): return lax.ppermute(stacked, ('grp', 'sx', 'sy'), route)  11.7 us
    pallas_call x1, Pallas kernels, product(): pl.pallas_call(product_kernel, grid=(blocks,), out_shape=jax.ShapeDtypeSt...  6.19 us
    ppermute x1, waiting for transfers between devices, gather_heads(): return (own, lax.ppermute(own, 'grp', [(0, 1), (1, 0)]))  4.47 us
  transfers between devices with their start and end apart: 7, of which 5 were waited for; matrix products, arithmetic and copies ran while one was open for 4% of the time, Pallas kernels for 0%

profile of v4, /device:TPU:4, one launch (start us, length us, event | category | flops | bytes accessed | tf_op | source)
XLA Modules:
  0.0 149.3 jit_solution(2100616500141957092)
XLA Ops:
  6.5 0.0 all-gather.2.cloned.1.call-start
  6.5 1.6 %collective-permute-start.4 = (bf16[512,256]{1,0:T(8,128)(2,1)}, bf16[512,256]{1,0:T(8,128)(2,1)S(1)}, u32[]{:S(2)}, u32[]{:S(2)}) collective-permute-start(bf16[512,256]{1,0:T(8,128)(2,1)} %bitcast.40), channel_id=1, source_target_pairs={{0,0},{1,4},{2,8},{3,12},{4,32},{5,36},{6,40},{7,44},{8,257},{9,26... | collective-permute-start | bytes 786440 | tf_op jit(solution)/shard_map/ppermute | solution.py:114
  8.1 0.9 pad_maximum_fusion.1
  9.0 8.6 %collective-permute-start.2 = (bf16[2,256,128]{2,1,0:T(8,128)(2,1)S(1)}, bf16[2,256,128]{2,1,0:T(8,128)(2,1)S(1)}, u32[]{:S(2)}, u32[]{:S(2)}) collective-permute-start(bf16[2,256,128]{2,1,0:T(8,128)(2,1)S(1)} %pad_maximum_fusion.1), channel_id=1, source_target_pairs={{0,1},{1,2},{2,3},{3,4},{4,5},{5,6},{6,7},{7,8},{8,9},{9,10},{10,1... | collective-permute-start | bytes 393224 | tf_op jit(solution)/shard_map/ppermute | solution.py:49
  17.6 3.1 %collective-permute-start.3 = (bf16[2,256,128]{2,1,0:T(8,128)(2,1)S(1)}, bf16[2,256,128]{2,1,0:T(8,128)(2,1)S(1)}, u32[]{:S(2)}, u32[]{:S(2)}) collective-permute-start(bf16[2,256,128]{2,1,0:T(8,128)(2,1)S(1)} %pad_maximum_fusion.1), channel_id=1, source_target_pairs={{0,2},{1,3},{2,4},{3,5},{4,6},{5,7},{6,8},{7,9},{8,10},{9,11},{10,... | collective-permute-start | bytes 393224 | tf_op jit(solution)/shard_map/ppermute | solution.py:49
  20.7 6.7 %collective-permute-done.2 = bf16[2,256,128]{2,1,0:T(8,128)(2,1)S(1)} collective-permute-done((bf16[2,256,128]{2,1,0:T(8,128)(2,1)S(1)}, bf16[2,256,128]{2,1,0:T(8,128)(2,1)S(1)}, u32[]{:S(2)}, u32[]{:S(2)}) %collective-permute-start.2) | collective-permute-done | bytes 131104 | tf_op jit(solution)/shard_map/ppermute | solution.py:49
  27.4 7.2 %collective-permute-done.3 = bf16[2,256,128]{2,1,0:T(8,128)(2,1)S(1)} collective-permute-done((bf16[2,256,128]{2,1,0:T(8,128)(2,1)S(1)}, bf16[2,256,128]{2,1,0:T(8,128)(2,1)S(1)}, u32[]{:S(2)}, u32[]{:S(2)}) %collective-permute-start.3) | collective-permute-done | bytes 131104 | tf_op jit(solution)/shard_map/ppermute | solution.py:49
  34.7 0.0 collective-permute-done.4
  34.7 0.0 copy-start
  34.7 0.7 copy-done
  35.4 0.0 all-gather.2.cloned.1.call-update
  36.1 45.0 %conditional.1 = (bf16[2,4,256,512]{3,2,1,0:T(8,128)(2,1)}, bf16[2,4,256,512]{3,2,1,0:T(8,128)(2,1)}) conditional(s32[]{:T(128)} %bitcast.14, () %tuple.15, (bf16[2,512,128]{2,1,0:T(8,128)(2,1)S(1)}, bf16[2,256,128]{2,1,0:T(8,128)(2,1)S(1)}, s32[]{:T(128)}, s32[]{:T(128)}, s32[]{:T(128)}, /*index=5*/s32[16]{0:T(128)}, ...), branch_computations={%region_0.0_spmd, %region_1.6_spmd} | conditional | flops 681521152 | bytes 35960300 | solution.py:133
  36.1 1.9 %collective-permute-start = (bf16[2,512,128]{2,1,0:T(8,128)(2,1)S(1)}, bf16[2,512,128]{2,1,0:T(8,128)(2,1)S(1)}, u32[]{:S(2)}, u32[]{:S(2)}) collective-permute-start(bf16[2,512,128]{2,1,0:T(8,128)(2,1)S(1)} %get-tuple-element.22), channel_id=1, source_target_pairs={{0,256},{256,0},{1,257},{257,1},{2,258},{258,2},{3,259},{259,3},{4... | collective-permute-start | bytes 786440 | tf_op jit(solution)/shard_map/cond/branch_1_fun/ppermute | solution.py:120
  38.0 0.1 stack.16
  38.1 0.1 iota_add_fusion
  38.2 0.8 select_reduce_fusion.1
  39.0 0.1 select_reduce_fusion
  39.1 0.3 compare_and_fusion
  39.4 1.1 copy.21
  40.5 0.0 collective-permute-done
  40.6 0.9 fusion.14
  41.5 0.7 fusion
  42.2 1.0 fusion.11
  43.3 0.1 copy.20
  43.4 0.2 broadcast_in_dim.35
  43.6 31.1 %all_to_all.9 = bf16[8,256,512]{2,1,0:T(8,128)(2,1)} all-to-all(bf16[8,256,512]{2,1,0:T(8,128)(2,1)S(1)} %broadcast_in_dim.35), channel_id=1, replica_groups=mesh['grp'=2,'zh'=4,'zl'=2,'sx'=4,'sy'=8] {'zl','sx'}, dimensions={0} | all-to-all | bytes 4194304 | tf_op jit(solution)/shard_map/cond/branch_1_fun/all_to_all | solution.py:125
  74.7 1.9 %collective-permute-start.1 = (bf16[2,4,256,512]{3,2,1,0:T(8,128)(2,1)}, bf16[2,4,256,512]{3,2,1,0:T(8,128)(2,1)}, u32[]{:S(2)}, u32[]{:S(2)}) collective-permute-start(bf16[2,4,256,512]{3,2,1,0:T(8,128)(2,1)} %bitcast.13), channel_id=1, source_target_pairs={{0,256},{256,0},{1,257},{257,1},{2,258},{258,2},{3,259},{259,3},{4... | collective-permute-start | bytes 6291464 | tf_op jit(solution)/shard_map/cond/branch_1_fun/ppermute | solution.py:127
  76.6 4.5 %collective-permute-done.1 = bf16[2,4,256,512]{3,2,1,0:T(8,128)(2,1)} collective-permute-done((bf16[2,4,256,512]{3,2,1,0:T(8,128)(2,1)}, bf16[2,4,256,512]{3,2,1,0:T(8,128)(2,1)}, u32[]{:S(2)}, u32[]{:S(2)}) %collective-permute-start.1) | collective-permute-done | bytes 2097184 | tf_op jit(solution)/shard_map/cond/branch_1_fun/ppermute | solution.py:127
  81.1 1.1 all-gather.2.cloned.1.call-done
  82.2 6.2 %shard_map.56 = bf16[4,256,512]{2,1,0:T(8,128)(2,1)} custom-call(bf16[2,4,256,512]{3,2,1,0:T(8,128)(2,1)} %get-tuple-element.34.own_ref, bf16[2,4,256,512]{3,2,1,0:T(8,128)(2,1)} %get-tuple-element.35.other_ref, bf16[2,4,512,256]{3,2,1,0:T(8,128)(2,1)} %bitcast.39), custom_call_target="tpu_custom_call" | custom-call | flops 2147483648 | bytes 7340032 | tf_op jit(solution)/shard_map/pallas_call | solution.py:67
  88.4 36.4 %all_to_all.10 = bf16[4,256,512]{2,1,0:T(8,128)(2,1)S(1)} all-to-all(bf16[4,256,512]{2,1,0:T(8,128)(2,1)} %shard_map.56), channel_id=1, replica_groups=mesh['grp'=2,'zh'=4,'zl'=2,'sx'=4,'sy'=8] {'zh'}, dimensions={0} | all-to-all | bytes 2097152 | tf_op jit(solution)/shard_map/all_to_all | solution.py:135
  124.8 0.2 reduce_sum.30
  125.1 2.3 %collective-permute-start.5 = (bf16[256,512]{1,0:T(8,128)(2,1)S(1)}, bf16[256,512]{1,0:T(8,128)(2,1)S(1)}, u32[]{:S(2)}, u32[]{:S(2)}) collective-permute-start(bf16[256,512]{1,0:T(8,128)(2,1)S(1)} %reduce_sum.30), channel_id=1, source_target_pairs={{0,0},{1,1},{2,2},{3,3},{4,4},{5,5},{6,6},{7,7},{8,32},{9,33},{10,... | collective-permute-start | bytes 786440 | tf_op jit(solution)/shard_map/ppermute | solution.py:137
  127.4 14.3 %collective-permute-done.5 = bf16[256,512]{1,0:T(8,128)(2,1)S(1)} collective-permute-done((bf16[256,512]{1,0:T(8,128)(2,1)S(1)}, bf16[256,512]{1,0:T(8,128)(2,1)S(1)}, u32[]{:S(2)}, u32[]{:S(2)}) %collective-permute-start.5) | collective-permute-done | bytes 262176 | tf_op jit(solution)/shard_map/ppermute | solution.py:137
  141.8 0.7 copy.33
  (7 shorter events, 0.1 us)
Async XLA Ops:
  6.5 75.7 %all-gather.2.cloned.1.call-start = ((), (), s32[]{:S(2)}) async-start(), calls=%async_computation.2 | async-start | bytes 2359296 | tf_op jit(solution)/shard_map/all_gather | solution.py:116
  6.5 28.1 %collective-permute-start.4 = (bf16[512,256]{1,0:T(8,128)(2,1)}, bf16[512,256]{1,0:T(8,128)(2,1)S(1)}, u32[]{:S(2)}, u32[]{:S(2)}) collective-permute-start(bf16[512,256]{1,0:T(8,128)(2,1)} %bitcast.40), channel_id=1, source_target_pairs={{0,0},{1,4},{2,8},{3,12},{4,32},{5,36},{6,40},{7,44},{8,257},{9,26... | collective-permute-start | bytes 786440 | tf_op jit(solution)/shard_map/ppermute | solution.py:114
  9.0 18.4 %collective-permute-start.2 = (bf16[2,256,128]{2,1,0:T(8,128)(2,1)S(1)}, bf16[2,256,128]{2,1,0:T(8,128)(2,1)S(1)}, u32[]{:S(2)}, u32[]{:S(2)}) collective-permute-start(bf16[2,256,128]{2,1,0:T(8,128)(2,1)S(1)} %pad_maximum_fusion.1), channel_id=1, source_target_pairs={{0,1},{1,2},{2,3},{3,4},{4,5},{5,6},{6,7},{7,8},{8,9},{9,10},{10,1... | collective-permute-start | bytes 393224 | tf_op jit(solution)/shard_map/ppermute | solution.py:49
  17.6 17.0 %collective-permute-start.3 = (bf16[2,256,128]{2,1,0:T(8,128)(2,1)S(1)}, bf16[2,256,128]{2,1,0:T(8,128)(2,1)S(1)}, u32[]{:S(2)}, u32[]{:S(2)}) collective-permute-start(bf16[2,256,128]{2,1,0:T(8,128)(2,1)S(1)} %pad_maximum_fusion.1), channel_id=1, source_target_pairs={{0,2},{1,3},{2,4},{3,5},{4,6},{5,7},{6,8},{7,9},{8,10},{9,11},{10,... | collective-permute-start | bytes 393224 | tf_op jit(solution)/shard_map/ppermute | solution.py:49
  34.7 0.7 copy-start
  36.1 4.4 %collective-permute-start = (bf16[2,512,128]{2,1,0:T(8,128)(2,1)S(1)}, bf16[2,512,128]{2,1,0:T(8,128)(2,1)S(1)}, u32[]{:S(2)}, u32[]{:S(2)}) collective-permute-start(bf16[2,512,128]{2,1,0:T(8,128)(2,1)S(1)} %get-tuple-element.22), channel_id=1, source_target_pairs={{0,256},{256,0},{1,257},{257,1},{2,258},{258,2},{3,259},{259,3},{4... | collective-permute-start | bytes 786440 | tf_op jit(solution)/shard_map/cond/branch_1_fun/ppermute | solution.py:120
  74.7 6.4 %collective-permute-start.1 = (bf16[2,4,256,512]{3,2,1,0:T(8,128)(2,1)}, bf16[2,4,256,512]{3,2,1,0:T(8,128)(2,1)}, u32[]{:S(2)}, u32[]{:S(2)}) collective-permute-start(bf16[2,4,256,512]{3,2,1,0:T(8,128)(2,1)} %bitcast.13), channel_id=1, source_target_pairs={{0,256},{256,0},{1,257},{257,1},{2,258},{258,2},{3,259},{259,3},{4... | collective-permute-start | bytes 6291464 | tf_op jit(solution)/shard_map/cond/branch_1_fun/ppermute | solution.py:127
  125.1 16.7 %collective-permute-start.5 = (bf16[256,512]{1,0:T(8,128)(2,1)S(1)}, bf16[256,512]{1,0:T(8,128)(2,1)S(1)}, u32[]{:S(2)}, u32[]{:S(2)}) collective-permute-start(bf16[256,512]{1,0:T(8,128)(2,1)S(1)} %reduce_sum.30), channel_id=1, source_target_pairs={{0,0},{1,1},{2,2},{3,3},{4,4},{5,5},{6,6},{7,7},{8,32},{9,33},{10,... | collective-permute-start | bytes 786440 | tf_op jit(solution)/shard_map/ppermute | solution.py:137
Sparse Core Ops, SparseCore 0:
  35.5 46.6 all-gather.1

commit v5 on v4

--- a/solution.py
+++ b/solution.py
@@ -49,34 +49,35 @@
     return lax.ppermute(stacked, ("grp", "sx", "sy"), route)
 
 
-def product_kernel(own_ref, other_ref, right_ref, out_ref):
-    left = jnp.concatenate(
-        [ref[z, 0] for z in range(own_ref.shape[0]) for ref in (own_ref, other_ref)], axis=1
-    )
-    halves, parts, depth, width = right_ref.shape
-    for half in range(halves):
-        out_ref[0, :, half * width : (half + 1) * width] = jnp.dot(
-            left, right_ref[half].reshape(parts * depth, width), preferred_element_type=jnp.float32
-        ).astype(out_ref.dtype)
+def product_kernel(turn_ref, *refs):
+    *left_refs, right_ref, out_ref = refs
+    left = jnp.concatenate([ref[0] for ref in left_refs], axis=1)
+    _, parts, depth, width = right_ref.shape
+    right = right_ref[0].reshape(parts * depth, width)
+    out_ref[...] = jnp.dot(left, right, preferred_element_type=jnp.float32).astype(out_ref.dtype)
 
 
-def product(own, other, right):
-    pairs, blocks, tokens, depth = own.shape
+def product(turn, lefts, right):
+    _, tokens, depth = lefts[0].shape
     halves, parts, _, width = right.shape
-    heads = pl.BlockSpec((pairs, 1, tokens, depth), lambda i: (0, i, 0, 0))
+    heads = pl.BlockSpec((1, tokens, depth), lambda h, turn: (turn[0], 0, 0))
+    grid_spec = pltpu.PrefetchScalarGridSpec(
+        num_scalar_prefetch=1,
+        grid=(halves,),
+        in_specs=[heads] * parts + [pl.BlockSpec((1, parts, depth, width), lambda h, turn: (h, 0, 0, 0))],
+        out_specs=pl.BlockSpec((tokens, width), lambda h, turn: (0, h)),
+    )
     return pl.pallas_call(
         product_kernel,
-        grid=(blocks,),
-        out_shape=jax.ShapeDtypeStruct((blocks, tokens, halves * width), jnp.bfloat16),
-        in_specs=[heads, heads, pl.BlockSpec((halves, parts, depth, width), lambda i: (0, 0, 0, 0))],
-        out_specs=pl.BlockSpec((1, tokens, halves * width), lambda i: (i, 0, 0)),
+        grid_spec=grid_spec,
+        out_shape=jax.ShapeDtypeStruct((tokens, halves * width), jnp.bfloat16),
         compiler_params=pltpu.CompilerParams(vmem_limit_bytes=58 * 2**20),
         cost_estimate=pl.CostEstimate(
-            flops=4 * own.size * halves * width,
-            bytes_accessed=2 * (2 * own.size + right.size + blocks * tokens * halves * width),
+            flops=2 * tokens * right.size,
+            bytes_accessed=2 * (parts * tokens * depth + right.size + tokens * halves * width),
             transcendentals=0,
         ),
-    )(own, other, right)
+    )(turn.reshape(1), *lefts, right)
 
 
 def solution(mesh):
@@ -91,7 +92,7 @@
             total = total * size + at
         return total
 
-    to_ring, to_owner = [], []
+    to_ring, to_owner = [], [[] for _ in range(SX)]
     for c in range(n_grp):
         for hi in range(zh):
             for lo in range(ZL):
@@ -99,11 +100,12 @@
                     for y in range(sy):
                         a, z = divmod((x * sy + y) // 2, n_kv)
                         g, w = divmod(z // 2, ZL)
-                        ring = index(g, hi, w, 2 * a + z % 2, (y % 2) * 4 + lo * 2 + (c ^ g))
+                        ring = index(g, hi, w, 2 * a + z % 2, (y % 2) * 4 + (lo ^ w) * 2 + (c ^ g))
                         to_ring.append((index(c, hi, lo, x, y), ring))
                         z = 2 * (c * ZL + lo) + x % 2
-                        owner = index(x // 2, z // ZL, z % ZL, hi, y)
-                        to_owner.append((index(c, hi, lo, x, y), owner))
+                        for t in range(SX):
+                            owner = index(x // 2, z // ZL, z % ZL, (hi + t) % SX, y)
+                            to_owner[t].append((index(c, hi, lo, x, y), owner))
 
     def on_device(queries, keys, values, lengths, weight):
         tokens = queries.shape[0]
@@ -122,19 +124,22 @@
             query_pos = shard * tokens + jnp.arange(tokens, dtype=jnp.int32)
             key_pos = ((shard - behind) * tokens)[:, None] + jnp.arange(tokens, dtype=jnp.int32)[None, :]
             heads = attend(queries, window[0], window[1], query_pos, key_pos.reshape(-1), lengths)
-            along = lax.all_to_all(jnp.broadcast_to(heads, (ZL * SX,) + heads.shape), ("zl", "sx"), 0, 0)
-            own = along.reshape((ZL, SX) + heads.shape)
-            return own, lax.ppermute(own, "grp", [(0, 1), (1, 0)])
+            pair = lax.ppermute(heads, "zl", [(0, 1), (1, 0)])
+            parts = []
+            for part in (heads, pair):
+                own = lax.all_to_all(jnp.broadcast_to(part, (SX,) + part.shape), "sx", 0, 0)
+                parts += [own, lax.ppermute(own, "grp", [(0, 1), (1, 0)])]
+            return tuple(parts)
 
         def nothing(queries, stacked, mine, lengths):
-            empty = jnp.zeros((ZL, SX) + queries.shape, queries.dtype)
-            return empty, empty
+            return (jnp.zeros((SX,) + queries.shape, queries.dtype),) * (ZL * n_grp)
 
-        own, other = lax.cond(lengths[0] > 0, gather_heads, nothing, queries[:, 0], stacked, mine, lengths)
-        partial = product(own, other, columns)
-        parts = lax.all_to_all(partial, "zh", 0, 0)
-        tile = jnp.sum(parts.astype(jnp.float32), axis=0).astype(jnp.bfloat16)
-        return lax.ppermute(tile, ALL, to_owner)
+        parts = lax.cond(lengths[0] > 0, gather_heads, nothing, queries[:, 0], stacked, mine, lengths)
+        turn = lax.axis_index("zh")
+        tiles = []
+        for t in range(SX):
+            tiles.append(lax.ppermute(product((turn + t) % SX, parts, columns), ALL, to_owner[t]))
+        return sum(tile.astype(jnp.float32) for tile in tiles).astype(jnp.bfloat16)
 
     q = P(("sx", "sy"), ("zh", "zl"), "grp")
     k = P(("sx", "sy"), ("zh", "zl"), None)

time: 150 us -> 152 us (1.013)
  the two profiles are of different devices: /device:TPU:4 before, /device:TPU:3 now
where the time goes in v5:
time: 152 us
  starting transfers between devices  65.4 us (43%)
  waiting for transfers between devices  49.5 us (33%)
  between operations  14.2 us (9%)
  Pallas kernels  12.4 us (8%)
  local copies, waits for them, and re-layouts  4.38 us (3%)
  other arithmetic  3.72 us (2%)
  matrix products  1.96 us (1%)
    ppermute x4, starting transfers between devices, on_device(): lax.ppermute(product((turn + t) % SX, parts, columns), ALL, to_owner[t])  24 us
    ppermute x4, waiting for transfers between devices, on_device(): lax.ppermute(product((turn + t) % SX, parts, columns), ALL, to_owner[t])  18.2 us
    all_to_all x2, waiting for transfers between devices, gather_heads(): own = lax.all_to_all(jnp.broadcast_to(part, (SX,) + part.shape), 'sx', 0, 0)  13.6 us
    ppermute x2, starting transfers between devices, fetch_behind(): return lax.ppermute(stacked, ('grp', 'sx', 'sy'), route)  12.9 us
    pallas_call x4, Pallas kernels, product(): pl.pallas_call(product_kernel, grid_spec=grid_spec, out_shape=jax.ShapeDt...  12.4 us
    all_to_all x2, starting transfers between devices, gather_heads(): own = lax.all_to_all(jnp.broadcast_to(part, (SX,) + part.shape), 'sx', 0, 0)  9.01 us
    ppermute x2, waiting for transfers between devices, fetch_behind(): return lax.ppermute(stacked, ('grp', 'sx', 'sy'), route)  8.6 us
    ppermute x2, starting transfers between devices, gather_heads(): parts += [own, lax.ppermute(own, 'grp', [(0, 1), (1, 0)])]  7.22 us
  transfers between devices with their start and end apart: 14, of which 8 were waited for; matrix products, arithmetic and copies ran while one was open for 6% of the time, Pallas kernels for 6%

profile of v5, /device:TPU:3, one launch (start us, length us, event | category | flops | bytes accessed | tf_op | source)
XLA Modules:
  0.0 151.6 jit_solution(4355659787888187923)
XLA Ops:
  6.5 0.0 all-gather.2.cloned.1.call-start
  6.5 1.9 %collective-permute-start.6 = (bf16[512,256]{1,0:T(8,128)(2,1)}, bf16[512,256]{1,0:T(8,128)(2,1)S(1)}, u32[]{:S(2)}, u32[]{:S(2)}) collective-permute-start(bf16[512,256]{1,0:T(8,128)(2,1)} %bitcast.47), channel_id=1, source_target_pairs={{0,0},{1,4},{2,8},{3,12},{4,34},{5,38},{6,42},{7,46},{8,257},{9,26... | collective-permute-start | bytes 786440 | tf_op jit(solution)/shard_map/ppermute | solution.py:116
  8.5 0.9 pad_maximum_fusion.1
  9.3 7.7 %collective-permute-start.4 = (bf16[2,256,128]{2,1,0:T(8,128)(2,1)S(1)}, bf16[2,256,128]{2,1,0:T(8,128)(2,1)S(1)}, u32[]{:S(2)}, u32[]{:S(2)}) collective-permute-start(bf16[2,256,128]{2,1,0:T(8,128)(2,1)S(1)} %pad_maximum_fusion.1), channel_id=1, source_target_pairs={{0,1},{1,2},{2,3},{3,4},{4,5},{5,6},{6,7},{7,8},{8,9},{9,10},{10,1... | collective-permute-start | bytes 393224 | tf_op jit(solution)/shard_map/ppermute | solution.py:49
  17.1 5.1 %collective-permute-start.5 = (bf16[2,256,128]{2,1,0:T(8,128)(2,1)S(1)}, bf16[2,256,128]{2,1,0:T(8,128)(2,1)S(1)}, u32[]{:S(2)}, u32[]{:S(2)}) collective-permute-start(bf16[2,256,128]{2,1,0:T(8,128)(2,1)S(1)} %pad_maximum_fusion.1), channel_id=1, source_target_pairs={{0,2},{1,3},{2,4},{3,5},{4,6},{5,7},{6,8},{7,9},{8,10},{9,11},{10,... | collective-permute-start | bytes 393224 | tf_op jit(solution)/shard_map/ppermute | solution.py:49
  22.2 4.2 %collective-permute-done.4 = bf16[2,256,128]{2,1,0:T(8,128)(2,1)S(1)} collective-permute-done((bf16[2,256,128]{2,1,0:T(8,128)(2,1)S(1)}, bf16[2,256,128]{2,1,0:T(8,128)(2,1)S(1)}, u32[]{:S(2)}, u32[]{:S(2)}) %collective-permute-start.4) | collective-permute-done | bytes 131104 | tf_op jit(solution)/shard_map/ppermute | solution.py:49
  26.4 4.4 %collective-permute-done.5 = bf16[2,256,128]{2,1,0:T(8,128)(2,1)S(1)} collective-permute-done((bf16[2,256,128]{2,1,0:T(8,128)(2,1)S(1)}, bf16[2,256,128]{2,1,0:T(8,128)(2,1)S(1)}, u32[]{:S(2)}, u32[]{:S(2)}) %collective-permute-start.5) | collective-permute-done | bytes 131104 | tf_op jit(solution)/shard_map/ppermute | solution.py:49
  30.8 0.0 collective-permute-done.6
  30.8 0.0 copy-start
  30.9 0.7 copy-done
  31.5 0.0 all-gather.2.cloned.1.call-update
  32.3 57.0 %conditional.1 = (bf16[4,256,512]{2,1,0:T(8,128)(2,1)}, bf16[4,256,512]{2,1,0:T(8,128)(2,1)}, bf16[4,256,512]{2,1,0:T(8,128)(2,1)}, bf16[4,256,512]{2,1,0:T(8,128)(2,1)}) conditional(s32[]{:T(128)} %bitcast.14, () %tuple.15, (bf16[2,512,128]{2,1,0:T(8,128)(2,1)S(1)}, bf16[2,256,128]{2,1,0:T(8,128)(2,1)S(1)}, s32[]{:T(128)}, s32[]{:T(128)}, s32[]{:T(128)}, ...), branch_computations={%region_0.0_spmd, %region_1.6_spmd} | conditional | flops 681521152 | bytes 39892620 | solution.py:137
  32.3 6.6 %collective-permute-start = (bf16[2,512,128]{2,1,0:T(8,128)(2,1)S(1)}, bf16[2,512,128]{2,1,0:T(8,128)(2,1)S(1)}, u32[]{:S(2)}, u32[]{:S(2)}) collective-permute-start(bf16[2,512,128]{2,1,0:T(8,128)(2,1)S(1)} %get-tuple-element.22), channel_id=1, source_target_pairs={{0,256},{256,0},{1,257},{257,1},{2,258},{258,2},{3,259},{259,3},{4... | collective-permute-start | bytes 786440 | tf_op jit(solution)/shard_map/cond/branch_1_fun/ppermute | solution.py:122
  38.9 0.1 stack.16
  39.0 0.1 iota_add_fusion
  39.0 0.8 select_reduce_fusion.1
  39.8 0.1 select_reduce_fusion
  39.9 0.3 compare_and_fusion
  40.2 1.1 copy.24
  41.3 0.0 collective-permute-done
  41.4 0.9 fusion.14
  42.4 0.7 fusion
  43.1 1.0 fusion.11
  44.1 0.1 copy.22
  44.3 1.1 broadcast_in_dim.36
  45.3 4.2 %all-to-all-start = ((bf16[4,256,512]{2,1,0:T(8,128)(2,1)}), bf16[4,256,512]{2,1,0:T(8,128)(2,1)}, u32[]{:S(2)}, u32[]{:S(2)}) async-start(bf16[4,256,512]{2,1,0:T(8,128)(2,1)} %broadcast_in_dim.36), calls=%async_computation | async-start | bytes 2097152 | tf_op jit(solution)/shard_map/cond/branch_1_fun/all_to_all | solution.py:130
  49.6 3.8 %collective-permute-start.2 = (bf16[256,512]{0,1:T(8,128)(2,1)S(1)}, bf16[256,512]{0,1:T(8,128)(2,1)S(1)}, u32[]{:S(2)}, u32[]{:S(2)}) collective-permute-start(bf16[256,512]{0,1:T(8,128)(2,1)S(1)} %bitcast.42), channel_id=1, source_target_pairs={{0,32},{32,0},{1,33},{33,1},{2,34},{34,2},{3,35},{35,3},{4,36},{36... | collective-permute-start | bytes 786440 | tf_op jit(solution)/shard_map/cond/branch_1_fun/ppermute | solution.py:127
  53.4 6.5 %collective-permute-done.2 = bf16[256,512]{0,1:T(8,128)(2,1)S(1)} collective-permute-done((bf16[256,512]{0,1:T(8,128)(2,1)S(1)}, bf16[256,512]{0,1:T(8,128)(2,1)S(1)}, u32[]{:S(2)}, u32[]{:S(2)}) %collective-permute-start.2) | collective-permute-done | bytes 262176 | tf_op jit(solution)/shard_map/cond/branch_1_fun/ppermute | solution.py:127
  59.9 0.1 copy.23
  60.0 3.9 %all-to-all-done = bf16[4,256,512]{2,1,0:T(8,128)(2,1)} async-done(((bf16[4,256,512]{2,1,0:T(8,128)(2,1)}), bf16[4,256,512]{2,1,0:T(8,128)(2,1)}, u32[]{:S(2)}, u32[]{:S(2)}) %all-to-all-start) | async-done | bytes 1048608 | tf_op jit(solution)/shard_map/cond/branch_1_fun/all_to_all | solution.py:130
  63.9 1.1 broadcast_in_dim.37
  65.0 4.8 %all-to-all-start.1 = ((bf16[4,256,512]{2,1,0:T(8,128)(2,1)}), bf16[4,256,512]{2,1,0:T(8,128)(2,1)}, u32[]{:S(2)}, u32[]{:S(2)}) async-start(bf16[4,256,512]{2,1,0:T(8,128)(2,1)} %broadcast_in_dim.37), calls=%async_computation.1 | async-start | bytes 2097152 | tf_op jit(solution)/shard_map/cond/branch_1_fun/all_to_all | solution.py:130
  69.8 3.3 %collective-permute-start.1 = (bf16[4,256,512]{2,1,0:T(8,128)(2,1)}, bf16[4,256,512]{2,1,0:T(8,128)(2,1)}, u32[]{:S(2)}, u32[]{:S(2)}) collective-permute-start(bf16[4,256,512]{2,1,0:T(8,128)(2,1)} %all-to-all-done), channel_id=1, source_target_pairs={{0,256},{256,0},{1,257},{257,1},{2,258},{258,2},{3,259},{259,3},{4... | collective-permute-start | bytes 3145736 | tf_op jit(solution)/shard_map/cond/branch_1_fun/ppermute | solution.py:131
  73.1 9.6 %all-to-all-done.1 = bf16[4,256,512]{2,1,0:T(8,128)(2,1)} async-done(((bf16[4,256,512]{2,1,0:T(8,128)(2,1)}), bf16[4,256,512]{2,1,0:T(8,128)(2,1)}, u32[]{:S(2)}, u32[]{:S(2)}) %all-to-all-start.1) | async-done | bytes 1048608 | tf_op jit(solution)/shard_map/cond/branch_1_fun/all_to_all | solution.py:130
  82.7 3.9 %collective-permute-start.3 = (bf16[4,256,512]{2,1,0:T(8,128)(2,1)}, bf16[4,256,512]{2,1,0:T(8,128)(2,1)}, u32[]{:S(2)}, u32[]{:S(2)}) collective-permute-start(bf16[4,256,512]{2,1,0:T(8,128)(2,1)} %all-to-all-done.1), channel_id=1, source_target_pairs={{0,256},{256,0},{1,257},{257,1},{2,258},{258,2},{3,259},{259,3},{4... | collective-permute-start | bytes 3145736 | tf_op jit(solution)/shard_map/cond/branch_1_fun/ppermute | solution.py:131
  86.7 0.0 collective-permute-done.1
  86.7 2.6 %collective-permute-done.3 = bf16[4,256,512]{2,1,0:T(8,128)(2,1)} collective-permute-done((bf16[4,256,512]{2,1,0:T(8,128)(2,1)}, bf16[4,256,512]{2,1,0:T(8,128)(2,1)}, u32[]{:S(2)}, u32[]{:S(2)}) %collective-permute-start.3) | collective-permute-done | bytes 1048608 | tf_op jit(solution)/shard_map/cond/branch_1_fun/ppermute | solution.py:131
  89.3 0.0 all-gather.2.cloned.1.call-done
  89.3 3.1 %shard_map.56 = bf16[256,512]{1,0:T(8,128)(2,1)} custom-call(s32[1]{0:T(128)} %bitcast.13.turn_ref, bf16[4,256,512]{2,1,0:T(8,128)(2,1)} %get-tuple-element.36.refs_0_, bf16[4,256,512]{2,1,0:T(8,128)(2,1)} %get-tuple-element.37.refs_1_, bf16[4,256,512]{2,1,0:T(8,128)(2,1)} %get-tuple-element.38.refs_2_, bf16[4,256,512]{2,1,0:T(8,128)(2,1)} %get-tuple-element.39.refs_3_, ...), custom_call_target="tpu_custom_call" | custom-call | flops 536870912 | bytes 3407872 | tf_op jit(solution)/shard_map/pallas_call | solution.py:70
  92.4 11.4 %collective-permute-start.7 = (bf16[256,512]{1,0:T(8,128)(2,1)}, bf16[256,512]{1,0:T(8,128)(2,1)S(1)}, u32[]{:S(2)}, u32[]{:S(2)}) collective-permute-start(bf16[256,512]{1,0:T(8,128)(2,1)} %shard_map.56), channel_id=1, source_target_pairs={{0,0},{1,1},{2,2},{3,3},{4,4},{5,5},{6,6},{7,7},{8,32},{9,33},{10,... | collective-permute-start | bytes 786440 | tf_op jit(solution)/shard_map/ppermute | solution.py:141
  103.8 3.1 %shard_map.57 = bf16[256,512]{1,0:T(8,128)(2,1)} custom-call(s32[1]{0:T(128)} %bitcast.19.turn_ref, bf16[4,256,512]{2,1,0:T(8,128)(2,1)} %get-tuple-element.36.refs_0_, bf16[4,256,512]{2,1,0:T(8,128)(2,1)} %get-tuple-element.37.refs_1_, bf16[4,256,512]{2,1,0:T(8,128)(2,1)} %get-tuple-element.38.refs_2_, bf16[4,256,512]{2,1,0:T(8,128)(2,1)} %get-tuple-element.39.refs_3_, ...), custom_call_target="tpu_custom_call" | custom-call | flops 536870912 | bytes 3407872 | tf_op jit(solution)/shard_map/pallas_call | solution.py:70
  106.9 1.9 %collective-permute-start.8 = (bf16[256,512]{1,0:T(8,128)(2,1)}, bf16[256,512]{1,0:T(8,128)(2,1)S(1)}, u32[]{:S(2)}, u32[]{:S(2)}) collective-permute-start(bf16[256,512]{1,0:T(8,128)(2,1)} %shard_map.57), channel_id=1, source_target_pairs={{0,8},{1,9},{2,10},{3,11},{4,12},{5,13},{6,14},{7,15},{8,40},{9,41... | collective-permute-start | bytes 786440 | tf_op jit(solution)/shard_map/ppermute | solution.py:141
  108.8 3.1 %shard_map.58 = bf16[256,512]{1,0:T(8,128)(2,1)} custom-call(s32[1]{0:T(128)} %bitcast.20.turn_ref, bf16[4,256,512]{2,1,0:T(8,128)(2,1)} %get-tuple-element.36.refs_0_, bf16[4,256,512]{2,1,0:T(8,128)(2,1)} %get-tuple-element.37.refs_1_, bf16[4,256,512]{2,1,0:T(8,128)(2,1)} %get-tuple-element.38.refs_2_, bf16[4,256,512]{2,1,0:T(8,128)(2,1)} %get-tuple-element.39.refs_3_, ...), custom_call_target="tpu_custom_call" | custom-call | flops 536870912 | bytes 3407872 | tf_op jit(solution)/shard_map/pallas_call | solution.py:70
  111.9 7.9 %collective-permute-start.9 = (bf16[256,512]{1,0:T(8,128)(2,1)}, bf16[256,512]{1,0:T(8,128)(2,1)S(1)}, u32[]{:S(2)}, u32[]{:S(2)}) collective-permute-start(bf16[256,512]{1,0:T(8,128)(2,1)} %shard_map.58), channel_id=1, source_target_pairs={{0,16},{1,17},{2,18},{3,19},{4,20},{5,21},{6,22},{7,23},{8,48},{9,... | collective-permute-start | bytes 786440 | tf_op jit(solution)/shard_map/ppermute | solution.py:141
  119.8 3.1 %shard_map.59 = bf16[256,512]{1,0:T(8,128)(2,1)} custom-call(s32[1]{0:T(128)} %bitcast.21.turn_ref, bf16[4,256,512]{2,1,0:T(8,128)(2,1)} %get-tuple-element.36.refs_0_, bf16[4,256,512]{2,1,0:T(8,128)(2,1)} %get-tuple-element.37.refs_1_, bf16[4,256,512]{2,1,0:T(8,128)(2,1)} %get-tuple-element.38.refs_2_, bf16[4,256,512]{2,1,0:T(8,128)(2,1)} %get-tuple-element.39.refs_3_, ...), custom_call_target="tpu_custom_call" | custom-call | flops 536870912 | bytes 3407872 | tf_op jit(solution)/shard_map/pallas_call | solution.py:70
  122.9 2.8 %collective-permute-start.10 = (bf16[256,512]{1,0:T(8,128)(2,1)}, bf16[256,512]{1,0:T(8,128)(2,1)S(1)}, u32[]{:S(2)}, u32[]{:S(2)}) collective-permute-start(bf16[256,512]{1,0:T(8,128)(2,1)} %shard_map.59), channel_id=1, source_target_pairs={{0,24},{1,25},{2,26},{3,27},{4,28},{5,29},{6,30},{7,31},{8,56},{9,... | collective-permute-start | bytes 786440 | tf_op jit(solution)/shard_map/ppermute | solution.py:141
  125.8 0.0 collective-permute-done.7
  125.8 0.0 collective-permute-done.8
  125.8 7.4 %collective-permute-done.9 = bf16[256,512]{1,0:T(8,128)(2,1)S(1)} collective-permute-done((bf16[256,512]{1,0:T(8,128)(2,1)}, bf16[256,512]{1,0:T(8,128)(2,1)S(1)}, u32[]{:S(2)}, u32[]{:S(2)}) %collective-permute-start.9) | collective-permute-done | bytes 262176 | tf_op jit(solution)/shard_map/ppermute | solution.py:141
  133.2 10.7 %collective-permute-done.10 = bf16[256,512]{1,0:T(8,128)(2,1)S(1)} collective-permute-done((bf16[256,512]{1,0:T(8,128)(2,1)}, bf16[256,512]{1,0:T(8,128)(2,1)S(1)}, u32[]{:S(2)}, u32[]{:S(2)}) %collective-permute-start.10) | collective-permute-done | bytes 262176 | tf_op jit(solution)/shard_map/ppermute | solution.py:141
  144.0 0.8 add_convert_fusion
  (7 shorter events, 0.1 us)
Async XLA Ops:
  6.5 82.8 %all-gather.2.cloned.1.call-start = ((), (), s32[]{:S(2)}) async-start(), calls=%async_computation.2 | async-start | bytes 2359296 | tf_op jit(solution)/shard_map/all_gather | solution.py:118
  6.5 24.3 %collective-permute-start.6 = (bf16[512,256]{1,0:T(8,128)(2,1)}, bf16[512,256]{1,0:T(8,128)(2,1)S(1)}, u32[]{:S(2)}, u32[]{:S(2)}) collective-permute-start(bf16[512,256]{1,0:T(8,128)(2,1)} %bitcast.47), channel_id=1, source_target_pairs={{0,0},{1,4},{2,8},{3,12},{4,34},{5,38},{6,42},{7,46},{8,257},{9,26... | collective-permute-start | bytes 786440 | tf_op jit(solution)/shard_map/ppermute | solution.py:116
  9.3 17.1 %collective-permute-start.4 = (bf16[2,256,128]{2,1,0:T(8,128)(2,1)S(1)}, bf16[2,256,128]{2,1,0:T(8,128)(2,1)S(1)}, u32[]{:S(2)}, u32[]{:S(2)}) collective-permute-start(bf16[2,256,128]{2,1,0:T(8,128)(2,1)S(1)} %pad_maximum_fusion.1), channel_id=1, source_target_pairs={{0,1},{1,2},{2,3},{3,4},{4,5},{5,6},{6,7},{7,8},{8,9},{9,10},{10,1... | collective-permute-start | bytes 393224 | tf_op jit(solution)/shard_map/ppermute | solution.py:49
  17.1 13.7 %collective-permute-start.5 = (bf16[2,256,128]{2,1,0:T(8,128)(2,1)S(1)}, bf16[2,256,128]{2,1,0:T(8,128)(2,1)S(1)}, u32[]{:S(2)}, u32[]{:S(2)}) collective-permute-start(bf16[2,256,128]{2,1,0:T(8,128)(2,1)S(1)} %pad_maximum_fusion.1), channel_id=1, source_target_pairs={{0,2},{1,3},{2,4},{3,5},{4,6},{5,7},{6,8},{7,9},{8,10},{9,11},{10,... | collective-permute-start | bytes 393224 | tf_op jit(solution)/shard_map/ppermute | solution.py:49
  30.8 0.7 copy-start
  32.3 9.1 %collective-permute-start = (bf16[2,512,128]{2,1,0:T(8,128)(2,1)S(1)}, bf16[2,512,128]{2,1,0:T(8,128)(2,1)S(1)}, u32[]{:S(2)}, u32[]{:S(2)}) collective-permute-start(bf16[2,512,128]{2,1,0:T(8,128)(2,1)S(1)} %get-tuple-element.22), channel_id=1, source_target_pairs={{0,256},{256,0},{1,257},{257,1},{2,258},{258,2},{3,259},{259,3},{4... | collective-permute-start | bytes 786440 | tf_op jit(solution)/shard_map/cond/branch_1_fun/ppermute | solution.py:122
  45.3 18.6 %all-to-all-start = ((bf16[4,256,512]{2,1,0:T(8,128)(2,1)}), bf16[4,256,512]{2,1,0:T(8,128)(2,1)}, u32[]{:S(2)}, u32[]{:S(2)}) async-start(bf16[4,256,512]{2,1,0:T(8,128)(2,1)} %broadcast_in_dim.36), calls=%async_computation | async-start | bytes 2097152 | tf_op jit(solution)/shard_map/cond/branch_1_fun/all_to_all | solution.py:130
  49.6 10.3 %collective-permute-start.2 = (bf16[256,512]{0,1:T(8,128)(2,1)S(1)}, bf16[256,512]{0,1:T(8,128)(2,1)S(1)}, u32[]{:S(2)}, u32[]{:S(2)}) collective-permute-start(bf16[256,512]{0,1:T(8,128)(2,1)S(1)} %bitcast.42), channel_id=1, source_target_pairs={{0,32},{32,0},{1,33},{33,1},{2,34},{34,2},{3,35},{35,3},{4,36},{36... | collective-permute-start | bytes 786440 | tf_op jit(solution)/shard_map/cond/branch_1_fun/ppermute | solution.py:127
  65.0 17.7 %all-to-all-start.1 = ((bf16[4,256,512]{2,1,0:T(8,128)(2,1)}), bf16[4,256,512]{2,1,0:T(8,128)(2,1)}, u32[]{:S(2)}, u32[]{:S(2)}) async-start(bf16[4,256,512]{2,1,0:T(8,128)(2,1)} %broadcast_in_dim.37), calls=%async_computation.1 | async-start | bytes 2097152 | tf_op jit(solution)/shard_map/cond/branch_1_fun/all_to_all | solution.py:130
  69.8 16.9 %collective-permute-start.1 = (bf16[4,256,512]{2,1,0:T(8,128)(2,1)}, bf16[4,256,512]{2,1,0:T(8,128)(2,1)}, u32[]{:S(2)}, u32[]{:S(2)}) collective-permute-start(bf16[4,256,512]{2,1,0:T(8,128)(2,1)} %all-to-all-done), channel_id=1, source_target_pairs={{0,256},{256,0},{1,257},{257,1},{2,258},{258,2},{3,259},{259,3},{4... | collective-permute-start | bytes 3145736 | tf_op jit(solution)/shard_map/cond/branch_1_fun/ppermute | solution.py:131
  82.7 6.5 %collective-permute-start.3 = (bf16[4,256,512]{2,1,0:T(8,128)(2,1)}, bf16[4,256,512]{2,1,0:T(8,128)(2,1)}, u32[]{:S(2)}, u32[]{:S(2)}) collective-permute-start(bf16[4,256,512]{2,1,0:T(8,128)(2,1)} %all-to-all-done.1), channel_id=1, source_target_pairs={{0,256},{256,0},{1,257},{257,1},{2,258},{258,2},{3,259},{259,3},{4... | collective-permute-start | bytes 3145736 | tf_op jit(solution)/shard_map/cond/branch_1_fun/ppermute | solution.py:131
  92.4 33.4 %collective-permute-start.7 = (bf16[256,512]{1,0:T(8,128)(2,1)}, bf16[256,512]{1,0:T(8,128)(2,1)S(1)}, u32[]{:S(2)}, u32[]{:S(2)}) collective-permute-start(bf16[256,512]{1,0:T(8,128)(2,1)} %shard_map.56), channel_id=1, source_target_pairs={{0,0},{1,1},{2,2},{3,3},{4,4},{5,5},{6,6},{7,7},{8,32},{9,33},{10,... | collective-permute-start | bytes 786440 | tf_op jit(solution)/shard_map/ppermute | solution.py:141
  106.9 18.9 %collective-permute-start.8 = (bf16[256,512]{1,0:T(8,128)(2,1)}, bf16[256,512]{1,0:T(8,128)(2,1)S(1)}, u32[]{:S(2)}, u32[]{:S(2)}) collective-permute-start(bf16[256,512]{1,0:T(8,128)(2,1)} %shard_map.57), channel_id=1, source_target_pairs={{0,8},{1,9},{2,10},{3,11},{4,12},{5,13},{6,14},{7,15},{8,40},{9,41... | collective-permute-start | bytes 786440 | tf_op jit(solution)/shard_map/ppermute | solution.py:141
  111.9 21.3 %collective-permute-start.9 = (bf16[256,512]{1,0:T(8,128)(2,1)}, bf16[256,512]{1,0:T(8,128)(2,1)S(1)}, u32[]{:S(2)}, u32[]{:S(2)}) collective-permute-start(bf16[256,512]{1,0:T(8,128)(2,1)} %shard_map.58), channel_id=1, source_target_pairs={{0,16},{1,17},{2,18},{3,19},{4,20},{5,21},{6,22},{7,23},{8,48},{9,... | collective-permute-start | bytes 786440 | tf_op jit(solution)/shard_map/ppermute | solution.py:141
  122.9 21.0 %collective-permute-start.10 = (bf16[256,512]{1,0:T(8,128)(2,1)}, bf16[256,512]{1,0:T(8,128)(2,1)S(1)}, u32[]{:S(2)}, u32[]{:S(2)}) collective-permute-start(bf16[256,512]{1,0:T(8,128)(2,1)} %shard_map.59), channel_id=1, source_target_pairs={{0,24},{1,25},{2,26},{3,27},{4,28},{5,29},{6,30},{7,31},{8,56},{9,... | collective-permute-start | bytes 786440 | tf_op jit(solution)/shard_map/ppermute | solution.py:141
Sparse Core Ops, SparseCore 0:
  31.7 46.9 all-gather.1

commit v6 on v2

v6 whole, which is shorter than its diff:
```python
import math

import jax
import jax.numpy as jnp
from jax import lax
from jax.experimental import pallas as pl
from jax.experimental.pallas import tpu as pltpu
from jax.sharding import PartitionSpec as P

REACH = 4
ALL = ("grp", "kv", "sx", "sy")
SX = 4


def doc_starts(lengths, position):
    count = lengths.shape[0]
    before = jnp.arange(count)[None, :] < jnp.arange(count)[:, None]
    starts = jnp.sum(jnp.where(before, lengths[None, :], 0), axis=1)
    chosen = jnp.where(starts[None, :] <= position[:, None], starts[None, :], 0)
    return jnp.max(chosen, axis=1)


def attend(queries, window_keys, window_values, query_pos, key_pos, lengths):
    token_count = queries.shape[0]
    head_size = window_keys.shape[1]
    heads = queries.shape[1] // head_size
    split = queries.reshape(token_count, heads, head_size)
    scores = jnp.einsum("thd,wd->htw", split, window_keys, preferred_element_type=jnp.float32)
    scores = scores * (1.0 / math.sqrt(head_size))
    first_key = doc_starts(lengths, query_pos)
    allowed = (key_pos[None, :] >= first_key[:, None]) & (key_pos[None, :] <= query_pos[:, None])
    scores = jnp.where(allowed[None], scores, -jnp.inf)
    peak = jnp.max(scores, axis=2, keepdims=True)
    weights = jnp.exp(scores - peak)
    total = jnp.sum(weights, axis=2)
    numer = jnp.einsum(
        "htw,wd->thd", weights.astype(jnp.bfloat16), window_values, preferred_element_type=jnp.float32
    )
    result = numer / jnp.transpose(total, (1, 0))[..., None]
    return result.astype(jnp.bfloat16).reshape(token_count, heads * head_size)


def fetch_behind(stacked, near, n_srv):
    route = []
    for c in range(2):
        distance = near + 2 * c
        route += [(c * n_srv + i - distance, c * n_srv + i) for i in range(distance, n_srv)]
    return lax.ppermute(stacked, ("grp", "sx", "sy"), route)


def product_kernel(place_ref, left_ref, right_ref, out_ref):
    rows, _, cores, tokens, depth = left_ref.shape
    left = jnp.concatenate(
        [jnp.concatenate([left_ref[h, 0, c] for c in range(cores)], axis=1) for h in range(rows)], axis=0
    )
    pieces, _, _, width = right_ref.shape
    for piece in range(pieces):
        total = jnp.dot(
            left, right_ref[piece].reshape(cores * depth, width), preferred_element_type=jnp.float32
        ).astype(out_ref.dtype)
        for h in range(rows):
            out_ref[h, :, piece * width : (piece + 1) * width] = total[h * tokens : (h + 1) * tokens]


def product(place, left, right):
    rows, _, cores, tokens, depth = left.shape
    pieces, _, _, width = right.shape
    tiles = pieces // 2
    grid_spec = pltpu.PrefetchScalarGridSpec(
        num_scalar_prefetch=1,
        grid=(tiles,),
        in_specs=[
            pl.BlockSpec((rows, 1, cores, tokens, depth), lambda j, place: (0, place[0], 0, 0, 0)),
            pl.BlockSpec((2, cores, depth, width), lambda j, place: (j, 0, 0, 0)),
        ],
        out_specs=pl.BlockSpec((rows, tokens, 2 * width), lambda j, place: ((j + place[1]) % tiles, 0, 0)),
    )
    return pl.pallas_call(
        product_kernel,
        grid_spec=grid_spec,
        out_shape=jax.ShapeDtypeStruct((tiles * rows, tokens, 2 * width), jnp.bfloat16),
        compiler_params=pltpu.CompilerParams(vmem_limit_bytes=58 * 2**20),
        cost_estimate=pl.CostEstimate(
            flops=2 * rows * tokens * right.size,
            bytes_accessed=2 * (left.size // 2 + right.size + tiles * rows * tokens * 2 * width),
            transcendentals=0,
        ),
    )(place, left, right)


def solution(mesh):
    n_grp, n_kv, n_srv = mesh.shape["grp"], mesh.shape["kv"], mesh.shape["srv"]
    sy = n_srv // SX
    sizes = (n_grp, n_kv, SX, sy)
    fine = jax.sharding.Mesh(mesh.devices.reshape(sizes), ALL)
    tiles = n_grp * n_kv // SX

    def index(*place):
        total = 0
        for at, size in zip(place, sizes):
            total = total * size + at
        return total

    def shift_of(x):
        return tiles - 1 + (x % 2) * (tiles // 2)

    to_owner = [[], []]
    for t in range(2):
        for c in range(n_grp):
            for z in range(n_kv):
                for x in range(SX):
                    j = (z // 2 - shift_of(x)) % tiles
                    to_x = 2 * (z % 2) + (c ^ t)
                    owner = x * tiles + j
                    for y in range(sy):
                        to_owner[t].append(
                            (index(c, z, x, y), index(owner // n_kv, owner % n_kv, to_x, y))
                        )

    def on_device(queries, keys, values, lengths, weight):
        tokens = queries.shape[0]
        core = lax.axis_index("grp")
        across = lax.axis_index("sx")
        shard = across * sy + lax.axis_index("sy")
        columns = lax.all_gather(weight[0], ("sy", "grp"), axis=0, tiled=True)
        columns = columns.reshape(sy, n_grp, weight.shape[1], weight.shape[2])

        stacked = jnp.stack([keys[:, 0], values[:, 0]])
        mine = jnp.concatenate([fetch_behind(stacked, 1, n_srv), fetch_behind(stacked, 2, n_srv)], axis=1)
        window = jnp.concatenate([mine, lax.ppermute(mine, "grp", [(0, 1), (1, 0)]), stacked], axis=1)
        behind = jnp.stack([1 + 2 * core, 2 + 2 * core, 3 - 2 * core, 4 - 2 * core, 0 * core])
        query_pos = shard * tokens + jnp.arange(tokens, dtype=jnp.int32)
        key_pos = ((shard - behind) * tokens)[:, None] + jnp.arange(tokens, dtype=jnp.int32)[None, :]
        heads = attend(queries[:, 0], window[0], window[1], query_pos, key_pos.reshape(-1), lengths)
        heads = lax.all_to_all(heads.reshape(n_grp, tokens // n_grp, heads.shape[1]), "grp", 0, 0)
        along = lax.all_to_all(jnp.broadcast_to(heads, (SX,) + heads.shape), "sx", 0, 0)
        along = along.reshape((SX // 2, 2) + heads.shape)

        partial = [product(jnp.stack([core ^ t, shift_of(across)]), along, columns) for t in range(2)]
        late = lax.psum_scatter(partial[1], "kv", scatter_dimension=0, tiled=True)[0]
        early = lax.all_to_all(partial[0], "kv", 0, 0, tiled=True)
        early = jnp.sum(early.astype(jnp.float32), axis=0).astype(jnp.bfloat16)
        early = lax.ppermute(early, ALL, to_owner[0])
        late = lax.ppermute(late, ALL, to_owner[1])
        even = across % 2 == 0
        return jnp.concatenate([jnp.where(even, early, late), jnp.where(even, late, early)], axis=0)

    q = P(("sx", "sy"), "kv", "grp")
    k = P(("sx", "sy"), "kv", None)
    placed = (q, k, k, P(), P("kv", "grp", ("sx", "sy")))
    return jax.shard_map(
        on_device, mesh=fine, in_specs=placed, out_specs=P(("sx", "sy"), ("grp", "kv")), check_vma=False
    )
```

time: 163 us -> 146 us (0.90)
  the two profiles are of different devices: /device:TPU:129 before, /device:TPU:6 now
where the time goes in v6:
time: 146 us; the launch traced here: 143 us
  blocking collectives  50.2 us (34%)
  waiting for transfers between devices  36.1 us (25%)
  starting transfers between devices  21.7 us (15%)
  between operations  13.5 us (9%)
  Pallas kernels  11.2 us (8%)
  other arithmetic  5.94 us (4%)
  local copies, waits for them, and re-layouts  2.42 us (2%)
  matrix products  1.98 us (1%)
    all_to_all x1, blocking collectives, on_device(): early = lax.all_to_all(partial[0], 'kv', 0, 0, tiled=True)  46.3 us
    all_to_all x1, waiting for transfers between devices, on_device(): lax.all_to_all(jnp.broadcast_to(heads, (SX,) + heads.shape), 'sx', 0, 0)  12.7 us
    pallas_call x2, Pallas kernels, product(): pl.pallas_call(product_kernel, grid_spec=grid_spec, out_shape=jax.ShapeDt...  11.2 us
    ppermute x1, waiting for transfers between devices, on_device(): early = lax.ppermute(early, ALL, to_owner[0])  9.18 us
    ppermute x2, waiting for transfers between devices, fetch_behind(): return lax.ppermute(stacked, ('grp', 'sx', 'sy'), route)  8.13 us
    ppermute x2, starting transfers between devices, fetch_behind(): return lax.ppermute(stacked, ('grp', 'sx', 'sy'), route)  7.98 us
    all_to_all x1, starting transfers between devices, on_device(): lax.all_to_all(jnp.broadcast_to(heads, (SX,) + heads.shape), 'sx', 0, 0)  4.72 us
    ppermute x1, starting transfers between devices, on_device(): late = lax.ppermute(late, ALL, to_owner[1])  4.62 us
  transfers between devices with their start and end apart: 8, of which 7 were waited for; matrix products, arithmetic and copies ran while one was open for 7% of the time, Pallas kernels for 4%

profile of v6, /device:TPU:6, one launch (start us, length us, event | category | flops | bytes accessed | tf_op | source)
XLA Modules:
  0.0 143.1 jit_solution(6093408015666427861)
XLA Ops:
  6.5 0.0 all-gather.3.cloned.1.call-start
  6.5 0.7 all-gather.3.cloned.1.call-update
  7.3 0.9 pad_maximum_fusion.2
  8.1 3.5 %collective-permute-start = (bf16[2,256,128]{2,1,0:T(8,128)(2,1)S(1)}, bf16[2,256,128]{2,1,0:T(8,128)(2,1)S(1)}, u32[]{:S(2)}, u32[]{:S(2)}) collective-permute-start(bf16[2,256,128]{2,1,0:T(8,128)(2,1)S(1)} %pad_maximum_fusion.2), channel_id=1, source_target_pairs={{0,1},{1,2},{2,3},{3,4},{4,5},{5,6},{6,7},{7,8},{8,9},{9,10},{10,1... | collective-permute-start | bytes 393224 | tf_op jit(solution)/shard_map/ppermute | solution.py:48
  11.6 4.5 %collective-permute-start.1 = (bf16[2,256,128]{2,1,0:T(8,128)(2,1)S(1)}, bf16[2,256,128]{2,1,0:T(8,128)(2,1)S(1)}, u32[]{:S(2)}, u32[]{:S(2)}) collective-permute-start(bf16[2,256,128]{2,1,0:T(8,128)(2,1)S(1)} %pad_maximum_fusion.2), channel_id=1, source_target_pairs={{0,2},{1,3},{2,4},{3,5},{4,6},{5,7},{6,8},{7,9},{8,10},{9,11},{10,... | collective-permute-start | bytes 393224 | tf_op jit(solution)/shard_map/ppermute | solution.py:48
  16.2 0.1 stack.42
  16.2 0.8 select_reduce_fusion.1
  17.0 0.1 iota_add_fusion
  17.1 1.0 reshape_squeeze.3
  18.1 0.1 select_reduce_fusion
  18.2 1.0 collective-permute-done
  19.2 7.2 %collective-permute-done.1 = bf16[2,256,128]{2,1,0:T(8,128)(2,1)S(1)} collective-permute-done((bf16[2,256,128]{2,1,0:T(8,128)(2,1)S(1)}, bf16[2,256,128]{2,1,0:T(8,128)(2,1)S(1)}, u32[]{:S(2)}, u32[]{:S(2)}) %collective-permute-start.1) | collective-permute-done | bytes 131104 | tf_op jit(solution)/shard_map/ppermute | solution.py:48
  26.4 2.5 %collective-permute-start.2 = (bf16[2,512,128]{2,1,0:T(8,128)(2,1)S(1)}, bf16[2,512,128]{2,1,0:T(8,128)(2,1)S(1)}, u32[]{:S(2)}, u32[]{:S(2)}) collective-permute-start(bf16[2,512,128]{2,1,0:T(8,128)(2,1)S(1)} %pad_maximum_fusion), channel_id=1, source_target_pairs={{0,256},{256,0},{1,257},{257,1},{2,258},{258,2},{3,259},{259,3},{4... | collective-permute-start | bytes 786440 | tf_op jit(solution)/shard_map/ppermute | solution.py:130
  28.9 0.3 compare_and_fusion
  29.2 0.8 collective-permute-done.2
  30.0 0.9 maximum_maximum_fusion
  30.9 1.0 fusion.15
  31.9 0.7 fusion
  32.6 1.0 fusion.11
  33.6 0.1 reshape_reshape.3
  33.7 3.9 %all_to_all.15 = bf16[2,128,512]{1,2,0:T(8,128)(2,1)S(1)} all-to-all(bf16[2,128,512]{1,2,0:T(8,128)(2,1)S(1)} %copy.18), channel_id=1, replica_groups=mesh['grp'=2,'kv'=8,'sx'=4,'sy'=8] {'grp'}, dimensions={0} | all-to-all | bytes 524288 | tf_op jit(solution)/shard_map/all_to_all | solution.py:135
  37.7 0.1 copy.19
  37.8 1.1 broadcast_in_dim.55
  38.9 4.7 %all-to-all-start.1 = ((bf16[4,2,128,512]{3,2,1,0:T(8,128)(2,1)}), bf16[4,2,128,512]{3,2,1,0:T(8,128)(2,1)S(1)}, u32[]{:S(2)}, u32[]{:S(2)}) async-start(bf16[4,2,128,512]{3,2,1,0:T(8,128)(2,1)} %broadcast_in_dim.55), calls=%async_computation.1 | async-start | bytes 2097152 | tf_op jit(solution)/shard_map/all_to_all | solution.py:136
  43.6 0.0 reduce-scatter.2.cloned.1.call-start
  43.6 0.6 pad_add_fusion.1.place_ref
  44.2 12.7 %all-to-all-done.1 = bf16[4,2,128,512]{3,2,1,0:T(8,128)(2,1)S(1)} async-done(((bf16[4,2,128,512]{3,2,1,0:T(8,128)(2,1)}), bf16[4,2,128,512]{3,2,1,0:T(8,128)(2,1)S(1)}, u32[]{:S(2)}, u32[]{:S(2)}) %all-to-all-start.1) | async-done | bytes 1048608 | tf_op jit(solution)/shard_map/all_to_all | solution.py:136
  57.0 0.0 copy-start
  57.0 1.7 %all-gather.3.cloned.1.call-done = bf16[1,8192,256]{2,1,0:T(8,128)(2,1)} async-done(((bf16[1,512,256]{2,1,0:T(8,128)(2,1)}), bf16[1,8192,256]{2,1,0:T(8,128)(2,1)}) %all-gather.3.cloned.1.call-update) | async-done | bytes 4194320 | tf_op jit(solution)/shard_map/all_gather | solution.py:125
  58.7 0.0 copy-done
  58.7 5.6 %shard_map.56 = bf16[8,128,512]{2,1,0:T(8,128)(2,1)} custom-call(s32[2]{0:T(128)} %pad_add_fusion.1.place_ref, bf16[2,2,2,128,512]{4,3,2,1,0:T(8,128)(2,1)} %bitcast.38, bf16[8,2,512,256]{3,2,1,0:T(8,128)(2,1)} %bitcast.36), custom_call_target="tpu_custom_call" | custom-call | flops 1073741824 | bytes 5767168 | tf_op jit(solution)/shard_map/pallas_call | solution.py:78
  64.3 0.0 reduce-scatter.2.cloned.1.call-update
  64.3 0.7 pad_add_fusion.place_ref
  65.0 5.6 %shard_map.55 = bf16[8,128,512]{2,1,0:T(8,128)(2,1)} custom-call(s32[2]{0:T(128)} %pad_add_fusion.place_ref, bf16[2,2,2,128,512]{4,3,2,1,0:T(8,128)(2,1)} %bitcast.39, bf16[8,2,512,256]{3,2,1,0:T(8,128)(2,1)} %bitcast.37), custom_call_target="tpu_custom_call" | custom-call | flops 1073741824 | bytes 5767168 | tf_op jit(solution)/shard_map/pallas_call | solution.py:78
  70.6 46.3 %all_to_all.16 = bf16[8,128,512]{2,1,0:T(8,128)(2,1)S(1)} all-to-all(bf16[8,128,512]{2,1,0:T(8,128)(2,1)} %shard_map.55), channel_id=1, replica_groups=mesh['grp'=2,'kv'=8,'sx'=4,'sy'=8] {'kv'}, dimensions={0} | all-to-all | bytes 2097152 | tf_op jit(solution)/shard_map/all_to_all | solution.py:141
  116.9 0.1 reduce_sum.32
  117.0 1.9 %collective-permute-start.3 = (bf16[128,512]{1,0:T(8,128)(2,1)S(1)}, bf16[128,512]{1,0:T(8,128)(2,1)S(1)}, u32[]{:S(2)}, u32[]{:S(2)}) collective-permute-start(bf16[128,512]{1,0:T(8,128)(2,1)S(1)} %reduce_sum.32), channel_id=1, source_target_pairs={{0,32},{1,33},{2,34},{3,35},{4,36},{5,37},{6,38},{7,39},{8,224},{9... | collective-permute-start | bytes 393224 | tf_op jit(solution)/shard_map/ppermute | solution.py:143
  118.9 0.0 reduce-scatter.2.cloned.1.call-done
  119.0 4.6 %collective-permute-start.4 = (bf16[128,512]{1,0:T(8,128)(2,1)}, bf16[128,512]{1,0:T(8,128)(2,1)S(1)}, u32[]{:S(2)}, u32[]{:S(2)}) collective-permute-start(bf16[128,512]{1,0:T(8,128)(2,1)} %bitcast.45), channel_id=1, source_target_pairs={{0,40},{1,41},{2,42},{3,43},{4,44},{5,45},{6,46},{7,47},{8,232},{9... | collective-permute-start | bytes 393224 | tf_op jit(solution)/shard_map/ppermute | solution.py:144
  123.6 9.2 %collective-permute-done.3 = bf16[128,512]{1,0:T(8,128)(2,1)S(1)} collective-permute-done((bf16[128,512]{1,0:T(8,128)(2,1)S(1)}, bf16[128,512]{1,0:T(8,128)(2,1)S(1)}, u32[]{:S(2)}, u32[]{:S(2)}) %collective-permute-start.3) | collective-permute-done | bytes 131104 | tf_op jit(solution)/shard_map/ppermute | solution.py:143
  132.8 2.7 %collective-permute-done.4 = bf16[128,512]{1,0:T(8,128)(2,1)S(1)} collective-permute-done((bf16[128,512]{1,0:T(8,128)(2,1)}, bf16[128,512]{1,0:T(8,128)(2,1)S(1)}, u32[]{:S(2)}, u32[]{:S(2)}) %collective-permute-start.4) | collective-permute-done | bytes 131104 | tf_op jit(solution)/shard_map/ppermute | solution.py:144
  135.6 0.7 pad_maximum_fusion.1
  (6 shorter events, 0.1 us)
Async XLA Ops:
  6.5 52.1 %all-gather.3.cloned.1.call-start = ((), (), s32[]{:S(2)}) async-start(), calls=%async_computation.5 | async-start | bytes 4456448 | tf_op jit(solution)/shard_map/all_gather | solution.py:125
  8.1 11.0 %collective-permute-start = (bf16[2,256,128]{2,1,0:T(8,128)(2,1)S(1)}, bf16[2,256,128]{2,1,0:T(8,128)(2,1)S(1)}, u32[]{:S(2)}, u32[]{:S(2)}) collective-permute-start(bf16[2,256,128]{2,1,0:T(8,128)(2,1)S(1)} %pad_maximum_fusion.2), channel_id=1, source_target_pairs={{0,1},{1,2},{2,3},{3,4},{4,5},{5,6},{6,7},{7,8},{8,9},{9,10},{10,1... | collective-permute-start | bytes 393224 | tf_op jit(solution)/shard_map/ppermute | solution.py:48
  11.6 14.7 %collective-permute-start.1 = (bf16[2,256,128]{2,1,0:T(8,128)(2,1)S(1)}, bf16[2,256,128]{2,1,0:T(8,128)(2,1)S(1)}, u32[]{:S(2)}, u32[]{:S(2)}) collective-permute-start(bf16[2,256,128]{2,1,0:T(8,128)(2,1)S(1)} %pad_maximum_fusion.2), channel_id=1, source_target_pairs={{0,2},{1,3},{2,4},{3,5},{4,6},{5,7},{6,8},{7,9},{8,10},{9,11},{10,... | collective-permute-start | bytes 393224 | tf_op jit(solution)/shard_map/ppermute | solution.py:48
  26.4 3.6 %collective-permute-start.2 = (bf16[2,512,128]{2,1,0:T(8,128)(2,1)S(1)}, bf16[2,512,128]{2,1,0:T(8,128)(2,1)S(1)}, u32[]{:S(2)}, u32[]{:S(2)}) collective-permute-start(bf16[2,512,128]{2,1,0:T(8,128)(2,1)S(1)} %pad_maximum_fusion), channel_id=1, source_target_pairs={{0,256},{256,0},{1,257},{257,1},{2,258},{258,2},{3,259},{259,3},{4... | collective-permute-start | bytes 786440 | tf_op jit(solution)/shard_map/ppermute | solution.py:130
  38.9 18.1 %all-to-all-start.1 = ((bf16[4,2,128,512]{3,2,1,0:T(8,128)(2,1)}), bf16[4,2,128,512]{3,2,1,0:T(8,128)(2,1)S(1)}, u32[]{:S(2)}, u32[]{:S(2)}) async-start(bf16[4,2,128,512]{3,2,1,0:T(8,128)(2,1)} %broadcast_in_dim.55), calls=%async_computation.1 | async-start | bytes 2097152 | tf_op jit(solution)/shard_map/all_to_all | solution.py:136
  43.6 75.4 %reduce-scatter.2.cloned.1.call-start = ((), (), s32[]{:S(2)}) async-start(), calls=%async_computation.4 | async-start | bytes 1179648 | tf_op jit(solution)/shard_map/reduce_scatter | solution.py:140
  57.0 1.7 %copy-start = (bf16[4,2,128,512]{3,2,1,0:T(8,128)(2,1)}, bf16[4,2,128,512]{3,2,1,0:T(8,128)(2,1)S(1)}, u32[]{:S(2)}) copy-start(bf16[4,2,128,512]{3,2,1,0:T(8,128)(2,1)S(1)} %all-to-all-done.1) | copy-start | bytes 3145732
  117.0 15.8 %collective-permute-start.3 = (bf16[128,512]{1,0:T(8,128)(2,1)S(1)}, bf16[128,512]{1,0:T(8,128)(2,1)S(1)}, u32[]{:S(2)}, u32[]{:S(2)}) collective-permute-start(bf16[128,512]{1,0:T(8,128)(2,1)S(1)} %reduce_sum.32), channel_id=1, source_target_pairs={{0,32},{1,33},{2,34},{3,35},{4,36},{5,37},{6,38},{7,39},{8,224},{9... | collective-permute-start | bytes 393224 | tf_op jit(solution)/shard_map/ppermute | solution.py:143
  119.0 16.6 %collective-permute-start.4 = (bf16[128,512]{1,0:T(8,128)(2,1)}, bf16[128,512]{1,0:T(8,128)(2,1)S(1)}, u32[]{:S(2)}, u32[]{:S(2)}) collective-permute-start(bf16[128,512]{1,0:T(8,128)(2,1)} %bitcast.45), channel_id=1, source_target_pairs={{0,40},{1,41},{2,42},{3,43},{4,44},{5,45},{6,46},{7,47},{8,232},{9... | collective-permute-start | bytes 393224 | tf_op jit(solution)/shard_map/ppermute | solution.py:144
Sparse Core Ops, SparseCore 0:
  9.5 49.1 all-gather.2
  64.4 53.7 reduce-scatter.1

commit v7 on v6

--- a/solution.py
+++ b/solution.py
@@ -1,3 +1,4 @@
+import functools
 import math
 
 import jax
@@ -48,16 +49,16 @@
     return lax.ppermute(stacked, ("grp", "sx", "sy"), route)
 
 
-def product_kernel(place_ref, left_ref, right_ref, out_ref):
+def product_kernel(place_ref, left_ref, *refs):
+    *right_refs, out_ref = refs
     rows, _, cores, tokens, depth = left_ref.shape
     left = jnp.concatenate(
         [jnp.concatenate([left_ref[h, 0, c] for c in range(cores)], axis=1) for h in range(rows)], axis=0
     )
-    pieces, _, _, width = right_ref.shape
-    for piece in range(pieces):
-        total = jnp.dot(
-            left, right_ref[piece].reshape(cores * depth, width), preferred_element_type=jnp.float32
-        ).astype(out_ref.dtype)
+    for piece in range(2):
+        right = jnp.concatenate([right_refs[piece * cores + c][0, 0] for c in range(cores)], axis=0)
+        width = right.shape[1]
+        total = jnp.dot(left, right, preferred_element_type=jnp.float32).astype(out_ref.dtype)
         for h in range(rows):
             out_ref[h, :, piece * width : (piece + 1) * width] = total[h * tokens : (h + 1) * tokens]
 
@@ -71,7 +72,11 @@
         grid=(tiles,),
         in_specs=[
             pl.BlockSpec((rows, 1, cores, tokens, depth), lambda j, place: (0, place[0], 0, 0, 0)),
-            pl.BlockSpec((2, cores, depth, width), lambda j, place: (j, 0, 0, 0)),
+        ]
+        + [
+            pl.BlockSpec((1, 1, depth, width), functools.partial(lambda p, c, j, place: (2 * j + p, c, 0, 0), p, c))
+            for p in range(2)
+            for c in range(cores)
         ],
         out_specs=pl.BlockSpec((rows, tokens, 2 * width), lambda j, place: ((j + place[1]) % tiles, 0, 0)),
     )
@@ -85,7 +90,7 @@
             bytes_accessed=2 * (left.size // 2 + right.size + tiles * rows * tokens * 2 * width),
             transcendentals=0,
         ),
-    )(place, left, right)
+    )(place, left, *[right] * (2 * cores))
 
 
 def solution(mesh):
@@ -137,11 +142,12 @@
         along = along.reshape((SX // 2, 2) + heads.shape)
 
         partial = [product(jnp.stack([core ^ t, shift_of(across)]), along, columns) for t in range(2)]
-        late = lax.psum_scatter(partial[1], "kv", scatter_dimension=0, tiled=True)[0]
-        early = lax.all_to_all(partial[0], "kv", 0, 0, tiled=True)
-        early = jnp.sum(early.astype(jnp.float32), axis=0).astype(jnp.bfloat16)
-        early = lax.ppermute(early, ALL, to_owner[0])
-        late = lax.ppermute(late, ALL, to_owner[1])
+        tiles_in = []
+        for t in range(2):
+            terms = lax.all_to_all(partial[t], "kv", 0, 0, tiled=True)
+            tile = jnp.sum(terms.astype(jnp.float32), axis=0).astype(jnp.bfloat16)
+            tiles_in.append(lax.ppermute(tile, ALL, to_owner[t]))
+        early, late = tiles_in
         even = across % 2 == 0
         return jnp.concatenate([jnp.where(even, early, late), jnp.where(even, late, early)], axis=0)
 

time: 146 us -> 158 us (1.082)
  blocking collectives: 50.2 us -> 3.94 us
  waiting for transfers between devices: 36.1 us -> 80.6 us
  starting transfers between devices: 21.7 us -> 36.3 us
    all_to_all x1 -> x0, blocking collectives: 46.3 us -> none  [on_device(): early = lax.all_to_all(partial[0], 'kv', 0, 0, tiled=True)]
    all_to_all x0 -> x2, waiting for transfers between devices: none -> 44.8 us  [on_device(): terms = lax.all_to_all(partial[t], 'kv', 0, 0, tiled=True)]
    all_to_all x0 -> x2, starting transfers between devices: none -> 13.2 us  [on_device(): terms = lax.all_to_all(partial[t], 'kv', 0, 0, tiled=True)]
  transfers between devices with their start and end apart: 8 -> 9, of which waited for: 7 -> 9; matrix products, arithmetic and copies ran while one was open for 7% -> 6% of each run, Pallas kernels for 4% -> 4%
where the time goes in v7:
time: 158 us; the launch traced here: 156 us
  waiting for transfers between devices  80.6 us (51%)
  starting transfers between devices  36.3 us (23%)
  between operations  13.5 us (9%)
  Pallas kernels  11.2 us (7%)
  other arithmetic  6.1 us (4%)
  blocking collectives  3.94 us (2%)
  local copies, waits for them, and re-layouts  2.42 us (2%)
  matrix products  1.98 us (1%)
    all_to_all x2, waiting for transfers between devices, on_device(): terms = lax.all_to_all(partial[t], 'kv', 0, 0, tiled=True)  44.8 us
    all_to_all x2, starting transfers between devices, on_device(): terms = lax.all_to_all(partial[t], 'kv', 0, 0, tiled=True)  13.2 us
    all_to_all x1, waiting for transfers between devices, on_device(): lax.all_to_all(jnp.broadcast_to(heads, (SX,) + heads.shape), 'sx', 0, 0)  12.7 us
    ppermute x2, waiting for transfers between devices, on_device(): tiles_in.append(lax.ppermute(tile, ALL, to_owner[t]))  11.7 us
    pallas_call x2, Pallas kernels, product(): pl.pallas_call(product_kernel, grid_spec=grid_spec, out_shape=jax.ShapeDt...  11.2 us
    ppermute x2, waiting for transfers between devices, fetch_behind(): return lax.ppermute(stacked, ('grp', 'sx', 'sy'), route)  8.13 us
    ppermute x2, starting transfers between devices, fetch_behind(): return lax.ppermute(stacked, ('grp', 'sx', 'sy'), route)  7.98 us
    ppermute x2, starting transfers between devices, on_device(): tiles_in.append(lax.ppermute(tile, ALL, to_owner[t]))  7.84 us
  transfers between devices with their start and end apart: 9, of which 9 were waited for; matrix products, arithmetic and copies ran while one was open for 6% of the time, Pallas kernels for 4%

profile of v7, /device:TPU:6, one launch (start us, length us, event | category | flops | bytes accessed | tf_op | source)
XLA Modules:
  0.0 156.0 jit_solution(2749875265191228718)
XLA Ops:
  6.5 0.0 all-gather.3.cloned.1.call-start
  6.5 0.7 all-gather.3.cloned.1.call-update
  7.3 0.9 pad_maximum_fusion.2
  8.1 3.5 %collective-permute-start = (bf16[2,256,128]{2,1,0:T(8,128)(2,1)S(1)}, bf16[2,256,128]{2,1,0:T(8,128)(2,1)S(1)}, u32[]{:S(2)}, u32[]{:S(2)}) collective-permute-start(bf16[2,256,128]{2,1,0:T(8,128)(2,1)S(1)} %pad_maximum_fusion.2), channel_id=1, source_target_pairs={{0,1},{1,2},{2,3},{3,4},{4,5},{5,6},{6,7},{7,8},{8,9},{9,10},{10,1... | collective-permute-start | bytes 393224 | tf_op jit(solution)/shard_map/ppermute | solution.py:49
  11.6 4.5 %collective-permute-start.1 = (bf16[2,256,128]{2,1,0:T(8,128)(2,1)S(1)}, bf16[2,256,128]{2,1,0:T(8,128)(2,1)S(1)}, u32[]{:S(2)}, u32[]{:S(2)}) collective-permute-start(bf16[2,256,128]{2,1,0:T(8,128)(2,1)S(1)} %pad_maximum_fusion.2), channel_id=1, source_target_pairs={{0,2},{1,3},{2,4},{3,5},{4,6},{5,7},{6,8},{7,9},{8,10},{9,11},{10,... | collective-permute-start | bytes 393224 | tf_op jit(solution)/shard_map/ppermute | solution.py:49
  16.2 0.1 stack.42
  16.2 0.8 select_reduce_fusion.1
  17.0 0.1 iota_add_fusion
  17.1 1.0 reshape_squeeze.3
  18.1 0.1 select_reduce_fusion
  18.2 1.0 collective-permute-done
  19.2 7.2 %collective-permute-done.1 = bf16[2,256,128]{2,1,0:T(8,128)(2,1)S(1)} collective-permute-done((bf16[2,256,128]{2,1,0:T(8,128)(2,1)S(1)}, bf16[2,256,128]{2,1,0:T(8,128)(2,1)S(1)}, u32[]{:S(2)}, u32[]{:S(2)}) %collective-permute-start.1) | collective-permute-done | bytes 131104 | tf_op jit(solution)/shard_map/ppermute | solution.py:49
  26.4 2.5 %collective-permute-start.2 = (bf16[2,512,128]{2,1,0:T(8,128)(2,1)S(1)}, bf16[2,512,128]{2,1,0:T(8,128)(2,1)S(1)}, u32[]{:S(2)}, u32[]{:S(2)}) collective-permute-start(bf16[2,512,128]{2,1,0:T(8,128)(2,1)S(1)} %pad_maximum_fusion), channel_id=1, source_target_pairs={{0,256},{256,0},{1,257},{257,1},{2,258},{258,2},{3,259},{259,3},{4... | collective-permute-start | bytes 786440 | tf_op jit(solution)/shard_map/ppermute | solution.py:135
  28.9 0.3 compare_and_fusion
  29.2 0.8 collective-permute-done.2
  30.0 0.9 maximum_maximum_fusion
  30.9 1.0 fusion.15
  31.9 0.7 fusion
  32.6 1.0 fusion.11
  33.6 0.1 reshape_reshape.3
  33.7 3.9 %all_to_all.20 = bf16[2,128,512]{1,2,0:T(8,128)(2,1)S(1)} all-to-all(bf16[2,128,512]{1,2,0:T(8,128)(2,1)S(1)} %copy.18), channel_id=1, replica_groups=mesh['grp'=2,'kv'=8,'sx'=4,'sy'=8] {'grp'}, dimensions={0} | all-to-all | bytes 524288 | tf_op jit(solution)/shard_map/all_to_all | solution.py:140
  37.7 0.1 copy.19
  37.8 1.1 broadcast_in_dim.55
  38.9 4.7 %all-to-all-start.1 = ((bf16[4,2,128,512]{3,2,1,0:T(8,128)(2,1)}), bf16[4,2,128,512]{3,2,1,0:T(8,128)(2,1)S(1)}, u32[]{:S(2)}, u32[]{:S(2)}) async-start(bf16[4,2,128,512]{3,2,1,0:T(8,128)(2,1)} %broadcast_in_dim.55), calls=%async_computation.1 | async-start | bytes 2097152 | tf_op jit(solution)/shard_map/all_to_all | solution.py:141
  43.6 0.6 pad_add_fusion.1.place_ref
  44.2 12.7 %all-to-all-done.1 = bf16[4,2,128,512]{3,2,1,0:T(8,128)(2,1)S(1)} async-done(((bf16[4,2,128,512]{3,2,1,0:T(8,128)(2,1)}), bf16[4,2,128,512]{3,2,1,0:T(8,128)(2,1)S(1)}, u32[]{:S(2)}, u32[]{:S(2)}) %all-to-all-start.1) | async-done | bytes 1048608 | tf_op jit(solution)/shard_map/all_to_all | solution.py:141
  57.0 0.0 copy-start
  57.0 1.7 %all-gather.3.cloned.1.call-done = bf16[1,8192,256]{2,1,0:T(8,128)(2,1)} async-done(((bf16[1,512,256]{2,1,0:T(8,128)(2,1)}), bf16[1,8192,256]{2,1,0:T(8,128)(2,1)}) %all-gather.3.cloned.1.call-update) | async-done | bytes 4194320 | tf_op jit(solution)/shard_map/all_gather | solution.py:130
  58.7 0.0 copy-done
  58.7 5.6 %shard_map.56 = bf16[8,128,512]{2,1,0:T(8,128)(2,1)} custom-call(s32[2]{0:T(128)} %pad_add_fusion.1.place_ref, bf16[2,2,2,128,512]{4,3,2,1,0:T(8,128)(2,1)} %bitcast.43, bf16[8,2,512,256]{3,2,1,0:T(8,128)(2,1)} %bitcast.35, bf16[8,2,512,256]{3,2,1,0:T(8,128)(2,1)} %bitcast.36, bf16[8,2,512,256]{3,2,1,0:T(8,128)(2,1)} %bitcast.37, ...), custom_call_target="tpu_custom_call" | custom-call | flops 1073741824 | bytes 5767168 | tf_op jit(solution)/shard_map/pallas_call | solution.py:83
  64.3 9.7 %all-to-all-start.3 = ((bf16[8,128,512]{2,1,0:T(8,128)(2,1)}), bf16[8,128,512]{2,1,0:T(8,128)(2,1)S(1)}, u32[]{:S(2)}, u32[]{:S(2)}) async-start(bf16[8,128,512]{2,1,0:T(8,128)(2,1)} %shard_map.56), calls=%async_computation.3 | async-start | bytes 2097152 | tf_op jit(solution)/shard_map/all_to_all | solution.py:147
  73.9 0.7 pad_add_fusion.place_ref
  74.6 5.6 %shard_map.55 = bf16[8,128,512]{2,1,0:T(8,128)(2,1)} custom-call(s32[2]{0:T(128)} %pad_add_fusion.place_ref, bf16[2,2,2,128,512]{4,3,2,1,0:T(8,128)(2,1)} %bitcast.44, bf16[8,2,512,256]{3,2,1,0:T(8,128)(2,1)} %bitcast.39, bf16[8,2,512,256]{3,2,1,0:T(8,128)(2,1)} %bitcast.40, bf16[8,2,512,256]{3,2,1,0:T(8,128)(2,1)} %bitcast.41, bf16[8,2,512,256]{3,2,1,0:T(8,128)(2,1)} %bitcast.42), custom_call_target="tpu_custom_call" | custom-call | flops 1073741824 | bytes 5767168 | tf_op jit(solution)/shard_map/pallas_call | solution.py:83
  80.2 21.6 %all-to-all-done.3 = bf16[8,128,512]{2,1,0:T(8,128)(2,1)S(1)} async-done(((bf16[8,128,512]{2,1,0:T(8,128)(2,1)}), bf16[8,128,512]{2,1,0:T(8,128)(2,1)S(1)}, u32[]{:S(2)}, u32[]{:S(2)}) %all-to-all-start.3) | async-done | bytes 1048608 | tf_op jit(solution)/shard_map/all_to_all | solution.py:147
  101.8 3.6 %all-to-all-start.2 = ((bf16[8,128,512]{2,1,0:T(8,128)(2,1)}), bf16[8,128,512]{2,1,0:T(8,128)(2,1)S(1)}, u32[]{:S(2)}, u32[]{:S(2)}) async-start(bf16[8,128,512]{2,1,0:T(8,128)(2,1)} %shard_map.55), calls=%async_computation.2 | async-start | bytes 2097152 | tf_op jit(solution)/shard_map/all_to_all | solution.py:147
  105.4 0.1 reduce_sum.45
  105.6 5.9 %collective-permute-start.4 = (bf16[128,512]{1,0:T(8,128)(2,1)S(1)}, bf16[128,512]{1,0:T(8,128)(2,1)S(1)}, u32[]{:S(2)}, u32[]{:S(2)}) collective-permute-start(bf16[128,512]{1,0:T(8,128)(2,1)S(1)} %reduce_sum.45), channel_id=1, source_target_pairs={{0,40},{1,41},{2,42},{3,43},{4,44},{5,45},{6,46},{7,47},{8,232},{9... | collective-permute-start | bytes 393224 | tf_op jit(solution)/shard_map/ppermute | solution.py:149
  111.5 23.2 %all-to-all-done.2 = bf16[8,128,512]{2,1,0:T(8,128)(2,1)S(1)} async-done(((bf16[8,128,512]{2,1,0:T(8,128)(2,1)}), bf16[8,128,512]{2,1,0:T(8,128)(2,1)S(1)}, u32[]{:S(2)}, u32[]{:S(2)}) %all-to-all-start.2) | async-done | bytes 1048608 | tf_op jit(solution)/shard_map/all_to_all | solution.py:147
  134.6 0.1 reduce_sum.44
  134.8 1.9 %collective-permute-start.3 = (bf16[128,512]{1,0:T(8,128)(2,1)S(1)}, bf16[128,512]{1,0:T(8,128)(2,1)S(1)}, u32[]{:S(2)}, u32[]{:S(2)}) collective-permute-start(bf16[128,512]{1,0:T(8,128)(2,1)S(1)} %reduce_sum.44), channel_id=1, source_target_pairs={{0,32},{1,33},{2,34},{3,35},{4,36},{5,37},{6,38},{7,39},{8,224},{9... | collective-permute-start | bytes 393224 | tf_op jit(solution)/shard_map/ppermute | solution.py:149
  136.7 2.3 %collective-permute-done.4 = bf16[128,512]{1,0:T(8,128)(2,1)S(1)} collective-permute-done((bf16[128,512]{1,0:T(8,128)(2,1)S(1)}, bf16[128,512]{1,0:T(8,128)(2,1)S(1)}, u32[]{:S(2)}, u32[]{:S(2)}) %collective-permute-start.4) | collective-permute-done | bytes 131104 | tf_op jit(solution)/shard_map/ppermute | solution.py:149
  139.0 9.4 %collective-permute-done.3 = bf16[128,512]{1,0:T(8,128)(2,1)S(1)} collective-permute-done((bf16[128,512]{1,0:T(8,128)(2,1)S(1)}, bf16[128,512]{1,0:T(8,128)(2,1)S(1)}, u32[]{:S(2)}, u32[]{:S(2)}) %collective-permute-start.3) | collective-permute-done | bytes 131104 | tf_op jit(solution)/shard_map/ppermute | solution.py:149
  148.5 0.7 pad_maximum_fusion.1
  (6 shorter events, 0.1 us)
Async XLA Ops:
  6.5 52.1 %all-gather.3.cloned.1.call-start = ((), (), s32[]{:S(2)}) async-start(), calls=%async_computation.4 | async-start | bytes 4456448 | tf_op jit(solution)/shard_map/all_gather | solution.py:130
  8.1 11.0 %collective-permute-start = (bf16[2,256,128]{2,1,0:T(8,128)(2,1)S(1)}, bf16[2,256,128]{2,1,0:T(8,128)(2,1)S(1)}, u32[]{:S(2)}, u32[]{:S(2)}) collective-permute-start(bf16[2,256,128]{2,1,0:T(8,128)(2,1)S(1)} %pad_maximum_fusion.2), channel_id=1, source_target_pairs={{0,1},{1,2},{2,3},{3,4},{4,5},{5,6},{6,7},{7,8},{8,9},{9,10},{10,1... | collective-permute-start | bytes 393224 | tf_op jit(solution)/shard_map/ppermute | solution.py:49
  11.6 14.7 %collective-permute-start.1 = (bf16[2,256,128]{2,1,0:T(8,128)(2,1)S(1)}, bf16[2,256,128]{2,1,0:T(8,128)(2,1)S(1)}, u32[]{:S(2)}, u32[]{:S(2)}) collective-permute-start(bf16[2,256,128]{2,1,0:T(8,128)(2,1)S(1)} %pad_maximum_fusion.2), channel_id=1, source_target_pairs={{0,2},{1,3},{2,4},{3,5},{4,6},{5,7},{6,8},{7,9},{8,10},{9,11},{10,... | collective-permute-start | bytes 393224 | tf_op jit(solution)/shard_map/ppermute | solution.py:49
  26.4 3.6 %collective-permute-start.2 = (bf16[2,512,128]{2,1,0:T(8,128)(2,1)S(1)}, bf16[2,512,128]{2,1,0:T(8,128)(2,1)S(1)}, u32[]{:S(2)}, u32[]{:S(2)}) collective-permute-start(bf16[2,512,128]{2,1,0:T(8,128)(2,1)S(1)} %pad_maximum_fusion), channel_id=1, source_target_pairs={{0,256},{256,0},{1,257},{257,1},{2,258},{258,2},{3,259},{259,3},{4... | collective-permute-start | bytes 786440 | tf_op jit(solution)/shard_map/ppermute | solution.py:135
  38.9 18.1 %all-to-all-start.1 = ((bf16[4,2,128,512]{3,2,1,0:T(8,128)(2,1)}), bf16[4,2,128,512]{3,2,1,0:T(8,128)(2,1)S(1)}, u32[]{:S(2)}, u32[]{:S(2)}) async-start(bf16[4,2,128,512]{3,2,1,0:T(8,128)(2,1)} %broadcast_in_dim.55), calls=%async_computation.1 | async-start | bytes 2097152 | tf_op jit(solution)/shard_map/all_to_all | solution.py:141
  57.0 1.7 %copy-start = (bf16[4,2,128,512]{3,2,1,0:T(8,128)(2,1)}, bf16[4,2,128,512]{3,2,1,0:T(8,128)(2,1)S(1)}, u32[]{:S(2)}) copy-start(bf16[4,2,128,512]{3,2,1,0:T(8,128)(2,1)S(1)} %all-to-all-done.1) | copy-start | bytes 3145732
  64.3 37.6 %all-to-all-start.3 = ((bf16[8,128,512]{2,1,0:T(8,128)(2,1)}), bf16[8,128,512]{2,1,0:T(8,128)(2,1)S(1)}, u32[]{:S(2)}, u32[]{:S(2)}) async-start(bf16[8,128,512]{2,1,0:T(8,128)(2,1)} %shard_map.56), calls=%async_computation.3 | async-start | bytes 2097152 | tf_op jit(solution)/shard_map/all_to_all | solution.py:147
  101.8 32.8 %all-to-all-start.2 = ((bf16[8,128,512]{2,1,0:T(8,128)(2,1)}), bf16[8,128,512]{2,1,0:T(8,128)(2,1)S(1)}, u32[]{:S(2)}, u32[]{:S(2)}) async-start(bf16[8,128,512]{2,1,0:T(8,128)(2,1)} %shard_map.55), calls=%async_computation.2 | async-start | bytes 2097152 | tf_op jit(solution)/shard_map/all_to_all | solution.py:147
  105.6 33.4 %collective-permute-start.4 = (bf16[128,512]{1,0:T(8,128)(2,1)S(1)}, bf16[128,512]{1,0:T(8,128)(2,1)S(1)}, u32[]{:S(2)}, u32[]{:S(2)}) collective-permute-start(bf16[128,512]{1,0:T(8,128)(2,1)S(1)} %reduce_sum.45), channel_id=1, source_target_pairs={{0,40},{1,41},{2,42},{3,43},{4,44},{5,45},{6,46},{7,47},{8,232},{9... | collective-permute-start | bytes 393224 | tf_op jit(solution)/shard_map/ppermute | solution.py:149
  134.8 13.7 %collective-permute-start.3 = (bf16[128,512]{1,0:T(8,128)(2,1)S(1)}, bf16[128,512]{1,0:T(8,128)(2,1)S(1)}, u32[]{:S(2)}, u32[]{:S(2)}) collective-permute-start(bf16[128,512]{1,0:T(8,128)(2,1)S(1)} %reduce_sum.44), channel_id=1, source_target_pairs={{0,32},{1,33},{2,34},{3,35},{4,36},{5,37},{6,38},{7,39},{8,224},{9... | collective-permute-start | bytes 393224 | tf_op jit(solution)/shard_map/ppermute | solution.py:149
Sparse Core Ops, SparseCore 0:
  9.5 49.1 all-gather.2

commit v8 on v6

--- a/solution.py
+++ b/solution.py
@@ -48,44 +48,49 @@
     return lax.ppermute(stacked, ("grp", "sx", "sy"), route)
 
 
-def product_kernel(place_ref, left_ref, right_ref, out_ref):
-    rows, _, cores, tokens, depth = left_ref.shape
-    left = jnp.concatenate(
-        [jnp.concatenate([left_ref[h, 0, c] for c in range(cores)], axis=1) for h in range(rows)], axis=0
-    )
-    pieces, _, _, width = right_ref.shape
-    for piece in range(pieces):
-        total = jnp.dot(
-            left, right_ref[piece].reshape(cores * depth, width), preferred_element_type=jnp.float32
-        ).astype(out_ref.dtype)
-        for h in range(rows):
-            out_ref[h, :, piece * width : (piece + 1) * width] = total[h * tokens : (h + 1) * tokens]
+def product_kernel(place_ref, left_ref, own_ref, other_ref, out_ref):
+    blocks, tokens, depth = left_ref.shape
+    left = left_ref[...].reshape(blocks * tokens, depth)
+    half = depth // 2
+    core = place_ref[0]
+    for piece in range(own_ref.shape[0]):
+        total = jnp.dot(left[:, :half], own_ref[piece, 0], preferred_element_type=jnp.float32)
+        total += jnp.dot(left[:, half:], other_ref[piece, 0], preferred_element_type=jnp.float32)
+        total = total.astype(out_ref.dtype)
+        width = total.shape[1]
+        for x in range(blocks):
+            out_ref[x // 2, (x % 2) ^ core, :, piece * width : (piece + 1) * width] = total[
+                x * tokens : (x + 1) * tokens
+            ]
 
 
 def product(place, left, right):
-    rows, _, cores, tokens, depth = left.shape
-    pieces, _, _, width = right.shape
+    blocks, tokens, depth = left.shape
+    pieces, _, half, width = right.shape
     tiles = pieces // 2
     grid_spec = pltpu.PrefetchScalarGridSpec(
         num_scalar_prefetch=1,
         grid=(tiles,),
         in_specs=[
-            pl.BlockSpec((rows, 1, cores, tokens, depth), lambda j, place: (0, place[0], 0, 0, 0)),
-            pl.BlockSpec((2, cores, depth, width), lambda j, place: (j, 0, 0, 0)),
+            pl.BlockSpec((blocks, tokens, depth), lambda j, place: (0, 0, 0)),
+            pl.BlockSpec((2, 1, half, width), lambda j, place: (j, place[0], 0, 0)),
+            pl.BlockSpec((2, 1, half, width), lambda j, place: (j, 1 - place[0], 0, 0)),
         ],
-        out_specs=pl.BlockSpec((rows, tokens, 2 * width), lambda j, place: ((j + place[1]) % tiles, 0, 0)),
+        out_specs=pl.BlockSpec(
+            (blocks // 2, 2, tokens, 2 * width), lambda j, place: ((j + place[1]) % tiles, 0, 0, 0)
+        ),
     )
     return pl.pallas_call(
         product_kernel,
         grid_spec=grid_spec,
-        out_shape=jax.ShapeDtypeStruct((tiles * rows, tokens, 2 * width), jnp.bfloat16),
+        out_shape=jax.ShapeDtypeStruct((tiles * blocks // 2, 2, tokens, 2 * width), jnp.bfloat16),
         compiler_params=pltpu.CompilerParams(vmem_limit_bytes=58 * 2**20),
         cost_estimate=pl.CostEstimate(
-            flops=2 * rows * tokens * right.size,
-            bytes_accessed=2 * (left.size // 2 + right.size + tiles * rows * tokens * 2 * width),
+            flops=2 * blocks * tokens * right.size,
+            bytes_accessed=2 * (left.size + right.size + tiles * blocks * tokens * 2 * width),
             transcendentals=0,
         ),
-    )(place, left, right)
+    )(place, left, right, right)
 
 
 def solution(mesh):
@@ -125,23 +130,24 @@
         columns = lax.all_gather(weight[0], ("sy", "grp"), axis=0, tiled=True)
         columns = columns.reshape(sy, n_grp, weight.shape[1], weight.shape[2])
 
+        half = tokens // n_grp
         stacked = jnp.stack([keys[:, 0], values[:, 0]])
         mine = jnp.concatenate([fetch_behind(stacked, 1, n_srv), fetch_behind(stacked, 2, n_srv)], axis=1)
+        own = lax.dynamic_slice_in_dim(queries[:, 0], core * half, half, 0)
+        other = lax.dynamic_slice_in_dim(queries[:, 0], (1 - core) * half, half, 0)
+        other = lax.ppermute(other, "grp", [(0, 1), (1, 0)])
         window = jnp.concatenate([mine, lax.ppermute(mine, "grp", [(0, 1), (1, 0)]), stacked], axis=1)
         behind = jnp.stack([1 + 2 * core, 2 + 2 * core, 3 - 2 * core, 4 - 2 * core, 0 * core])
-        query_pos = shard * tokens + jnp.arange(tokens, dtype=jnp.int32)
+        query_pos = shard * tokens + core * half + jnp.arange(half, dtype=jnp.int32)
         key_pos = ((shard - behind) * tokens)[:, None] + jnp.arange(tokens, dtype=jnp.int32)[None, :]
-        heads = attend(queries[:, 0], window[0], window[1], query_pos, key_pos.reshape(-1), lengths)
-        heads = lax.all_to_all(heads.reshape(n_grp, tokens // n_grp, heads.shape[1]), "grp", 0, 0)
+        both = jnp.concatenate([own, other], axis=1)
+        heads = attend(both, window[0], window[1], query_pos, key_pos.reshape(-1), lengths)
         along = lax.all_to_all(jnp.broadcast_to(heads, (SX,) + heads.shape), "sx", 0, 0)
-        along = along.reshape((SX // 2, 2) + heads.shape)
 
-        partial = [product(jnp.stack([core ^ t, shift_of(across)]), along, columns) for t in range(2)]
-        late = lax.psum_scatter(partial[1], "kv", scatter_dimension=0, tiled=True)[0]
-        early = lax.all_to_all(partial[0], "kv", 0, 0, tiled=True)
-        early = jnp.sum(early.astype(jnp.float32), axis=0).astype(jnp.bfloat16)
-        early = lax.ppermute(early, ALL, to_owner[0])
-        late = lax.ppermute(late, ALL, to_owner[1])
+        partial = product(jnp.stack([core, shift_of(across)]), along, columns)
+        partial = partial.reshape(n_kv * 2 * half, partial.shape[3])
+        summed = lax.psum_scatter(partial, "kv", scatter_dimension=0, tiled=True).reshape(2, half, -1)
+        early, late = [lax.ppermute(summed[t], ALL, to_owner[t]) for t in range(2)]
         even = across % 2 == 0
         return jnp.concatenate([jnp.where(even, early, late), jnp.where(even, late, early)], axis=0)
 

time: 146 us -> 139 us (0.952); the launches traced: 143 us -> 138 us
  blocking collectives: 50.2 us -> 0 us
  waiting for transfers between devices: 36.1 us -> 80 us
  starting transfers between devices: 21.7 us -> 26.9 us
  Pallas kernels: 11.2 us -> 6.81 us
    all_to_all x2 -> x0, blocking collectives: 50.2 us -> none  [the longest x1 46.3 us: on_device(): early = lax.all_to_all(partial[0], 'kv', 0, 0, tiled=True)]
    reduce_scatter x1, waiting for transfers between devices: 0.02 us -> 45.1 us  [on_device(): lax.psum_scatter(partial, 'kv', scatter_dimension=0, tiled=True)]
    ppermute x2 -> x3, starting transfers between devices: 6.54 us -> 11.7 us  [the longest x2 7.96 us: on_device(): early, late = [lax.ppermute(summed[t], ALL, to_owner[t]) for t in range(2)]]
    pallas_call x2 -> x1, Pallas kernels: 11.2 us -> 6.81 us  [product(): pl.pallas_call(product_kernel, grid_spec=grid_spec, out_shape=jax.ShapeDt...]
    all_gather x1, waiting for transfers between devices: 1.72 us -> 5.72 us  [on_device(): columns = lax.all_gather(weight[0], ('sy', 'grp'), axis=0, tiled=True)]
    ppermute x2, waiting for transfers between devices: 8.13 us -> 4.26 us  [fetch_behind(): return lax.ppermute(stacked, ('grp', 'sx', 'sy'), route)]
    ppermute x2 -> x3, waiting for transfers between devices: 11.9 us -> 10.9 us  [the longest x2 10.9 us: on_device(): early, late = [lax.ppermute(summed[t], ALL, to_owner[t]) for t in range(2)]]
  transfers between devices with their start and end apart: 8 -> 9, of which waited for: 7 -> 7; matrix products, arithmetic and copies ran while one was open for 7% -> 7% of each run, Pallas kernels for 4% -> 0%
where the time goes in v8:
time: 139 us; the launch traced here: 138 us
  waiting for transfers between devices  80 us (58%)
  starting transfers between devices  26.9 us (19%)
  between operations  13.6 us (10%)
  Pallas kernels  6.81 us (5%)
  other arithmetic  5.05 us (4%)
  local copies, waits for them, and re-layouts  3.83 us (3%)
  matrix products  1.88 us (1%)
    reduce_scatter x1, waiting for transfers between devices, on_device(): lax.psum_scatter(partial, 'kv', scatter_dimension=0, tiled=True)  45.1 us
    all_to_all x1, waiting for transfers between devices, on_device(): lax.all_to_all(jnp.broadcast_to(heads, (SX,) + heads.shape), 'sx', 0, 0)  12.7 us
    ppermute x2, waiting for transfers between devices, on_device(): early, late = [lax.ppermute(summed[t], ALL, to_owner[t]) for t in range(2)]  10.9 us
    ppermute x2, starting transfers between devices, fetch_behind(): return lax.ppermute(stacked, ('grp', 'sx', 'sy'), route)  7.98 us
    ppermute x2, starting transfers between devices, on_device(): early, late = [lax.ppermute(summed[t], ALL, to_owner[t]) for t in range(2)]  7.96 us
    pallas_call x1, Pallas kernels, product(): pl.pallas_call(product_kernel, grid_spec=grid_spec, out_shape=jax.ShapeDt...  6.81 us
    all_gather x1, waiting for transfers between devices, on_device(): columns = lax.all_gather(weight[0], ('sy', 'grp'), axis=0, tiled=True)  5.72 us
    all_to_all x1, starting transfers between devices, on_device(): lax.all_to_all(jnp.broadcast_to(heads, (SX,) + heads.shape), 'sx', 0, 0)  4.72 us
  transfers between devices with their start and end apart: 9, of which 7 were waited for; matrix products, arithmetic and copies ran while one was open for 7% of the time, Pallas kernels for 0%

profile of v8, /device:TPU:6, one launch (start us, length us, event | category | flops | bytes accessed | tf_op | source)
XLA Modules:
  0.0 138.0 jit_solution(18431572418939817030)
XLA Ops:
  6.5 0.0 all-gather.3.cloned.1.call-start
  6.5 0.7 all-gather.3.cloned.1.call-update
  7.3 0.9 pad_maximum_fusion.2
  8.1 3.5 %collective-permute-start = (bf16[2,256,128]{2,1,0:T(8,128)(2,1)S(1)}, bf16[2,256,128]{2,1,0:T(8,128)(2,1)S(1)}, u32[]{:S(2)}, u32[]{:S(2)}) collective-permute-start(bf16[2,256,128]{2,1,0:T(8,128)(2,1)S(1)} %pad_maximum_fusion.2), channel_id=1, source_target_pairs={{0,1},{1,2},{2,3},{3,4},{4,5},{5,6},{6,7},{7,8},{8,9},{9,10},{10,1... | collective-permute-start | bytes 393224 | tf_op jit(solution)/shard_map/ppermute | solution.py:48
  11.6 4.5 %collective-permute-start.1 = (bf16[2,256,128]{2,1,0:T(8,128)(2,1)S(1)}, bf16[2,256,128]{2,1,0:T(8,128)(2,1)S(1)}, u32[]{:S(2)}, u32[]{:S(2)}) collective-permute-start(bf16[2,256,128]{2,1,0:T(8,128)(2,1)S(1)} %pad_maximum_fusion.2), channel_id=1, source_target_pairs={{0,2},{1,3},{2,4},{3,5},{4,6},{5,7},{6,8},{7,9},{8,10},{9,11},{10,... | collective-permute-start | bytes 393224 | tf_op jit(solution)/shard_map/ppermute | solution.py:48
  16.2 1.0 constant_dynamic-slice_fusion.1
  17.1 0.1 copy.17
  17.3 3.7 %collective-permute-start.3 = (bf16[128,512]{0,1:T(8,128)(2,1)S(1)}, bf16[128,512]{0,1:T(8,128)(2,1)S(1)}, u32[]{:S(2)}, u32[]{:S(2)}) collective-permute-start(bf16[128,512]{0,1:T(8,128)(2,1)S(1)} %bitcast.43), channel_id=1, source_target_pairs={{0,256},{256,0},{1,257},{257,1},{2,258},{258,2},{3,259},{259,3},{4... | collective-permute-start | bytes 393224 | tf_op jit(solution)/shard_map/ppermute | solution.py:138
  21.0 0.1 stack.35
  21.1 0.8 select_reduce_fusion.1
  21.9 0.1 iota_add_fusion
  22.0 0.1 select_reduce_fusion
  22.1 0.0 collective-permute-done
  22.1 4.3 %collective-permute-done.1 = bf16[2,256,128]{2,1,0:T(8,128)(2,1)S(1)} collective-permute-done((bf16[2,256,128]{2,1,0:T(8,128)(2,1)S(1)}, bf16[2,256,128]{2,1,0:T(8,128)(2,1)S(1)}, u32[]{:S(2)}, u32[]{:S(2)}) %collective-permute-start.1) | collective-permute-done | bytes 131104 | tf_op jit(solution)/shard_map/ppermute | solution.py:48
  26.4 2.5 %collective-permute-start.2 = (bf16[2,512,128]{2,1,0:T(8,128)(2,1)S(1)}, bf16[2,512,128]{2,1,0:T(8,128)(2,1)S(1)}, u32[]{:S(2)}, u32[]{:S(2)}) collective-permute-start(bf16[2,512,128]{2,1,0:T(8,128)(2,1)S(1)} %pad_maximum_fusion), channel_id=1, source_target_pairs={{0,256},{256,0},{1,257},{257,1},{2,258},{258,2},{3,259},{259,3},{4... | collective-permute-start | bytes 786440 | tf_op jit(solution)/shard_map/ppermute | solution.py:139
  28.9 0.2 compare_and_fusion
  29.1 0.1 copy.26
  29.2 0.1 copy.18
  29.4 0.0 collective-permute-done.3
  29.4 0.1 copy.19
  29.5 0.5 collective-permute-done.2
  30.0 0.9 maximum_maximum_fusion
  30.9 0.9 fusion.19
  31.8 0.7 fusion
  32.5 1.0 fusion.11
  33.5 0.1 copy.22
  33.7 1.1 broadcast_in_dim.55
  34.8 4.7 %all-to-all-start = ((bf16[4,128,1024]{2,1,0:T(8,128)(2,1)}), bf16[4,128,1024]{2,1,0:T(8,128)(2,1)S(1)}, u32[]{:S(2)}, u32[]{:S(2)}) async-start(bf16[4,128,1024]{2,1,0:T(8,128)(2,1)} %broadcast_in_dim.55), calls=%async_computation | async-start | bytes 2097152 | tf_op jit(solution)/shard_map/all_to_all | solution.py:145
  39.5 0.0 reduce-scatter.2.cloned.1.call-start
  39.5 0.6 pad_add_fusion.place_ref
  40.1 12.7 %all-to-all-done.left_ref = bf16[4,128,1024]{2,1,0:T(8,128)(2,1)S(1)} async-done(((bf16[4,128,1024]{2,1,0:T(8,128)(2,1)}), bf16[4,128,1024]{2,1,0:T(8,128)(2,1)S(1)}, u32[]{:S(2)}, u32[]{:S(2)}) %all-to-all-start) | async-done | bytes 1048608 | tf_op jit(solution)/shard_map/all_to_all | solution.py:145
  52.9 0.0 copy-start
  52.9 5.7 %all-gather.3.cloned.1.call-done = bf16[1,8192,256]{2,1,0:T(8,128)(2,1)} async-done(((bf16[1,512,256]{2,1,0:T(8,128)(2,1)}), bf16[1,8192,256]{2,1,0:T(8,128)(2,1)}) %all-gather.3.cloned.1.call-update) | async-done | bytes 4194320 | tf_op jit(solution)/shard_map/all_gather | solution.py:130
  58.6 0.0 copy-done
  58.6 6.8 %shard_map.55 = bf16[8,2,128,512]{3,2,1,0:T(8,128)(2,1)} custom-call(s32[2]{0:T(128)} %pad_add_fusion.place_ref, bf16[4,128,1024]{2,1,0:T(8,128)(2,1)} %copy-done, bf16[8,2,512,256]{3,2,1,0:T(8,128)(2,1)} %bitcast.34, bf16[8,2,512,256]{3,2,1,0:T(8,128)(2,1)} %bitcast.35), custom_call_target="tpu_custom_call" | custom-call | flops 2147483648 | bytes 7340032 | tf_op jit(solution)/shard_map/pallas_call | solution.py:83
  65.4 0.0 reduce-scatter.2.cloned.1.call-update
  65.4 45.1 %reduce-scatter.2.cloned.1.call-done = bf16[256,512]{1,0:T(8,128)(2,1)} async-done(((bf16[2048,512]{1,0:T(8,128)(2,1)}), bf16[256,512]{1,0:T(8,128)(2,1)}) %reduce-scatter.2.cloned.1.call-update) | async-done | bytes 262160 | tf_op jit(solution)/shard_map/reduce_scatter | solution.py:149
  110.5 1.0 fusion.18
  111.5 1.9 %collective-permute-start.4 = (bf16[128,512]{1,0:T(8,128)(2,1)S(1)}, bf16[128,512]{1,0:T(8,128)(2,1)S(1)}, u32[]{:S(2)}, u32[]{:S(2)}) collective-permute-start(bf16[128,512]{1,0:T(8,128)(2,1)S(1)} %get-tuple-element.7), channel_id=1, source_target_pairs={{0,32},{1,33},{2,34},{3,35},{4,36},{5,37},{6,38},{7,39},{8,224},{9... | collective-permute-start | bytes 393224 | tf_op jit(solution)/shard_map/ppermute | solution.py:150
  113.5 6.0 %collective-permute-start.5 = (bf16[128,512]{1,0:T(8,128)(2,1)S(1)}, bf16[128,512]{1,0:T(8,128)(2,1)S(1)}, u32[]{:S(2)}, u32[]{:S(2)}) collective-permute-start(bf16[128,512]{1,0:T(8,128)(2,1)S(1)} %get-tuple-element.8), channel_id=1, source_target_pairs={{0,40},{1,41},{2,42},{3,43},{4,44},{5,45},{6,46},{7,47},{8,232},{9... | collective-permute-start | bytes 393224 | tf_op jit(solution)/shard_map/ppermute | solution.py:150
  119.5 8.0 %collective-permute-done.4 = bf16[128,512]{1,0:T(8,128)(2,1)S(1)} collective-permute-done((bf16[128,512]{1,0:T(8,128)(2,1)S(1)}, bf16[128,512]{1,0:T(8,128)(2,1)S(1)}, u32[]{:S(2)}, u32[]{:S(2)}) %collective-permute-start.4) | collective-permute-done | bytes 131104 | tf_op jit(solution)/shard_map/ppermute | solution.py:150
  127.5 2.9 %collective-permute-done.5 = bf16[128,512]{1,0:T(8,128)(2,1)S(1)} collective-permute-done((bf16[128,512]{1,0:T(8,128)(2,1)S(1)}, bf16[128,512]{1,0:T(8,128)(2,1)S(1)}, u32[]{:S(2)}, u32[]{:S(2)}) %collective-permute-start.5) | collective-permute-done | bytes 131104 | tf_op jit(solution)/shard_map/ppermute | solution.py:150
  130.4 0.7 pad_maximum_fusion.1
  (5 shorter events, 0.0 us)
Async XLA Ops:
  6.5 52.0 %all-gather.3.cloned.1.call-start = ((), (), s32[]{:S(2)}) async-start(), calls=%async_computation.3 | async-start | bytes 4456448 | tf_op jit(solution)/shard_map/all_gather | solution.py:130
  8.1 13.9 %collective-permute-start = (bf16[2,256,128]{2,1,0:T(8,128)(2,1)S(1)}, bf16[2,256,128]{2,1,0:T(8,128)(2,1)S(1)}, u32[]{:S(2)}, u32[]{:S(2)}) collective-permute-start(bf16[2,256,128]{2,1,0:T(8,128)(2,1)S(1)} %pad_maximum_fusion.2), channel_id=1, source_target_pairs={{0,1},{1,2},{2,3},{3,4},{4,5},{5,6},{6,7},{7,8},{8,9},{9,10},{10,1... | collective-permute-start | bytes 393224 | tf_op jit(solution)/shard_map/ppermute | solution.py:48
  11.6 14.7 %collective-permute-start.1 = (bf16[2,256,128]{2,1,0:T(8,128)(2,1)S(1)}, bf16[2,256,128]{2,1,0:T(8,128)(2,1)S(1)}, u32[]{:S(2)}, u32[]{:S(2)}) collective-permute-start(bf16[2,256,128]{2,1,0:T(8,128)(2,1)S(1)} %pad_maximum_fusion.2), channel_id=1, source_target_pairs={{0,2},{1,3},{2,4},{3,5},{4,6},{5,7},{6,8},{7,9},{8,10},{9,11},{10,... | collective-permute-start | bytes 393224 | tf_op jit(solution)/shard_map/ppermute | solution.py:48
  17.3 12.1 %collective-permute-start.3 = (bf16[128,512]{0,1:T(8,128)(2,1)S(1)}, bf16[128,512]{0,1:T(8,128)(2,1)S(1)}, u32[]{:S(2)}, u32[]{:S(2)}) collective-permute-start(bf16[128,512]{0,1:T(8,128)(2,1)S(1)} %bitcast.43), channel_id=1, source_target_pairs={{0,256},{256,0},{1,257},{257,1},{2,258},{258,2},{3,259},{259,3},{4... | collective-permute-start | bytes 393224 | tf_op jit(solution)/shard_map/ppermute | solution.py:138
  26.4 3.6 %collective-permute-start.2 = (bf16[2,512,128]{2,1,0:T(8,128)(2,1)S(1)}, bf16[2,512,128]{2,1,0:T(8,128)(2,1)S(1)}, u32[]{:S(2)}, u32[]{:S(2)}) collective-permute-start(bf16[2,512,128]{2,1,0:T(8,128)(2,1)S(1)} %pad_maximum_fusion), channel_id=1, source_target_pairs={{0,256},{256,0},{1,257},{257,1},{2,258},{258,2},{3,259},{259,3},{4... | collective-permute-start | bytes 786440 | tf_op jit(solution)/shard_map/ppermute | solution.py:139
  34.8 18.1 %all-to-all-start = ((bf16[4,128,1024]{2,1,0:T(8,128)(2,1)}), bf16[4,128,1024]{2,1,0:T(8,128)(2,1)S(1)}, u32[]{:S(2)}, u32[]{:S(2)}) async-start(bf16[4,128,1024]{2,1,0:T(8,128)(2,1)} %broadcast_in_dim.55), calls=%async_computation | async-start | bytes 2097152 | tf_op jit(solution)/shard_map/all_to_all | solution.py:145
  39.5 71.0 %reduce-scatter.2.cloned.1.call-start = ((), (), s32[]{:S(2)}) async-start(), calls=%async_computation.2 | async-start | bytes 2359296 | tf_op jit(solution)/shard_map/reduce_scatter | solution.py:149
  52.9 5.7 %copy-start = (bf16[4,128,1024]{2,1,0:T(8,128)(2,1)}, bf16[4,128,1024]{2,1,0:T(8,128)(2,1)S(1)}, u32[]{:S(2)}) copy-start(bf16[4,128,1024]{2,1,0:T(8,128)(2,1)S(1)} %all-to-all-done.left_ref) | copy-start | bytes 3145732
  111.5 16.0 %collective-permute-start.4 = (bf16[128,512]{1,0:T(8,128)(2,1)S(1)}, bf16[128,512]{1,0:T(8,128)(2,1)S(1)}, u32[]{:S(2)}, u32[]{:S(2)}) collective-permute-start(bf16[128,512]{1,0:T(8,128)(2,1)S(1)} %get-tuple-element.7), channel_id=1, source_target_pairs={{0,32},{1,33},{2,34},{3,35},{4,36},{5,37},{6,38},{7,39},{8,224},{9... | collective-permute-start | bytes 393224 | tf_op jit(solution)/shard_map/ppermute | solution.py:150
  113.5 16.9 %collective-permute-start.5 = (bf16[128,512]{1,0:T(8,128)(2,1)S(1)}, bf16[128,512]{1,0:T(8,128)(2,1)S(1)}, u32[]{:S(2)}, u32[]{:S(2)}) collective-permute-start(bf16[128,512]{1,0:T(8,128)(2,1)S(1)} %get-tuple-element.8), channel_id=1, source_target_pairs={{0,40},{1,41},{2,42},{3,43},{4,44},{5,45},{6,46},{7,47},{8,232},{9... | collective-permute-start | bytes 393224 | tf_op jit(solution)/shard_map/ppermute | solution.py:150
Sparse Core Ops, SparseCore 0:
  9.5 49.0 all-gather.2
  65.5 44.9 reduce-scatter.1

commit v9 on v8

--- a/solution.py
+++ b/solution.py
@@ -48,16 +48,15 @@
     return lax.ppermute(stacked, ("grp", "sx", "sy"), route)
 
 
-def product_kernel(place_ref, left_ref, own_ref, other_ref, out_ref):
+def product_kernel(place_ref, left_ref, right_ref, out_ref):
     blocks, tokens, depth = left_ref.shape
     left = left_ref[...].reshape(blocks * tokens, depth)
-    half = depth // 2
     core = place_ref[0]
-    for piece in range(own_ref.shape[0]):
-        total = jnp.dot(left[:, :half], own_ref[piece, 0], preferred_element_type=jnp.float32)
-        total += jnp.dot(left[:, half:], other_ref[piece, 0], preferred_element_type=jnp.float32)
-        total = total.astype(out_ref.dtype)
-        width = total.shape[1]
+    pieces, _, _, width = right_ref.shape
+    for piece in range(pieces):
+        total = jnp.dot(
+            left, right_ref[piece].reshape(depth, width), preferred_element_type=jnp.float32
+        ).astype(out_ref.dtype)
         for x in range(blocks):
             out_ref[x // 2, (x % 2) ^ core, :, piece * width : (piece + 1) * width] = total[
                 x * tokens : (x + 1) * tokens
@@ -66,15 +65,14 @@
 
 def product(place, left, right):
     blocks, tokens, depth = left.shape
-    pieces, _, half, width = right.shape
+    pieces, cores, half, width = right.shape
     tiles = pieces // 2
     grid_spec = pltpu.PrefetchScalarGridSpec(
         num_scalar_prefetch=1,
         grid=(tiles,),
         in_specs=[
-            pl.BlockSpec((blocks, tokens, depth), lambda j, place: (0, 0, 0)),
-            pl.BlockSpec((2, 1, half, width), lambda j, place: (j, place[0], 0, 0)),
-            pl.BlockSpec((2, 1, half, width), lambda j, place: (j, 1 - place[0], 0, 0)),
+            pl.BlockSpec(memory_space=pltpu.VMEM),
+            pl.BlockSpec((2, cores, half, width), lambda j, place: (j, 0, 0, 0)),
         ],
         out_specs=pl.BlockSpec(
             (blocks // 2, 2, tokens, 2 * width), lambda j, place: ((j + place[1]) % tiles, 0, 0, 0)
@@ -84,13 +82,13 @@
         product_kernel,
         grid_spec=grid_spec,
         out_shape=jax.ShapeDtypeStruct((tiles * blocks // 2, 2, tokens, 2 * width), jnp.bfloat16),
-        compiler_params=pltpu.CompilerParams(vmem_limit_bytes=58 * 2**20),
+        compiler_params=pltpu.CompilerParams(vmem_limit_bytes=40 * 2**20),
         cost_estimate=pl.CostEstimate(
             flops=2 * blocks * tokens * right.size,
             bytes_accessed=2 * (left.size + right.size + tiles * blocks * tokens * 2 * width),
             transcendentals=0,
         ),
-    )(place, left, right, right)
+    )(place, left, right)
 
 
 def solution(mesh):
@@ -140,13 +138,14 @@
         behind = jnp.stack([1 + 2 * core, 2 + 2 * core, 3 - 2 * core, 4 - 2 * core, 0 * core])
         query_pos = shard * tokens + core * half + jnp.arange(half, dtype=jnp.int32)
         key_pos = ((shard - behind) * tokens)[:, None] + jnp.arange(tokens, dtype=jnp.int32)[None, :]
-        both = jnp.concatenate([own, other], axis=1)
+        first = core == 0
+        both = jnp.concatenate([jnp.where(first, own, other), jnp.where(first, other, own)], axis=1)
         heads = attend(both, window[0], window[1], query_pos, key_pos.reshape(-1), lengths)
         along = lax.all_to_all(jnp.broadcast_to(heads, (SX,) + heads.shape), "sx", 0, 0)
 
         partial = product(jnp.stack([core, shift_of(across)]), along, columns)
-        partial = partial.reshape(n_kv * 2 * half, partial.shape[3])
-        summed = lax.psum_scatter(partial, "kv", scatter_dimension=0, tiled=True).reshape(2, half, -1)
+        partial = partial.reshape(n_kv, 2 * half, partial.shape[3])
+        summed = lax.psum_scatter(partial, "kv", scatter_dimension=0).reshape(2, half, -1)
         early, late = [lax.ppermute(summed[t], ALL, to_owner[t]) for t in range(2)]
         even = across % 2 == 0
         return jnp.concatenate([jnp.where(even, early, late), jnp.where(even, late, early)], axis=0)

time: 139 us -> 138 us (level)
  Pallas kernels: 6.81 us -> 4.37 us
  local copies, waits for them, and re-layouts: 3.83 us -> 5.74 us
    pallas_call x1, Pallas kernels: 6.81 us -> 4.37 us  [product(): pl.pallas_call(product_kernel, grid_spec=grid_spec, out_shape=jax.ShapeDt...]
    unnamed x3 -> x2, local copies, waits for them, and re-layouts: 0.12 us -> 2.19 us
  transfers between devices with their start and end apart: 9 -> 9, of which waited for: 7 -> 7; matrix products, arithmetic and copies ran while one was open for 7% -> 6% of each run, Pallas kernels for 0% -> 0%
where the time goes in v9:
time: 138 us
  waiting for transfers between devices  80.7 us (58%)
  starting transfers between devices  26.9 us (19%)
  between operations  13.6 us (10%)
  local copies, waits for them, and re-layouts  5.74 us (4%)
  other arithmetic  4.57 us (3%)
  Pallas kernels  4.37 us (3%)
  matrix products  1.87 us (1%)
    reduce_scatter x1, waiting for transfers between devices, on_device(): lax.psum_scatter(partial, 'kv', scatter_dimension=0).reshape(2, half, -1)  45 us
    all_to_all x1, waiting for transfers between devices, on_device(): lax.all_to_all(jnp.broadcast_to(heads, (SX,) + heads.shape), 'sx', 0, 0)  13.3 us
    ppermute x2, waiting for transfers between devices, on_device(): early, late = [lax.ppermute(summed[t], ALL, to_owner[t]) for t in range(2)]  10.9 us
    ppermute x2, starting transfers between devices, fetch_behind(): return lax.ppermute(stacked, ('grp', 'sx', 'sy'), route)  7.98 us
    ppermute x2, starting transfers between devices, on_device(): early, late = [lax.ppermute(summed[t], ALL, to_owner[t]) for t in range(2)]  7.96 us
    all_gather x1, waiting for transfers between devices, on_device(): columns = lax.all_gather(weight[0], ('sy', 'grp'), axis=0, tiled=True)  5.9 us
    all_to_all x1, starting transfers between devices, on_device(): lax.all_to_all(jnp.broadcast_to(heads, (SX,) + heads.shape), 'sx', 0, 0)  4.71 us
    pallas_call x1, Pallas kernels, product(): pl.pallas_call(product_kernel, grid_spec=grid_spec, out_shape=jax.ShapeDt...  4.37 us
  transfers between devices with their start and end apart: 9, of which 7 were waited for; matrix products, arithmetic and copies ran while one was open for 6% of the time, Pallas kernels for 0%

profile of v9, /device:TPU:6, one launch (start us, length us, event | category | flops | bytes accessed | tf_op | source)
XLA Modules:
  0.0 137.8 jit_solution(6244974325145068351)
XLA Ops:
  6.5 0.0 all-gather.3.cloned.1.call-start
  6.5 0.7 all-gather.3.cloned.1.call-update
  7.3 0.9 pad_maximum_fusion.3
  8.1 3.5 %collective-permute-start = (bf16[2,256,128]{2,1,0:T(8,128)(2,1)S(1)}, bf16[2,256,128]{2,1,0:T(8,128)(2,1)S(1)}, u32[]{:S(2)}, u32[]{:S(2)}) collective-permute-start(bf16[2,256,128]{2,1,0:T(8,128)(2,1)S(1)} %pad_maximum_fusion.3), channel_id=1, source_target_pairs={{0,1},{1,2},{2,3},{3,4},{4,5},{5,6},{6,7},{7,8},{8,9},{9,10},{10,1... | collective-permute-start | bytes 393224 | tf_op jit(solution)/shard_map/ppermute | solution.py:48
  11.6 4.5 %collective-permute-start.1 = (bf16[2,256,128]{2,1,0:T(8,128)(2,1)S(1)}, bf16[2,256,128]{2,1,0:T(8,128)(2,1)S(1)}, u32[]{:S(2)}, u32[]{:S(2)}) collective-permute-start(bf16[2,256,128]{2,1,0:T(8,128)(2,1)S(1)} %pad_maximum_fusion.3), channel_id=1, source_target_pairs={{0,2},{1,3},{2,4},{3,5},{4,6},{5,7},{6,8},{7,9},{8,10},{9,11},{10,... | collective-permute-start | bytes 393224 | tf_op jit(solution)/shard_map/ppermute | solution.py:48
  16.2 1.0 constant_dynamic-slice_fusion.1
  17.1 0.1 copy.16
  17.3 3.7 %collective-permute-start.3 = (bf16[128,512]{0,1:T(8,128)(2,1)S(1)}, bf16[128,512]{0,1:T(8,128)(2,1)S(1)}, u32[]{:S(2)}, u32[]{:S(2)}) collective-permute-start(bf16[128,512]{0,1:T(8,128)(2,1)S(1)} %bitcast.48), channel_id=1, source_target_pairs={{0,256},{256,0},{1,257},{257,1},{2,258},{258,2},{3,259},{259,3},{4... | collective-permute-start | bytes 393224 | tf_op jit(solution)/shard_map/ppermute | solution.py:136
  21.0 0.1 stack.35
  21.1 0.1 iota_add_fusion
  21.2 0.8 select_reduce_fusion.1
  22.0 0.1 select_reduce_fusion
  22.1 0.2 compare_and_fusion
  22.3 0.1 copy.15
  22.5 0.0 collective-permute-done
  22.5 3.9 %collective-permute-done.1 = bf16[2,256,128]{2,1,0:T(8,128)(2,1)S(1)} collective-permute-done((bf16[2,256,128]{2,1,0:T(8,128)(2,1)S(1)}, bf16[2,256,128]{2,1,0:T(8,128)(2,1)S(1)}, u32[]{:S(2)}, u32[]{:S(2)}) %collective-permute-start.1) | collective-permute-done | bytes 131104 | tf_op jit(solution)/shard_map/ppermute | solution.py:48
  26.4 2.5 %collective-permute-start.2 = (bf16[2,512,128]{2,1,0:T(8,128)(2,1)S(1)}, bf16[2,512,128]{2,1,0:T(8,128)(2,1)S(1)}, u32[]{:S(2)}, u32[]{:S(2)}) collective-permute-start(bf16[2,512,128]{2,1,0:T(8,128)(2,1)S(1)} %pad_maximum_fusion), channel_id=1, source_target_pairs={{0,256},{256,0},{1,257},{257,1},{2,258},{258,2},{3,259},{259,3},{4... | collective-permute-start | bytes 786440 | tf_op jit(solution)/shard_map/ppermute | solution.py:137
  28.9 0.0 collective-permute-done.3
  28.9 1.1 collective-permute-done.2
  30.0 0.9 maximum_maximum_fusion
  30.9 0.8 fusion.14
  31.8 0.7 fusion
  32.5 1.0 fusion.11
  33.5 0.1 copy.20
  33.7 1.1 broadcast_in_dim.55
  34.8 4.7 %all-to-all-start = ((bf16[4,128,1024]{2,1,0:T(8,128)(2,1)}), bf16[4,128,1024]{2,1,0:T(8,128)(2,1)S(1)}, u32[]{:S(2)}, u32[]{:S(2)}) async-start(bf16[4,128,1024]{2,1,0:T(8,128)(2,1)} %broadcast_in_dim.55), calls=%async_computation | async-start | bytes 2097152 | tf_op jit(solution)/shard_map/all_to_all | solution.py:144
  39.5 0.0 reduce-scatter.2.cloned.1.call-start
  39.5 0.1 pad_add_fusion.place_ref
  39.6 13.3 %all-to-all-done.left_ref = bf16[4,128,1024]{2,1,0:T(8,128)(2,1)S(1)} async-done(((bf16[4,128,1024]{2,1,0:T(8,128)(2,1)}), bf16[4,128,1024]{2,1,0:T(8,128)(2,1)S(1)}, u32[]{:S(2)}, u32[]{:S(2)}) %all-to-all-start) | async-done | bytes 1048608 | tf_op jit(solution)/shard_map/all_to_all | solution.py:144
  52.8 5.9 %all-gather.3.cloned.1.call-done = bf16[1,8192,256]{2,1,0:T(8,128)(2,1)} async-done(((bf16[1,512,256]{2,1,0:T(8,128)(2,1)}), bf16[1,8192,256]{2,1,0:T(8,128)(2,1)}) %all-gather.3.cloned.1.call-update) | async-done | bytes 4194320 | tf_op jit(solution)/shard_map/all_gather | solution.py:128
  58.7 0.0 copy-start
  58.7 2.2 %copy-done = bf16[1,8192,256]{2,1,0:T(8,128)(2,1)S(1)} copy-done((bf16[1,8192,256]{2,1,0:T(8,128)(2,1)S(1)}, bf16[1,8192,256]{2,1,0:T(8,128)(2,1)}, u32[]{:S(2)}) %copy-start) | copy-done | bytes 4194328
  60.9 4.4 %shard_map.55 = bf16[8,2,128,512]{3,2,1,0:T(8,128)(2,1)} custom-call(s32[2]{0:T(128)S(1)} %pad_add_fusion.place_ref, bf16[4,128,1024]{2,1,0:T(8,128)(2,1)S(1)} %all-to-all-done.left_ref, bf16[8,2,512,256]{3,2,1,0:T(8,128)(2,1)S(1)} %bitcast.41), custom_call_target="tpu_custom_call" | custom-call | flops 2147483648 | bytes 7340032 | tf_op jit(solution)/shard_map/pallas_call | solution.py:81
  65.3 0.0 reduce-scatter.2.cloned.1.call-update
  65.3 45.0 %reduce-scatter.2.cloned.1.call-done = bf16[1,256,512]{2,1,0:T(8,128)(2,1)} async-done(((bf16[8,256,512]{2,1,0:T(8,128)(2,1)}), bf16[1,256,512]{2,1,0:T(8,128)(2,1)}) %reduce-scatter.2.cloned.1.call-update) | async-done | bytes 262160 | tf_op jit(solution)/shard_map/reduce_scatter | solution.py:148
  110.4 1.0 slice_bitcast_fusion.5
  111.4 1.9 %collective-permute-start.4 = (bf16[128,512]{1,0:T(8,128)(2,1)S(1)}, bf16[128,512]{1,0:T(8,128)(2,1)S(1)}, u32[]{:S(2)}, u32[]{:S(2)}) collective-permute-start(bf16[128,512]{1,0:T(8,128)(2,1)S(1)} %get-tuple-element.7), channel_id=1, source_target_pairs={{0,32},{1,33},{2,34},{3,35},{4,36},{5,37},{6,38},{7,39},{8,224},{9... | collective-permute-start | bytes 393224 | tf_op jit(solution)/shard_map/ppermute | solution.py:149
  113.3 6.0 %collective-permute-start.5 = (bf16[128,512]{1,0:T(8,128)(2,1)S(1)}, bf16[128,512]{1,0:T(8,128)(2,1)S(1)}, u32[]{:S(2)}, u32[]{:S(2)}) collective-permute-start(bf16[128,512]{1,0:T(8,128)(2,1)S(1)} %get-tuple-element.8), channel_id=1, source_target_pairs={{0,40},{1,41},{2,42},{3,43},{4,44},{5,45},{6,46},{7,47},{8,232},{9... | collective-permute-start | bytes 393224 | tf_op jit(solution)/shard_map/ppermute | solution.py:149
  119.3 8.0 %collective-permute-done.4 = bf16[128,512]{1,0:T(8,128)(2,1)S(1)} collective-permute-done((bf16[128,512]{1,0:T(8,128)(2,1)S(1)}, bf16[128,512]{1,0:T(8,128)(2,1)S(1)}, u32[]{:S(2)}, u32[]{:S(2)}) %collective-permute-start.4) | collective-permute-done | bytes 131104 | tf_op jit(solution)/shard_map/ppermute | solution.py:149
  127.3 2.9 %collective-permute-done.5 = bf16[128,512]{1,0:T(8,128)(2,1)S(1)} collective-permute-done((bf16[128,512]{1,0:T(8,128)(2,1)S(1)}, bf16[128,512]{1,0:T(8,128)(2,1)S(1)}, u32[]{:S(2)}, u32[]{:S(2)}) %collective-permute-start.5) | collective-permute-done | bytes 131104 | tf_op jit(solution)/shard_map/ppermute | solution.py:149
  130.2 0.7 pad_maximum_fusion.2
  (7 shorter events, 0.1 us)
Async XLA Ops:
  6.5 52.2 %all-gather.3.cloned.1.call-start = ((), (), s32[]{:S(2)}) async-start(), calls=%async_computation.3 | async-start | bytes 4456448 | tf_op jit(solution)/shard_map/all_gather | solution.py:128
  8.1 14.3 %collective-permute-start = (bf16[2,256,128]{2,1,0:T(8,128)(2,1)S(1)}, bf16[2,256,128]{2,1,0:T(8,128)(2,1)S(1)}, u32[]{:S(2)}, u32[]{:S(2)}) collective-permute-start(bf16[2,256,128]{2,1,0:T(8,128)(2,1)S(1)} %pad_maximum_fusion.3), channel_id=1, source_target_pairs={{0,1},{1,2},{2,3},{3,4},{4,5},{5,6},{6,7},{7,8},{8,9},{9,10},{10,1... | collective-permute-start | bytes 393224 | tf_op jit(solution)/shard_map/ppermute | solution.py:48
  11.6 14.7 %collective-permute-start.1 = (bf16[2,256,128]{2,1,0:T(8,128)(2,1)S(1)}, bf16[2,256,128]{2,1,0:T(8,128)(2,1)S(1)}, u32[]{:S(2)}, u32[]{:S(2)}) collective-permute-start(bf16[2,256,128]{2,1,0:T(8,128)(2,1)S(1)} %pad_maximum_fusion.3), channel_id=1, source_target_pairs={{0,2},{1,3},{2,4},{3,5},{4,6},{5,7},{6,8},{7,9},{8,10},{9,11},{10,... | collective-permute-start | bytes 393224 | tf_op jit(solution)/shard_map/ppermute | solution.py:48
  17.3 11.6 %collective-permute-start.3 = (bf16[128,512]{0,1:T(8,128)(2,1)S(1)}, bf16[128,512]{0,1:T(8,128)(2,1)S(1)}, u32[]{:S(2)}, u32[]{:S(2)}) collective-permute-start(bf16[128,512]{0,1:T(8,128)(2,1)S(1)} %bitcast.48), channel_id=1, source_target_pairs={{0,256},{256,0},{1,257},{257,1},{2,258},{258,2},{3,259},{259,3},{4... | collective-permute-start | bytes 393224 | tf_op jit(solution)/shard_map/ppermute | solution.py:136
  26.4 3.6 %collective-permute-start.2 = (bf16[2,512,128]{2,1,0:T(8,128)(2,1)S(1)}, bf16[2,512,128]{2,1,0:T(8,128)(2,1)S(1)}, u32[]{:S(2)}, u32[]{:S(2)}) collective-permute-start(bf16[2,512,128]{2,1,0:T(8,128)(2,1)S(1)} %pad_maximum_fusion), channel_id=1, source_target_pairs={{0,256},{256,0},{1,257},{257,1},{2,258},{258,2},{3,259},{259,3},{4... | collective-permute-start | bytes 786440 | tf_op jit(solution)/shard_map/ppermute | solution.py:137
  34.8 18.1 %all-to-all-start = ((bf16[4,128,1024]{2,1,0:T(8,128)(2,1)}), bf16[4,128,1024]{2,1,0:T(8,128)(2,1)S(1)}, u32[]{:S(2)}, u32[]{:S(2)}) async-start(bf16[4,128,1024]{2,1,0:T(8,128)(2,1)} %broadcast_in_dim.55), calls=%async_computation | async-start | bytes 2097152 | tf_op jit(solution)/shard_map/all_to_all | solution.py:144
  39.5 70.9 %reduce-scatter.2.cloned.1.call-start = ((), (), s32[]{:S(2)}) async-start(), calls=%async_computation.2 | async-start | bytes 2359296 | tf_op jit(solution)/shard_map/reduce_scatter | solution.py:148
  58.7 2.2 %copy-start = (bf16[1,8192,256]{2,1,0:T(8,128)(2,1)S(1)}, bf16[1,8192,256]{2,1,0:T(8,128)(2,1)}, u32[]{:S(2)}) copy-start(bf16[1,8192,256]{2,1,0:T(8,128)(2,1)} %all-gather.3.cloned.1.call-done) | copy-start | bytes 12582916
  111.4 16.0 %collective-permute-start.4 = (bf16[128,512]{1,0:T(8,128)(2,1)S(1)}, bf16[128,512]{1,0:T(8,128)(2,1)S(1)}, u32[]{:S(2)}, u32[]{:S(2)}) collective-permute-start(bf16[128,512]{1,0:T(8,128)(2,1)S(1)} %get-tuple-element.7), channel_id=1, source_target_pairs={{0,32},{1,33},{2,34},{3,35},{4,36},{5,37},{6,38},{7,39},{8,224},{9... | collective-permute-start | bytes 393224 | tf_op jit(solution)/shard_map/ppermute | solution.py:149
  113.3 16.9 %collective-permute-start.5 = (bf16[128,512]{1,0:T(8,128)(2,1)S(1)}, bf16[128,512]{1,0:T(8,128)(2,1)S(1)}, u32[]{:S(2)}, u32[]{:S(2)}) collective-permute-start(bf16[128,512]{1,0:T(8,128)(2,1)S(1)} %get-tuple-element.8), channel_id=1, source_target_pairs={{0,40},{1,41},{2,42},{3,43},{4,44},{5,45},{6,46},{7,47},{8,232},{9... | collective-permute-start | bytes 393224 | tf_op jit(solution)/shard_map/ppermute | solution.py:149
Sparse Core Ops, SparseCore 0:
  9.5 49.2 all-gather.2
  65.5 44.8 reduce-scatter.1

commit v10 on v9

--- a/solution.py
+++ b/solution.py
@@ -51,14 +51,15 @@
 def product_kernel(place_ref, left_ref, right_ref, out_ref):
     blocks, tokens, depth = left_ref.shape
     left = left_ref[...].reshape(blocks * tokens, depth)
-    core = place_ref[0]
+    core, across = place_ref[0], place_ref[2]
     pieces, _, _, width = right_ref.shape
     for piece in range(pieces):
         total = jnp.dot(
             left, right_ref[piece].reshape(depth, width), preferred_element_type=jnp.float32
         ).astype(out_ref.dtype)
         for x in range(blocks):
-            out_ref[x // 2, (x % 2) ^ core, :, piece * width : (piece + 1) * width] = total[
+            ahead = (x + blocks - across) % blocks
+            out_ref[ahead // 2, (ahead % 2) ^ core, :, piece * width : (piece + 1) * width] = total[
                 x * tokens : (x + 1) * tokens
             ]
 
@@ -113,7 +114,7 @@
             for z in range(n_kv):
                 for x in range(SX):
                     j = (z // 2 - shift_of(x)) % tiles
-                    to_x = 2 * (z % 2) + (c ^ t)
+                    to_x = (x + 2 * (z % 2) + (c ^ t)) % SX
                     owner = x * tiles + j
                     for y in range(sy):
                         to_owner[t].append(
@@ -143,11 +144,11 @@
         heads = attend(both, window[0], window[1], query_pos, key_pos.reshape(-1), lengths)
         along = lax.all_to_all(jnp.broadcast_to(heads, (SX,) + heads.shape), "sx", 0, 0)
 
-        partial = product(jnp.stack([core, shift_of(across)]), along, columns)
+        partial = product(jnp.stack([core, shift_of(across), across]), along, columns)
         partial = partial.reshape(n_kv, 2 * half, partial.shape[3])
         summed = lax.psum_scatter(partial, "kv", scatter_dimension=0).reshape(2, half, -1)
         early, late = [lax.ppermute(summed[t], ALL, to_owner[t]) for t in range(2)]
-        even = across % 2 == 0
+        even = (across + lax.axis_index("kv") // tiles) % 2 == 0
         return jnp.concatenate([jnp.where(even, early, late), jnp.where(even, late, early)], axis=0)
 
     q = P(("sx", "sy"), "kv", "grp")

time: 138 us -> 138 us (level)
  no operation moved by 1% of the time
where the time goes in v10:
time: 138 us
  waiting for transfers between devices  79.8 us (58%)
  starting transfers between devices  27.8 us (20%)
  between operations  13.6 us (10%)
  local copies, waits for them, and re-layouts  5.74 us (4%)
  other arithmetic  4.57 us (3%)
  Pallas kernels  4.37 us (3%)
  matrix products  1.87 us (1%)
    reduce_scatter x1, waiting for transfers between devices, on_device(): lax.psum_scatter(partial, 'kv', scatter_dimension=0).reshape(2, half, -1)  44.9 us
    all_to_all x1, waiting for transfers between devices, on_device(): lax.all_to_all(jnp.broadcast_to(heads, (SX,) + heads.shape), 'sx', 0, 0)  13.3 us
    ppermute x2, waiting for transfers between devices, on_device(): early, late = [lax.ppermute(summed[t], ALL, to_owner[t]) for t in range(2)]  9.99 us
    ppermute x2, starting transfers between devices, on_device(): early, late = [lax.ppermute(summed[t], ALL, to_owner[t]) for t in range(2)]  8.88 us
    ppermute x2, starting transfers between devices, fetch_behind(): return lax.ppermute(stacked, ('grp', 'sx', 'sy'), route)  7.98 us
    all_gather x1, waiting for transfers between devices, on_device(): columns = lax.all_gather(weight[0], ('sy', 'grp'), axis=0, tiled=True)  5.9 us
    all_to_all x1, starting transfers between devices, on_device(): lax.all_to_all(jnp.broadcast_to(heads, (SX,) + heads.shape), 'sx', 0, 0)  4.71 us
    pallas_call x1, Pallas kernels, product(): pl.pallas_call(product_kernel, grid_spec=grid_spec, out_shape=jax.ShapeDt...  4.37 us
  transfers between devices with their start and end apart: 9, of which 7 were waited for; matrix products, arithmetic and copies ran while one was open for 6% of the time, Pallas kernels for 0%

profile of v10, /device:TPU:6, one launch (start us, length us, event | category | flops | bytes accessed | tf_op | source)
XLA Modules:
  0.0 137.8 jit_solution(12581471467018849852)
XLA Ops:
  6.5 0.0 all-gather.3.cloned.1.call-start
  6.5 0.7 all-gather.3.cloned.1.call-update
  7.3 0.9 pad_maximum_fusion.3
  8.1 3.5 %collective-permute-start = (bf16[2,256,128]{2,1,0:T(8,128)(2,1)S(1)}, bf16[2,256,128]{2,1,0:T(8,128)(2,1)S(1)}, u32[]{:S(2)}, u32[]{:S(2)}) collective-permute-start(bf16[2,256,128]{2,1,0:T(8,128)(2,1)S(1)} %pad_maximum_fusion.3), channel_id=1, source_target_pairs={{0,1},{1,2},{2,3},{3,4},{4,5},{5,6},{6,7},{7,8},{8,9},{9,10},{10,1... | collective-permute-start | bytes 393224 | tf_op jit(solution)/shard_map/ppermute | solution.py:48
  11.6 4.5 %collective-permute-start.1 = (bf16[2,256,128]{2,1,0:T(8,128)(2,1)S(1)}, bf16[2,256,128]{2,1,0:T(8,128)(2,1)S(1)}, u32[]{:S(2)}, u32[]{:S(2)}) collective-permute-start(bf16[2,256,128]{2,1,0:T(8,128)(2,1)S(1)} %pad_maximum_fusion.3), channel_id=1, source_target_pairs={{0,2},{1,3},{2,4},{3,5},{4,6},{5,7},{6,8},{7,9},{8,10},{9,11},{10,... | collective-permute-start | bytes 393224 | tf_op jit(solution)/shard_map/ppermute | solution.py:48
  16.2 1.0 constant_dynamic-slice_fusion.1
  17.1 0.1 copy.16
  17.3 3.7 %collective-permute-start.3 = (bf16[128,512]{0,1:T(8,128)(2,1)S(1)}, bf16[128,512]{0,1:T(8,128)(2,1)S(1)}, u32[]{:S(2)}, u32[]{:S(2)}) collective-permute-start(bf16[128,512]{0,1:T(8,128)(2,1)S(1)} %bitcast.49), channel_id=1, source_target_pairs={{0,256},{256,0},{1,257},{257,1},{2,258},{258,2},{3,259},{259,3},{4... | collective-permute-start | bytes 393224 | tf_op jit(solution)/shard_map/ppermute | solution.py:137
  21.0 0.1 stack.39
  21.1 0.1 iota_add_fusion
  21.2 0.8 select_reduce_fusion.1
  22.0 0.1 select_reduce_fusion
  22.1 0.2 compare_and_fusion
  22.3 0.1 copy.15
  22.5 0.0 collective-permute-done
  22.5 3.9 %collective-permute-done.1 = bf16[2,256,128]{2,1,0:T(8,128)(2,1)S(1)} collective-permute-done((bf16[2,256,128]{2,1,0:T(8,128)(2,1)S(1)}, bf16[2,256,128]{2,1,0:T(8,128)(2,1)S(1)}, u32[]{:S(2)}, u32[]{:S(2)}) %collective-permute-start.1) | collective-permute-done | bytes 131104 | tf_op jit(solution)/shard_map/ppermute | solution.py:48
  26.4 2.5 %collective-permute-start.2 = (bf16[2,512,128]{2,1,0:T(8,128)(2,1)S(1)}, bf16[2,512,128]{2,1,0:T(8,128)(2,1)S(1)}, u32[]{:S(2)}, u32[]{:S(2)}) collective-permute-start(bf16[2,512,128]{2,1,0:T(8,128)(2,1)S(1)} %pad_maximum_fusion), channel_id=1, source_target_pairs={{0,256},{256,0},{1,257},{257,1},{2,258},{258,2},{3,259},{259,3},{4... | collective-permute-start | bytes 786440 | tf_op jit(solution)/shard_map/ppermute | solution.py:138
  28.9 0.0 collective-permute-done.3
  28.9 1.1 collective-permute-done.2
  30.0 0.9 maximum_maximum_fusion
  30.9 0.8 fusion.14
  31.8 0.7 fusion
  32.5 1.0 fusion.11
  33.5 0.1 copy.20
  33.7 1.1 broadcast_in_dim.55
  34.8 4.7 %all-to-all-start = ((bf16[4,128,1024]{2,1,0:T(8,128)(2,1)}), bf16[4,128,1024]{2,1,0:T(8,128)(2,1)S(1)}, u32[]{:S(2)}, u32[]{:S(2)}) async-start(bf16[4,128,1024]{2,1,0:T(8,128)(2,1)} %broadcast_in_dim.55), calls=%async_computation | async-start | bytes 2097152 | tf_op jit(solution)/shard_map/all_to_all | solution.py:145
  39.5 0.0 reduce-scatter.2.cloned.1.call-start
  39.5 0.1 pad_add_fusion.place_ref
  39.6 13.3 %all-to-all-done.left_ref = bf16[4,128,1024]{2,1,0:T(8,128)(2,1)S(1)} async-done(((bf16[4,128,1024]{2,1,0:T(8,128)(2,1)}), bf16[4,128,1024]{2,1,0:T(8,128)(2,1)S(1)}, u32[]{:S(2)}, u32[]{:S(2)}) %all-to-all-start) | async-done | bytes 1048608 | tf_op jit(solution)/shard_map/all_to_all | solution.py:145
  52.8 5.9 %all-gather.3.cloned.1.call-done = bf16[1,8192,256]{2,1,0:T(8,128)(2,1)} async-done(((bf16[1,512,256]{2,1,0:T(8,128)(2,1)}), bf16[1,8192,256]{2,1,0:T(8,128)(2,1)}) %all-gather.3.cloned.1.call-update) | async-done | bytes 4194320 | tf_op jit(solution)/shard_map/all_gather | solution.py:129
  58.7 0.0 copy-start
  58.7 2.2 %copy-done = bf16[1,8192,256]{2,1,0:T(8,128)(2,1)S(1)} copy-done((bf16[1,8192,256]{2,1,0:T(8,128)(2,1)S(1)}, bf16[1,8192,256]{2,1,0:T(8,128)(2,1)}, u32[]{:S(2)}) %copy-start) | copy-done | bytes 4194328
  60.9 4.4 %shard_map.55 = bf16[8,2,128,512]{3,2,1,0:T(8,128)(2,1)} custom-call(s32[3]{0:T(128)S(1)} %pad_add_fusion.place_ref, bf16[4,128,1024]{2,1,0:T(8,128)(2,1)S(1)} %all-to-all-done.left_ref, bf16[8,2,512,256]{3,2,1,0:T(8,128)(2,1)S(1)} %bitcast.42), custom_call_target="tpu_custom_call" | custom-call | flops 2147483648 | bytes 7340032 | tf_op jit(solution)/shard_map/pallas_call | solution.py:82
  65.3 0.0 reduce-scatter.2.cloned.1.call-update
  65.3 44.9 %reduce-scatter.2.cloned.1.call-done = bf16[1,256,512]{2,1,0:T(8,128)(2,1)} async-done(((bf16[8,256,512]{2,1,0:T(8,128)(2,1)}), bf16[1,256,512]{2,1,0:T(8,128)(2,1)}) %reduce-scatter.2.cloned.1.call-update) | async-done | bytes 262160 | tf_op jit(solution)/shard_map/reduce_scatter | solution.py:149
  110.3 1.0 slice_bitcast_fusion.5
  111.3 1.9 %collective-permute-start.4 = (bf16[128,512]{1,0:T(8,128)(2,1)S(1)}, bf16[128,512]{1,0:T(8,128)(2,1)S(1)}, u32[]{:S(2)}, u32[]{:S(2)}) collective-permute-start(bf16[128,512]{1,0:T(8,128)(2,1)S(1)} %get-tuple-element.7), channel_id=1, source_target_pairs={{0,32},{1,33},{2,34},{3,35},{4,36},{5,37},{6,38},{7,39},{8,232},{9... | collective-permute-start | bytes 393224 | tf_op jit(solution)/shard_map/ppermute | solution.py:150
  113.2 7.0 %collective-permute-start.5 = (bf16[128,512]{1,0:T(8,128)(2,1)S(1)}, bf16[128,512]{1,0:T(8,128)(2,1)S(1)}, u32[]{:S(2)}, u32[]{:S(2)}) collective-permute-start(bf16[128,512]{1,0:T(8,128)(2,1)S(1)} %get-tuple-element.8), channel_id=1, source_target_pairs={{0,40},{1,41},{2,42},{3,43},{4,44},{5,45},{6,46},{7,47},{8,240},{9... | collective-permute-start | bytes 393224 | tf_op jit(solution)/shard_map/ppermute | solution.py:150
  120.2 7.1 %collective-permute-done.4 = bf16[128,512]{1,0:T(8,128)(2,1)S(1)} collective-permute-done((bf16[128,512]{1,0:T(8,128)(2,1)S(1)}, bf16[128,512]{1,0:T(8,128)(2,1)S(1)}, u32[]{:S(2)}, u32[]{:S(2)}) %collective-permute-start.4) | collective-permute-done | bytes 131104 | tf_op jit(solution)/shard_map/ppermute | solution.py:150
  127.3 2.9 %collective-permute-done.5 = bf16[128,512]{1,0:T(8,128)(2,1)S(1)} collective-permute-done((bf16[128,512]{1,0:T(8,128)(2,1)S(1)}, bf16[128,512]{1,0:T(8,128)(2,1)S(1)}, u32[]{:S(2)}, u32[]{:S(2)}) %collective-permute-start.5) | collective-permute-done | bytes 131104 | tf_op jit(solution)/shard_map/ppermute | solution.py:150
  130.2 0.7 pad_maximum_fusion.2
  (7 shorter events, 0.1 us)
Async XLA Ops:
  6.5 52.2 %all-gather.3.cloned.1.call-start = ((), (), s32[]{:S(2)}) async-start(), calls=%async_computation.3 | async-start | bytes 4456448 | tf_op jit(solution)/shard_map/all_gather | solution.py:129
  8.1 14.3 %collective-permute-start = (bf16[2,256,128]{2,1,0:T(8,128)(2,1)S(1)}, bf16[2,256,128]{2,1,0:T(8,128)(2,1)S(1)}, u32[]{:S(2)}, u32[]{:S(2)}) collective-permute-start(bf16[2,256,128]{2,1,0:T(8,128)(2,1)S(1)} %pad_maximum_fusion.3), channel_id=1, source_target_pairs={{0,1},{1,2},{2,3},{3,4},{4,5},{5,6},{6,7},{7,8},{8,9},{9,10},{10,1... | collective-permute-start | bytes 393224 | tf_op jit(solution)/shard_map/ppermute | solution.py:48
  11.6 14.7 %collective-permute-start.1 = (bf16[2,256,128]{2,1,0:T(8,128)(2,1)S(1)}, bf16[2,256,128]{2,1,0:T(8,128)(2,1)S(1)}, u32[]{:S(2)}, u32[]{:S(2)}) collective-permute-start(bf16[2,256,128]{2,1,0:T(8,128)(2,1)S(1)} %pad_maximum_fusion.3), channel_id=1, source_target_pairs={{0,2},{1,3},{2,4},{3,5},{4,6},{5,7},{6,8},{7,9},{8,10},{9,11},{10,... | collective-permute-start | bytes 393224 | tf_op jit(solution)/shard_map/ppermute | solution.py:48
  17.3 11.6 %collective-permute-start.3 = (bf16[128,512]{0,1:T(8,128)(2,1)S(1)}, bf16[128,512]{0,1:T(8,128)(2,1)S(1)}, u32[]{:S(2)}, u32[]{:S(2)}) collective-permute-start(bf16[128,512]{0,1:T(8,128)(2,1)S(1)} %bitcast.49), channel_id=1, source_target_pairs={{0,256},{256,0},{1,257},{257,1},{2,258},{258,2},{3,259},{259,3},{4... | collective-permute-start | bytes 393224 | tf_op jit(solution)/shard_map/ppermute | solution.py:137
  26.4 3.6 %collective-permute-start.2 = (bf16[2,512,128]{2,1,0:T(8,128)(2,1)S(1)}, bf16[2,512,128]{2,1,0:T(8,128)(2,1)S(1)}, u32[]{:S(2)}, u32[]{:S(2)}) collective-permute-start(bf16[2,512,128]{2,1,0:T(8,128)(2,1)S(1)} %pad_maximum_fusion), channel_id=1, source_target_pairs={{0,256},{256,0},{1,257},{257,1},{2,258},{258,2},{3,259},{259,3},{4... | collective-permute-start | bytes 786440 | tf_op jit(solution)/shard_map/ppermute | solution.py:138
  34.8 18.1 %all-to-all-start = ((bf16[4,128,1024]{2,1,0:T(8,128)(2,1)}), bf16[4,128,1024]{2,1,0:T(8,128)(2,1)S(1)}, u32[]{:S(2)}, u32[]{:S(2)}) async-start(bf16[4,128,1024]{2,1,0:T(8,128)(2,1)} %broadcast_in_dim.55), calls=%async_computation | async-start | bytes 2097152 | tf_op jit(solution)/shard_map/all_to_all | solution.py:145
  39.5 70.8 %reduce-scatter.2.cloned.1.call-start = ((), (), s32[]{:S(2)}) async-start(), calls=%async_computation.2 | async-start | bytes 2359296 | tf_op jit(solution)/shard_map/reduce_scatter | solution.py:149
  58.7 2.2 %copy-start = (bf16[1,8192,256]{2,1,0:T(8,128)(2,1)S(1)}, bf16[1,8192,256]{2,1,0:T(8,128)(2,1)}, u32[]{:S(2)}) copy-start(bf16[1,8192,256]{2,1,0:T(8,128)(2,1)} %all-gather.3.cloned.1.call-done) | copy-start | bytes 12582916
  111.3 16.0 %collective-permute-start.4 = (bf16[128,512]{1,0:T(8,128)(2,1)S(1)}, bf16[128,512]{1,0:T(8,128)(2,1)S(1)}, u32[]{:S(2)}, u32[]{:S(2)}) collective-permute-start(bf16[128,512]{1,0:T(8,128)(2,1)S(1)} %get-tuple-element.7), channel_id=1, source_target_pairs={{0,32},{1,33},{2,34},{3,35},{4,36},{5,37},{6,38},{7,39},{8,232},{9... | collective-permute-start | bytes 393224 | tf_op jit(solution)/shard_map/ppermute | solution.py:150
  113.2 17.0 %collective-permute-start.5 = (bf16[128,512]{1,0:T(8,128)(2,1)S(1)}, bf16[128,512]{1,0:T(8,128)(2,1)S(1)}, u32[]{:S(2)}, u32[]{:S(2)}) collective-permute-start(bf16[128,512]{1,0:T(8,128)(2,1)S(1)} %get-tuple-element.8), channel_id=1, source_target_pairs={{0,40},{1,41},{2,42},{3,43},{4,44},{5,45},{6,46},{7,47},{8,240},{9... | collective-permute-start | bytes 393224 | tf_op jit(solution)/shard_map/ppermute | solution.py:150
Sparse Core Ops, SparseCore 0:
  9.5 49.2 all-gather.2
  65.5 44.7 reduce-scatter.1

commit v11 on v9

--- a/solution.py
+++ b/solution.py
@@ -107,18 +107,16 @@
     def shift_of(x):
         return tiles - 1 + (x % 2) * (tiles // 2)
 
-    to_owner = [[], []]
-    for t in range(2):
-        for c in range(n_grp):
+    to_rows, to_owner = [[] for _ in range(SX)], []
+    for c in range(n_grp):
+        for x in range(SX):
+            for b in range(SX):
+                to_rows[b].append(((c ^ (b % 2)) * SX + (x + c + 2 * (b // 2)) % SX, c * SX + x))
             for z in range(n_kv):
-                for x in range(SX):
-                    j = (z // 2 - shift_of(x)) % tiles
-                    to_x = 2 * (z % 2) + (c ^ t)
-                    owner = x * tiles + j
-                    for y in range(sy):
-                        to_owner[t].append(
-                            (index(c, z, x, y), index(owner // n_kv, owner % n_kv, to_x, y))
-                        )
+                owner = x * tiles + (z // 2 - shift_of(x)) % tiles
+                to_x = (x + c + 2 * (z % 2)) % SX
+                for y in range(sy):
+                    to_owner.append((index(c, z, x, y), index(owner // n_kv, owner % n_kv, to_x, y)))
 
     def on_device(queries, keys, values, lengths, weight):
         tokens = queries.shape[0]
@@ -141,14 +139,12 @@
         first = core == 0
         both = jnp.concatenate([jnp.where(first, own, other), jnp.where(first, other, own)], axis=1)
         heads = attend(both, window[0], window[1], query_pos, key_pos.reshape(-1), lengths)
-        along = lax.all_to_all(jnp.broadcast_to(heads, (SX,) + heads.shape), "sx", 0, 0)
+        along = jnp.stack([lax.ppermute(heads, ("grp", "sx"), to_rows[b]) for b in range(SX)])
 
         partial = product(jnp.stack([core, shift_of(across)]), along, columns)
         partial = partial.reshape(n_kv, 2 * half, partial.shape[3])
-        summed = lax.psum_scatter(partial, "kv", scatter_dimension=0).reshape(2, half, -1)
-        early, late = [lax.ppermute(summed[t], ALL, to_owner[t]) for t in range(2)]
-        even = across % 2 == 0
-        return jnp.concatenate([jnp.where(even, early, late), jnp.where(even, late, early)], axis=0)
+        tile = lax.psum_scatter(partial, "kv", scatter_dimension=0)
+        return lax.ppermute(tile, ALL, to_owner)
 
     q = P(("sx", "sy"), "kv", "grp")
     k = P(("sx", "sy"), "kv", None)

time: 138 us -> 137 us (level)
  waiting for transfers between devices: 80.7 us -> 82.4 us
  local copies, waits for them, and re-layouts: 5.74 us -> 4.35 us
    ppermute x2 -> x5, waiting for transfers between devices: 10.9 us -> 25.3 us  [the longest x1 17.1 us: on_device(): return lax.ppermute(tile, ALL, to_owner)]
    all_to_all x1 -> x0, waiting for transfers between devices: 13.3 us -> none  [on_device(): lax.all_to_all(jnp.broadcast_to(heads, (SX,) + heads.shape), 'sx', 0, 0)]
    all_to_all x1 -> x0, starting transfers between devices: 4.71 us -> none  [on_device(): lax.all_to_all(jnp.broadcast_to(heads, (SX,) + heads.shape), 'sx', 0, 0)]
    ppermute x2 -> x5, starting transfers between devices: 7.96 us -> 12 us  [the longest x4 10.1 us: on_device(): lax.ppermute(heads, ('grp', 'sx'), to_rows[b])]
    unnamed x2 -> x3, local copies, waits for them, and re-layouts: 2.19 us -> 2.89 us
  transfers between devices with their start and end apart: 9 -> 11, of which waited for: 7 -> 7; matrix products, arithmetic and copies ran while one was open for 6% -> 5% of each run, Pallas kernels for 0% -> 0%
where the time goes in v11:
time: 137 us
  waiting for transfers between devices  82.4 us (60%)
  starting transfers between devices  26.3 us (19%)
  between operations  13.6 us (10%)
  Pallas kernels  4.41 us (3%)
  local copies, waits for them, and re-layouts  4.35 us (3%)
  other arithmetic  3.95 us (3%)
  matrix products  1.86 us (1%)
    reduce_scatter x1, waiting for transfers between devices, on_device(): tile = lax.psum_scatter(partial, 'kv', scatter_dimension=0)  45.1 us
    ppermute x1, waiting for transfers between devices, on_device(): return lax.ppermute(tile, ALL, to_owner)  17.1 us
    ppermute x4, starting transfers between devices, on_device(): lax.ppermute(heads, ('grp', 'sx'), to_rows[b])  10.1 us
    ppermute x4, waiting for transfers between devices, on_device(): lax.ppermute(heads, ('grp', 'sx'), to_rows[b])  8.27 us
    ppermute x2, starting transfers between devices, fetch_behind(): return lax.ppermute(stacked, ('grp', 'sx', 'sy'), route)  7.98 us
    all_gather x1, waiting for transfers between devices, on_device(): columns = lax.all_gather(weight[0], ('sy', 'grp'), axis=0, tiled=True)  6.34 us
    pallas_call x1, Pallas kernels, product(): pl.pallas_call(product_kernel, grid_spec=grid_spec, out_shape=jax.ShapeDt...  4.41 us
    ppermute x2, waiting for transfers between devices, fetch_behind(): return lax.ppermute(stacked, ('grp', 'sx', 'sy'), route)  3.87 us
  transfers between devices with their start and end apart: 11, of which 7 were waited for; matrix products, arithmetic and copies ran while one was open for 5% of the time, Pallas kernels for 0%

profile of v11, /device:TPU:6, one launch (start us, length us, event | category | flops | bytes accessed | tf_op | source)
XLA Modules:
  0.0 136.9 jit_solution(17168516966327817623)
XLA Ops:
  6.5 0.0 all-gather.3.cloned.1.call-start
  6.5 0.7 all-gather.3.cloned.1.call-update
  7.3 0.0 reduce-scatter.2.cloned.1.call-start
  7.3 0.9 pad_maximum_fusion.3
  8.2 3.5 %collective-permute-start = (bf16[2,256,128]{2,1,0:T(8,128)(2,1)S(1)}, bf16[2,256,128]{2,1,0:T(8,128)(2,1)S(1)}, u32[]{:S(2)}, u32[]{:S(2)}) collective-permute-start(bf16[2,256,128]{2,1,0:T(8,128)(2,1)S(1)} %pad_maximum_fusion.3), channel_id=1, source_target_pairs={{0,1},{1,2},{2,3},{3,4},{4,5},{5,6},{6,7},{7,8},{8,9},{9,10},{10,1... | collective-permute-start | bytes 393224 | tf_op jit(solution)/shard_map/ppermute | solution.py:48
  11.7 4.5 %collective-permute-start.1 = (bf16[2,256,128]{2,1,0:T(8,128)(2,1)S(1)}, bf16[2,256,128]{2,1,0:T(8,128)(2,1)S(1)}, u32[]{:S(2)}, u32[]{:S(2)}) collective-permute-start(bf16[2,256,128]{2,1,0:T(8,128)(2,1)S(1)} %pad_maximum_fusion.3), channel_id=1, source_target_pairs={{0,2},{1,3},{2,4},{3,5},{4,6},{5,7},{6,8},{7,9},{8,10},{9,11},{10,... | collective-permute-start | bytes 393224 | tf_op jit(solution)/shard_map/ppermute | solution.py:48
  16.2 1.0 constant_dynamic-slice_fusion.1
  17.2 0.1 copy.16
  17.3 3.7 %collective-permute-start.3 = (bf16[128,512]{0,1:T(8,128)(2,1)S(1)}, bf16[128,512]{0,1:T(8,128)(2,1)S(1)}, u32[]{:S(2)}, u32[]{:S(2)}) collective-permute-start(bf16[128,512]{0,1:T(8,128)(2,1)S(1)} %bitcast.53), channel_id=1, source_target_pairs={{0,256},{256,0},{1,257},{257,1},{2,258},{258,2},{3,259},{259,3},{4... | collective-permute-start | bytes 393224 | tf_op jit(solution)/shard_map/ppermute | solution.py:134
  21.1 0.1 stack.50
  21.2 0.1 iota_add_fusion
  21.3 0.8 select_reduce_fusion.1
  22.0 0.1 select_reduce_fusion
  22.1 0.2 compare_and_fusion
  22.4 0.1 copy.15
  22.5 0.0 collective-permute-done
  22.5 3.9 %collective-permute-done.1 = bf16[2,256,128]{2,1,0:T(8,128)(2,1)S(1)} collective-permute-done((bf16[2,256,128]{2,1,0:T(8,128)(2,1)S(1)}, bf16[2,256,128]{2,1,0:T(8,128)(2,1)S(1)}, u32[]{:S(2)}, u32[]{:S(2)}) %collective-permute-start.1) | collective-permute-done | bytes 131104 | tf_op jit(solution)/shard_map/ppermute | solution.py:48
  26.4 2.5 %collective-permute-start.2 = (bf16[2,512,128]{2,1,0:T(8,128)(2,1)S(1)}, bf16[2,512,128]{2,1,0:T(8,128)(2,1)S(1)}, u32[]{:S(2)}, u32[]{:S(2)}) collective-permute-start(bf16[2,512,128]{2,1,0:T(8,128)(2,1)S(1)} %pad_maximum_fusion.1), channel_id=1, source_target_pairs={{0,256},{256,0},{1,257},{257,1},{2,258},{258,2},{3,259},{259,3},{4... | collective-permute-start | bytes 786440 | tf_op jit(solution)/shard_map/ppermute | solution.py:135
  28.9 0.0 collective-permute-done.3
  29.0 1.1 collective-permute-done.2
  30.0 0.9 maximum_maximum_fusion
  31.0 0.8 fusion.14
  31.8 0.7 fusion
  32.5 1.0 fusion.11
  33.5 0.1 copy.25
  33.7 0.7 collective-permute-start.4
  34.4 2.2 %collective-permute-start.5 = (bf16[128,1024]{1,0:T(8,128)(2,1)S(1)}, bf16[128,1024]{1,0:T(8,128)(2,1)S(1)}, u32[]{:S(2)}, u32[]{:S(2)}) collective-permute-start(bf16[128,1024]{1,0:T(8,128)(2,1)S(1)} %copy.25), channel_id=1, source_target_pairs={{256,0},{264,8},{272,16},{280,24},{8,256},{16,264},{24,272},{0,280... | collective-permute-start | bytes 786440 | tf_op jit(solution)/shard_map/ppermute | solution.py:142
  36.5 5.4 %collective-permute-start.6 = (bf16[128,1024]{1,0:T(8,128)(2,1)S(1)}, bf16[128,1024]{1,0:T(8,128)(2,1)S(1)}, u32[]{:S(2)}, u32[]{:S(2)}) collective-permute-start(bf16[128,1024]{1,0:T(8,128)(2,1)S(1)} %copy.25), channel_id=1, source_target_pairs={{16,0},{24,8},{0,16},{8,24},{280,256},{256,264},{264,272},{272,280... | collective-permute-start | bytes 786440 | tf_op jit(solution)/shard_map/ppermute | solution.py:142
  41.9 1.9 %collective-permute-start.7 = (bf16[128,1024]{1,0:T(8,128)(2,1)S(1)}, bf16[128,1024]{1,0:T(8,128)(2,1)S(1)}, u32[]{:S(2)}, u32[]{:S(2)}) collective-permute-start(bf16[128,1024]{1,0:T(8,128)(2,1)S(1)} %copy.25), channel_id=1, source_target_pairs={{272,0},{280,8},{256,16},{264,24},{24,256},{0,264},{8,272},{16,280... | collective-permute-start | bytes 786440 | tf_op jit(solution)/shard_map/ppermute | solution.py:142
  43.9 0.1 pad_add_fusion.place_ref
  43.9 0.0 collective-permute-done.4
  43.9 0.0 collective-permute-done.5
  43.9 3.3 %collective-permute-done.6 = bf16[128,1024]{1,0:T(8,128)(2,1)S(1)} collective-permute-done((bf16[128,1024]{1,0:T(8,128)(2,1)S(1)}, bf16[128,1024]{1,0:T(8,128)(2,1)S(1)}, u32[]{:S(2)}, u32[]{:S(2)}) %collective-permute-start.6) | collective-permute-done | bytes 262176 | tf_op jit(solution)/shard_map/ppermute | solution.py:142
  47.3 4.9 %collective-permute-done.7 = bf16[128,1024]{1,0:T(8,128)(2,1)S(1)} collective-permute-done((bf16[128,1024]{1,0:T(8,128)(2,1)S(1)}, bf16[128,1024]{1,0:T(8,128)(2,1)S(1)}, u32[]{:S(2)}, u32[]{:S(2)}) %collective-permute-start.7) | collective-permute-done | bytes 262176 | tf_op jit(solution)/shard_map/ppermute | solution.py:142
  52.2 0.1 pad_maximum_fusion.left_ref
  52.3 6.3 %all-gather.3.cloned.1.call-done = bf16[1,8192,256]{2,1,0:T(8,128)(2,1)} async-done(((bf16[1,512,256]{2,1,0:T(8,128)(2,1)}), bf16[1,8192,256]{2,1,0:T(8,128)(2,1)}) %all-gather.3.cloned.1.call-update) | async-done | bytes 4194320 | tf_op jit(solution)/shard_map/all_gather | solution.py:126
  58.7 0.0 copy-start
  58.7 2.2 %copy-done = bf16[1,8192,256]{2,1,0:T(8,128)(2,1)S(1)} copy-done((bf16[1,8192,256]{2,1,0:T(8,128)(2,1)S(1)}, bf16[1,8192,256]{2,1,0:T(8,128)(2,1)}, u32[]{:S(2)}) %copy-start) | copy-done | bytes 4194328
  60.9 4.4 %shard_map.55 = bf16[8,2,128,512]{3,2,1,0:T(8,128)(2,1)} custom-call(s32[2]{0:T(128)S(1)} %pad_add_fusion.place_ref, bf16[4,128,1024]{2,1,0:T(8,128)(2,1)S(1)} %pad_maximum_fusion.left_ref, bf16[8,2,512,256]{3,2,1,0:T(8,128)(2,1)S(1)} %bitcast.42), custom_call_target="tpu_custom_call" | custom-call | flops 2147483648 | bytes 7340032 | tf_op jit(solution)/shard_map/pallas_call | solution.py:81
  65.3 0.0 reduce-scatter.2.cloned.1.call-update
  65.3 45.1 %reduce-scatter.2.cloned.1.call-done = bf16[1,256,512]{2,1,0:T(8,128)(2,1)} async-done(((bf16[8,256,512]{2,1,0:T(8,128)(2,1)}), bf16[1,256,512]{2,1,0:T(8,128)(2,1)}) %reduce-scatter.2.cloned.1.call-update) | async-done | bytes 262160 | tf_op jit(solution)/shard_map/reduce_scatter | solution.py:146
  110.4 1.9 %collective-permute-start.8 = (bf16[256,512]{1,0:T(8,128)(2,1)}, bf16[256,512]{1,0:T(8,128)(2,1)S(1)}, u32[]{:S(2)}, u32[]{:S(2)}) collective-permute-start(bf16[256,512]{1,0:T(8,128)(2,1)} %bitcast.55), channel_id=1, source_target_pairs={{0,32},{1,33},{2,34},{3,35},{4,36},{5,37},{6,38},{7,39},{32,48},{3... | collective-permute-start | bytes 786440 | tf_op jit(solution)/shard_map/ppermute | solution.py:147
  112.3 17.1 %collective-permute-done.8 = bf16[256,512]{1,0:T(8,128)(2,1)S(1)} collective-permute-done((bf16[256,512]{1,0:T(8,128)(2,1)}, bf16[256,512]{1,0:T(8,128)(2,1)S(1)}, u32[]{:S(2)}, u32[]{:S(2)}) %collective-permute-start.8) | collective-permute-done | bytes 262176 | tf_op jit(solution)/shard_map/ppermute | solution.py:147
  129.3 0.7 copy.27
  (6 shorter events, 0.1 us)
Async XLA Ops:
  6.5 52.1 %all-gather.3.cloned.1.call-start = ((), (), s32[]{:S(2)}) async-start(), calls=%async_computation.2 | async-start | bytes 4456448 | tf_op jit(solution)/shard_map/all_gather | solution.py:126
  7.3 103.1 %reduce-scatter.2.cloned.1.call-start = ((), (), s32[]{:S(2)}) async-start(), calls=%async_computation.1 | async-start | bytes 2359296 | tf_op jit(solution)/shard_map/reduce_scatter | solution.py:146
  8.2 14.3 %collective-permute-start = (bf16[2,256,128]{2,1,0:T(8,128)(2,1)S(1)}, bf16[2,256,128]{2,1,0:T(8,128)(2,1)S(1)}, u32[]{:S(2)}, u32[]{:S(2)}) collective-permute-start(bf16[2,256,128]{2,1,0:T(8,128)(2,1)S(1)} %pad_maximum_fusion.3), channel_id=1, source_target_pairs={{0,1},{1,2},{2,3},{3,4},{4,5},{5,6},{6,7},{7,8},{8,9},{9,10},{10,1... | collective-permute-start | bytes 393224 | tf_op jit(solution)/shard_map/ppermute | solution.py:48
  11.7 14.7 %collective-permute-start.1 = (bf16[2,256,128]{2,1,0:T(8,128)(2,1)S(1)}, bf16[2,256,128]{2,1,0:T(8,128)(2,1)S(1)}, u32[]{:S(2)}, u32[]{:S(2)}) collective-permute-start(bf16[2,256,128]{2,1,0:T(8,128)(2,1)S(1)} %pad_maximum_fusion.3), channel_id=1, source_target_pairs={{0,2},{1,3},{2,4},{3,5},{4,6},{5,7},{6,8},{7,9},{8,10},{9,11},{10,... | collective-permute-start | bytes 393224 | tf_op jit(solution)/shard_map/ppermute | solution.py:48
  17.3 11.6 %collective-permute-start.3 = (bf16[128,512]{0,1:T(8,128)(2,1)S(1)}, bf16[128,512]{0,1:T(8,128)(2,1)S(1)}, u32[]{:S(2)}, u32[]{:S(2)}) collective-permute-start(bf16[128,512]{0,1:T(8,128)(2,1)S(1)} %bitcast.53), channel_id=1, source_target_pairs={{0,256},{256,0},{1,257},{257,1},{2,258},{258,2},{3,259},{259,3},{4... | collective-permute-start | bytes 393224 | tf_op jit(solution)/shard_map/ppermute | solution.py:134
  26.4 3.6 %collective-permute-start.2 = (bf16[2,512,128]{2,1,0:T(8,128)(2,1)S(1)}, bf16[2,512,128]{2,1,0:T(8,128)(2,1)S(1)}, u32[]{:S(2)}, u32[]{:S(2)}) collective-permute-start(bf16[2,512,128]{2,1,0:T(8,128)(2,1)S(1)} %pad_maximum_fusion.1), channel_id=1, source_target_pairs={{0,256},{256,0},{1,257},{257,1},{2,258},{258,2},{3,259},{259,3},{4... | collective-permute-start | bytes 786440 | tf_op jit(solution)/shard_map/ppermute | solution.py:135
  33.7 10.2 %collective-permute-start.4 = (bf16[128,1024]{1,0:T(8,128)(2,1)S(1)}, bf16[128,1024]{1,0:T(8,128)(2,1)S(1)}, u32[]{:S(2)}, u32[]{:S(2)}) collective-permute-start(bf16[128,1024]{1,0:T(8,128)(2,1)S(1)} %copy.25), channel_id=1, source_target_pairs={{0,0},{8,8},{16,16},{24,24},{264,256},{272,264},{280,272},{256,280... | collective-permute-start | bytes 786440 | tf_op jit(solution)/shard_map/ppermute | solution.py:142
  34.4 9.6 %collective-permute-start.5 = (bf16[128,1024]{1,0:T(8,128)(2,1)S(1)}, bf16[128,1024]{1,0:T(8,128)(2,1)S(1)}, u32[]{:S(2)}, u32[]{:S(2)}) collective-permute-start(bf16[128,1024]{1,0:T(8,128)(2,1)S(1)} %copy.25), channel_id=1, source_target_pairs={{256,0},{264,8},{272,16},{280,24},{8,256},{16,264},{24,272},{0,280... | collective-permute-start | bytes 786440 | tf_op jit(solution)/shard_map/ppermute | solution.py:142
  36.5 10.7 %collective-permute-start.6 = (bf16[128,1024]{1,0:T(8,128)(2,1)S(1)}, bf16[128,1024]{1,0:T(8,128)(2,1)S(1)}, u32[]{:S(2)}, u32[]{:S(2)}) collective-permute-start(bf16[128,1024]{1,0:T(8,128)(2,1)S(1)} %copy.25), channel_id=1, source_target_pairs={{16,0},{24,8},{0,16},{8,24},{280,256},{256,264},{264,272},{272,280... | collective-permute-start | bytes 786440 | tf_op jit(solution)/shard_map/ppermute | solution.py:142
  41.9 10.3 %collective-permute-start.7 = (bf16[128,1024]{1,0:T(8,128)(2,1)S(1)}, bf16[128,1024]{1,0:T(8,128)(2,1)S(1)}, u32[]{:S(2)}, u32[]{:S(2)}) collective-permute-start(bf16[128,1024]{1,0:T(8,128)(2,1)S(1)} %copy.25), channel_id=1, source_target_pairs={{272,0},{280,8},{256,16},{264,24},{24,256},{0,264},{8,272},{16,280... | collective-permute-start | bytes 786440 | tf_op jit(solution)/shard_map/ppermute | solution.py:142
  58.7 2.2 %copy-start = (bf16[1,8192,256]{2,1,0:T(8,128)(2,1)S(1)}, bf16[1,8192,256]{2,1,0:T(8,128)(2,1)}, u32[]{:S(2)}) copy-start(bf16[1,8192,256]{2,1,0:T(8,128)(2,1)} %all-gather.3.cloned.1.call-done) | copy-start | bytes 12582916
  110.4 19.0 %collective-permute-start.8 = (bf16[256,512]{1,0:T(8,128)(2,1)}, bf16[256,512]{1,0:T(8,128)(2,1)S(1)}, u32[]{:S(2)}, u32[]{:S(2)}) collective-permute-start(bf16[256,512]{1,0:T(8,128)(2,1)} %bitcast.55), channel_id=1, source_target_pairs={{0,32},{1,33},{2,34},{3,35},{4,36},{5,37},{6,38},{7,39},{32,48},{3... | collective-permute-start | bytes 786440 | tf_op jit(solution)/shard_map/ppermute | solution.py:147
Sparse Core Ops, SparseCore 0:
  9.5 49.1 all-gather.2
  65.4 44.8 reduce-scatter.1

commit v12 on v11

--- a/solution.py
+++ b/solution.py
@@ -51,16 +51,12 @@
 def product_kernel(place_ref, left_ref, right_ref, out_ref):
     blocks, tokens, depth = left_ref.shape
     left = left_ref[...].reshape(blocks * tokens, depth)
-    core = place_ref[0]
-    pieces, _, _, width = right_ref.shape
-    for piece in range(pieces):
-        total = jnp.dot(
-            left, right_ref[piece].reshape(depth, width), preferred_element_type=jnp.float32
-        ).astype(out_ref.dtype)
-        for x in range(blocks):
-            out_ref[x // 2, (x % 2) ^ core, :, piece * width : (piece + 1) * width] = total[
-                x * tokens : (x + 1) * tokens
-            ]
+    across = place_ref[0]
+    right = right_ref[0].reshape(depth, right_ref.shape[3])
+    total = jnp.dot(left, right, preferred_element_type=jnp.float32).astype(out_ref.dtype)
+    for b in range(blocks):
+        e = (across + b) % blocks
+        out_ref[0, (e % 2) ^ (across % 2), e // 2] = total[b * tokens : (b + 1) * tokens]
 
 
 def product(place, left, right):
@@ -69,23 +65,23 @@
     tiles = pieces // 2
     grid_spec = pltpu.PrefetchScalarGridSpec(
         num_scalar_prefetch=1,
-        grid=(tiles,),
+        grid=(pieces,),
         in_specs=[
             pl.BlockSpec(memory_space=pltpu.VMEM),
-            pl.BlockSpec((2, cores, half, width), lambda j, place: (j, 0, 0, 0)),
+            pl.BlockSpec(
+                (1, cores, half, width), lambda z, place: (2 * (z % tiles) + (z // tiles + place[1]) % 2, 0, 0, 0)
+            ),
         ],
-        out_specs=pl.BlockSpec(
-            (blocks // 2, 2, tokens, 2 * width), lambda j, place: ((j + place[1]) % tiles, 0, 0, 0)
-        ),
+        out_specs=pl.BlockSpec((1, 2, blocks // 2, tokens, width), lambda z, place: (z, 0, 0, 0, 0)),
     )
     return pl.pallas_call(
         product_kernel,
         grid_spec=grid_spec,
-        out_shape=jax.ShapeDtypeStruct((tiles * blocks // 2, 2, tokens, 2 * width), jnp.bfloat16),
+        out_shape=jax.ShapeDtypeStruct((pieces, 2, blocks // 2, tokens, width), jnp.bfloat16),
         compiler_params=pltpu.CompilerParams(vmem_limit_bytes=40 * 2**20),
         cost_estimate=pl.CostEstimate(
             flops=2 * blocks * tokens * right.size,
-            bytes_accessed=2 * (left.size + right.size + tiles * blocks * tokens * 2 * width),
+            bytes_accessed=2 * (left.size + right.size + pieces * blocks * tokens * width),
             transcendentals=0,
         ),
     )(place, left, right)
@@ -96,7 +92,6 @@
     sy = n_srv // SX
     sizes = (n_grp, n_kv, SX, sy)
     fine = jax.sharding.Mesh(mesh.devices.reshape(sizes), ALL)
-    tiles = n_grp * n_kv // SX
 
     def index(*place):
         total = 0
@@ -104,26 +99,31 @@
             total = total * size + at
         return total
 
-    def shift_of(x):
-        return tiles - 1 + (x % 2) * (tiles // 2)
-
-    to_rows, to_owner = [[] for _ in range(SX)], []
+    to_rows, to_owner = [[] for _ in range(SX)], [[], []]
     for c in range(n_grp):
         for x in range(SX):
             for b in range(SX):
-                to_rows[b].append(((c ^ (b % 2)) * SX + (x + c + 2 * (b // 2)) % SX, c * SX + x))
+                e = (x + b) % SX
+                to_rows[b].append(((e // 2) * SX + 2 * c + e % 2, c * SX + x))
             for z in range(n_kv):
-                owner = x * tiles + (z // 2 - shift_of(x)) % tiles
-                to_x = (x + c + 2 * (z % 2)) % SX
                 for y in range(sy):
-                    to_owner.append((index(c, z, x, y), index(owner // n_kv, owner % n_kv, to_x, y)))
+                    for h in range(2):
+                        owner = index(x // 2, z, 2 * c + (x % 2 ^ h), y)
+                        to_owner[h].append((index(c, z, x, y), owner))
+
+    groups = [
+        [index(c, z, 2 * a + (y + odd) % 2, y) for y in range(sy) for c in range(n_grp)]
+        for z in range(n_kv)
+        for a in range(SX // 2)
+        for odd in range(2)
+    ]
 
     def on_device(queries, keys, values, lengths, weight):
         tokens = queries.shape[0]
         core = lax.axis_index("grp")
         across = lax.axis_index("sx")
         shard = across * sy + lax.axis_index("sy")
-        columns = lax.all_gather(weight[0], ("sy", "grp"), axis=0, tiled=True)
+        columns = lax.all_gather(weight[0], ALL, axis=0, tiled=True, axis_index_groups=groups)
         columns = columns.reshape(sy, n_grp, weight.shape[1], weight.shape[2])
 
         half = tokens // n_grp
@@ -141,10 +141,13 @@
         heads = attend(both, window[0], window[1], query_pos, key_pos.reshape(-1), lengths)
         along = jnp.stack([lax.ppermute(heads, ("grp", "sx"), to_rows[b]) for b in range(SX)])
 
-        partial = product(jnp.stack([core, shift_of(across)]), along, columns)
-        partial = partial.reshape(n_kv, 2 * half, partial.shape[3])
-        tile = lax.psum_scatter(partial, "kv", scatter_dimension=0)
-        return lax.ppermute(tile, ALL, to_owner)
+        partial = product(jnp.stack([across, (across + lax.axis_index("sy")) % 2]), along, columns)
+        width = partial.shape[4]
+        summed = lax.psum_scatter(partial.reshape(n_kv, 2 * tokens, width), "kv", scatter_dimension=0)
+        summed = summed.reshape(2, tokens, width)
+        near, far = [lax.ppermute(summed[h], ALL, to_owner[h]) for h in range(2)]
+        flip = (across + lax.axis_index("sy") + lax.axis_index("kv") // (n_kv // 2)) % 2 == 1
+        return jnp.concatenate([jnp.where(flip, far, near), jnp.where(flip, near, far)], axis=1)
 
     q = P(("sx", "sy"), "kv", "grp")
     k = P(("sx", "sy"), "kv", None)

time: 137 us -> 162 us (1.18)
  the two profiles are of different devices: /device:TPU:6 before, /device:TPU:1 now
where the time goes in v12:
time: 162 us; the launch traced here: 161 us
  waiting for transfers between devices  89 us (55%)
  starting transfers between devices  42 us (26%)
  between operations  13.7 us (8%)
  Pallas kernels  5.59 us (3%)
  other arithmetic  4.7 us (3%)
  local copies, waits for them, and re-layouts  4.63 us (3%)
  matrix products  1.86 us (1%)
    reduce_scatter x1, waiting for transfers between devices, on_device(): lax.psum_scatter(partial.reshape(n_kv, 2 * tokens, width), 'kv', scatter_...  42.3 us
    ppermute x4, waiting for transfers between devices, on_device(): lax.ppermute(heads, ('grp', 'sx'), to_rows[b])  37.2 us
    ppermute x4, starting transfers between devices, on_device(): lax.ppermute(heads, ('grp', 'sx'), to_rows[b])  15.7 us
    ppermute x2, starting transfers between devices, on_device(): near, far = [lax.ppermute(summed[h], ALL, to_owner[h]) for h in range(2)]  11.6 us
    ppermute x2, starting transfers between devices, fetch_behind(): return lax.ppermute(stacked, ('grp', 'sx', 'sy'), route)  10.8 us
    pallas_call x1, Pallas kernels, product(): pl.pallas_call(product_kernel, grid_spec=grid_spec, out_shape=jax.ShapeDt...  5.59 us
    ppermute x2, waiting for transfers between devices, on_device(): near, far = [lax.ppermute(summed[h], ALL, to_owner[h]) for h in range(2)]  5.11 us
  transfers between devices with their start and end apart: 12, of which 7 were waited for; matrix products, arithmetic and copies ran while one was open for 5% of the time, Pallas kernels for 0%

profile of v12, /device:TPU:1, one launch (start us, length us, event | category | flops | bytes accessed | tf_op | source)
XLA Modules:
  0.0 161.4 jit_solution(15281607835041887625)
XLA Ops:
  6.5 0.0 all-gather.3.cloned.1.call-start
  6.5 0.7 all-gather.3.cloned.1.call-update
  7.3 0.0 reduce-scatter.2.cloned.1.call-start
  7.3 0.9 pad_maximum_fusion.4
  8.2 6.1 %collective-permute-start = (bf16[2,256,128]{2,1,0:T(8,128)(2,1)S(1)}, bf16[2,256,128]{2,1,0:T(8,128)(2,1)S(1)}, u32[]{:S(2)}, u32[]{:S(2)}) collective-permute-start(bf16[2,256,128]{2,1,0:T(8,128)(2,1)S(1)} %pad_maximum_fusion.4), channel_id=1, source_target_pairs={{0,1},{1,2},{2,3},{3,4},{4,5},{5,6},{6,7},{7,8},{8,9},{9,10},{10,1... | collective-permute-start | bytes 393224 | tf_op jit(solution)/shard_map/ppermute | solution.py:48
  14.3 4.8 %collective-permute-start.1 = (bf16[2,256,128]{2,1,0:T(8,128)(2,1)S(1)}, bf16[2,256,128]{2,1,0:T(8,128)(2,1)S(1)}, u32[]{:S(2)}, u32[]{:S(2)}) collective-permute-start(bf16[2,256,128]{2,1,0:T(8,128)(2,1)S(1)} %pad_maximum_fusion.4), channel_id=1, source_target_pairs={{0,2},{1,3},{2,4},{3,5},{4,6},{5,7},{6,8},{7,9},{8,10},{9,11},{10,... | collective-permute-start | bytes 393224 | tf_op jit(solution)/shard_map/ppermute | solution.py:48
  19.0 1.0 constant_dynamic-slice_fusion.1
  20.0 0.1 copy.16
  20.2 1.9 %collective-permute-start.3 = (bf16[128,512]{0,1:T(8,128)(2,1)S(1)}, bf16[128,512]{0,1:T(8,128)(2,1)S(1)}, u32[]{:S(2)}, u32[]{:S(2)}) collective-permute-start(bf16[128,512]{0,1:T(8,128)(2,1)S(1)} %bitcast.56), channel_id=1, source_target_pairs={{0,256},{256,0},{1,257},{257,1},{2,258},{258,2},{3,259},{259,3},{4... | collective-permute-start | bytes 393224 | tf_op jit(solution)/shard_map/ppermute | solution.py:134
  22.1 0.1 stack.50
  22.2 0.1 iota_add_fusion
  22.3 0.8 select_reduce_fusion.1
  23.0 0.1 select_reduce_fusion
  23.1 0.2 compare_and_fusion
  23.4 0.1 copy.15
  23.5 0.0 collective-permute-done
  23.5 2.1 %collective-permute-done.1 = bf16[2,256,128]{2,1,0:T(8,128)(2,1)S(1)} collective-permute-done((bf16[2,256,128]{2,1,0:T(8,128)(2,1)S(1)}, bf16[2,256,128]{2,1,0:T(8,128)(2,1)S(1)}, u32[]{:S(2)}, u32[]{:S(2)}) %collective-permute-start.1) | collective-permute-done | bytes 131104 | tf_op jit(solution)/shard_map/ppermute | solution.py:48
  25.6 1.9 %collective-permute-start.2 = (bf16[2,512,128]{2,1,0:T(8,128)(2,1)S(1)}, bf16[2,512,128]{2,1,0:T(8,128)(2,1)S(1)}, u32[]{:S(2)}, u32[]{:S(2)}) collective-permute-start(bf16[2,512,128]{2,1,0:T(8,128)(2,1)S(1)} %pad_maximum_fusion.1), channel_id=1, source_target_pairs={{0,256},{256,0},{1,257},{257,1},{2,258},{258,2},{3,259},{259,3},{4... | collective-permute-start | bytes 786440 | tf_op jit(solution)/shard_map/ppermute | solution.py:135
  27.6 0.0 collective-permute-done.3
  27.6 1.4 collective-permute-done.2
  29.1 0.9 maximum_maximum_fusion
  30.0 0.8 fusion.14
  30.8 0.7 fusion
  31.5 1.0 fusion.11
  32.6 0.1 copy.25
  32.7 7.0 %collective-permute-start.4 = (bf16[128,1024]{1,0:T(8,128)(2,1)S(1)}, bf16[128,1024]{1,0:T(8,128)(2,1)S(1)}, u32[]{:S(2)}, u32[]{:S(2)}) collective-permute-start(bf16[128,1024]{1,0:T(8,128)(2,1)S(1)} %copy.25), channel_id=1, source_target_pairs={{0,0},{8,8},{256,16},{264,24},{16,256},{24,264},{272,272},{280,280... | collective-permute-start | bytes 786440 | tf_op jit(solution)/shard_map/ppermute | solution.py:142
  39.7 1.9 %collective-permute-start.5 = (bf16[128,1024]{1,0:T(8,128)(2,1)S(1)}, bf16[128,1024]{1,0:T(8,128)(2,1)S(1)}, u32[]{:S(2)}, u32[]{:S(2)}) collective-permute-start(bf16[128,1024]{1,0:T(8,128)(2,1)S(1)} %copy.25), channel_id=1, source_target_pairs={{8,0},{256,8},{264,16},{0,24},{24,256},{272,264},{280,272},{16,280... | collective-permute-start | bytes 786440 | tf_op jit(solution)/shard_map/ppermute | solution.py:142
  41.6 3.3 %collective-permute-start.6 = (bf16[128,1024]{1,0:T(8,128)(2,1)S(1)}, bf16[128,1024]{1,0:T(8,128)(2,1)S(1)}, u32[]{:S(2)}, u32[]{:S(2)}) collective-permute-start(bf16[128,1024]{1,0:T(8,128)(2,1)S(1)} %copy.25), channel_id=1, source_target_pairs={{256,0},{264,8},{0,16},{8,24},{272,256},{280,264},{16,272},{24,280... | collective-permute-start | bytes 786440 | tf_op jit(solution)/shard_map/ppermute | solution.py:142
  45.0 3.5 %collective-permute-start.7 = (bf16[128,1024]{1,0:T(8,128)(2,1)S(1)}, bf16[128,1024]{1,0:T(8,128)(2,1)S(1)}, u32[]{:S(2)}, u32[]{:S(2)}) collective-permute-start(bf16[128,1024]{1,0:T(8,128)(2,1)S(1)} %copy.25), channel_id=1, source_target_pairs={{264,0},{0,8},{8,16},{256,24},{280,256},{16,264},{24,272},{272,280... | collective-permute-start | bytes 786440 | tf_op jit(solution)/shard_map/ppermute | solution.py:142
  48.4 0.1 pad_add_fusion.place_ref
  48.5 15.8 %collective-permute-done.4 = bf16[128,1024]{1,0:T(8,128)(2,1)S(1)} collective-permute-done((bf16[128,1024]{1,0:T(8,128)(2,1)S(1)}, bf16[128,1024]{1,0:T(8,128)(2,1)S(1)}, u32[]{:S(2)}, u32[]{:S(2)}) %collective-permute-start.4) | collective-permute-done | bytes 262176 | tf_op jit(solution)/shard_map/ppermute | solution.py:142
  64.3 21.4 %collective-permute-done.5 = bf16[128,1024]{1,0:T(8,128)(2,1)S(1)} collective-permute-done((bf16[128,1024]{1,0:T(8,128)(2,1)S(1)}, bf16[128,1024]{1,0:T(8,128)(2,1)S(1)}, u32[]{:S(2)}, u32[]{:S(2)}) %collective-permute-start.5) | collective-permute-done | bytes 262176 | tf_op jit(solution)/shard_map/ppermute | solution.py:142
  85.7 0.0 collective-permute-done.6
  85.7 0.0 collective-permute-done.7
  85.7 0.1 pad_maximum_fusion.left_ref
  85.8 0.2 all-gather.3.cloned.1.call-done
  86.0 0.0 copy-start
  86.0 2.2 %copy-done = bf16[1,8192,256]{2,1,0:T(8,128)(2,1)S(1)} copy-done((bf16[1,8192,256]{2,1,0:T(8,128)(2,1)S(1)}, bf16[1,8192,256]{2,1,0:T(8,128)(2,1)}, u32[]{:S(2)}) %copy-start) | copy-done | bytes 4194328
  88.2 5.6 %shard_map.55 = bf16[8,2,2,128,256]{4,3,2,1,0:T(8,128)(2,1)} custom-call(s32[2]{0:T(128)S(1)} %pad_add_fusion.place_ref, bf16[4,128,1024]{2,1,0:T(8,128)(2,1)S(1)} %pad_maximum_fusion.left_ref, bf16[8,2,512,256]{3,2,1,0:T(8,128)(2,1)S(1)} %bitcast.45), custom_call_target="tpu_custom_call" | custom-call | flops 2147483648 | bytes 7340032 | tf_op jit(solution)/shard_map/pallas_call | solution.py:77
  93.8 0.0 reduce-scatter.2.cloned.1.call-update
  93.8 42.3 %reduce-scatter.2.cloned.1.call-done = bf16[1,512,256]{2,1,0:T(8,128)(2,1)} async-done(((bf16[8,512,256]{2,1,0:T(8,128)(2,1)}), bf16[1,512,256]{2,1,0:T(8,128)(2,1)}) %reduce-scatter.2.cloned.1.call-update) | async-done | bytes 262160 | tf_op jit(solution)/shard_map/reduce_scatter | solution.py:146
  136.1 1.0 slice_bitcast_fusion.5
  137.1 8.9 %collective-permute-start.8 = (bf16[256,256]{1,0:T(8,128)(2,1)S(1)}, bf16[256,256]{1,0:T(8,128)(2,1)S(1)}, u32[]{:S(2)}, u32[]{:S(2)}) collective-permute-start(bf16[256,256]{1,0:T(8,128)(2,1)S(1)} %get-tuple-element.7), channel_id=1, source_target_pairs={{0,8},{1,9},{2,10},{3,11},{4,12},{5,13},{6,14},{7,15},{32,40},{33,... | collective-permute-start | bytes 393224 | tf_op jit(solution)/shard_map/ppermute | solution.py:148
  146.0 2.6 %collective-permute-start.9 = (bf16[256,256]{1,0:T(8,128)(2,1)S(1)}, bf16[256,256]{1,0:T(8,128)(2,1)S(1)}, u32[]{:S(2)}, u32[]{:S(2)}) collective-permute-start(bf16[256,256]{1,0:T(8,128)(2,1)S(1)} %get-tuple-element.8), channel_id=1, source_target_pairs={{0,0},{1,1},{2,2},{3,3},{4,4},{5,5},{6,6},{7,7},{32,32},{33,33},{3... | collective-permute-start | bytes 393224 | tf_op jit(solution)/shard_map/ppermute | solution.py:148
  148.7 0.0 collective-permute-done.8
  148.7 5.1 %collective-permute-done.9 = bf16[256,256]{1,0:T(8,128)(2,1)S(1)} collective-permute-done((bf16[256,256]{1,0:T(8,128)(2,1)S(1)}, bf16[256,256]{1,0:T(8,128)(2,1)S(1)}, u32[]{:S(2)}, u32[]{:S(2)}) %collective-permute-start.9) | collective-permute-done | bytes 131104 | tf_op jit(solution)/shard_map/ppermute | solution.py:148
  153.8 0.7 pad_maximum_fusion.3
  (7 shorter events, 0.1 us)
Async XLA Ops:
  6.5 79.5 %all-gather.3.cloned.1.call-start = ((), (), s32[]{:S(2)}) async-start(), calls=%async_computation.2 | async-start | bytes 4456448 | tf_op jit(solution)/shard_map/all_gather | solution.py:126
  7.3 128.8 %reduce-scatter.2.cloned.1.call-start = ((), (), s32[]{:S(2)}) async-start(), calls=%async_computation.1 | async-start | bytes 2359296 | tf_op jit(solution)/shard_map/reduce_scatter | solution.py:146
  8.2 15.3 %collective-permute-start = (bf16[2,256,128]{2,1,0:T(8,128)(2,1)S(1)}, bf16[2,256,128]{2,1,0:T(8,128)(2,1)S(1)}, u32[]{:S(2)}, u32[]{:S(2)}) collective-permute-start(bf16[2,256,128]{2,1,0:T(8,128)(2,1)S(1)} %pad_maximum_fusion.4), channel_id=1, source_target_pairs={{0,1},{1,2},{2,3},{3,4},{4,5},{5,6},{6,7},{7,8},{8,9},{9,10},{10,1... | collective-permute-start | bytes 393224 | tf_op jit(solution)/shard_map/ppermute | solution.py:48
  14.3 11.3 %collective-permute-start.1 = (bf16[2,256,128]{2,1,0:T(8,128)(2,1)S(1)}, bf16[2,256,128]{2,1,0:T(8,128)(2,1)S(1)}, u32[]{:S(2)}, u32[]{:S(2)}) collective-permute-start(bf16[2,256,128]{2,1,0:T(8,128)(2,1)S(1)} %pad_maximum_fusion.4), channel_id=1, source_target_pairs={{0,2},{1,3},{2,4},{3,5},{4,6},{5,7},{6,8},{7,9},{8,10},{9,11},{10,... | collective-permute-start | bytes 393224 | tf_op jit(solution)/shard_map/ppermute | solution.py:48
  20.2 7.4 %collective-permute-start.3 = (bf16[128,512]{0,1:T(8,128)(2,1)S(1)}, bf16[128,512]{0,1:T(8,128)(2,1)S(1)}, u32[]{:S(2)}, u32[]{:S(2)}) collective-permute-start(bf16[128,512]{0,1:T(8,128)(2,1)S(1)} %bitcast.56), channel_id=1, source_target_pairs={{0,256},{256,0},{1,257},{257,1},{2,258},{258,2},{3,259},{259,3},{4... | collective-permute-start | bytes 393224 | tf_op jit(solution)/shard_map/ppermute | solution.py:134
  25.6 3.4 %collective-permute-start.2 = (bf16[2,512,128]{2,1,0:T(8,128)(2,1)S(1)}, bf16[2,512,128]{2,1,0:T(8,128)(2,1)S(1)}, u32[]{:S(2)}, u32[]{:S(2)}) collective-permute-start(bf16[2,512,128]{2,1,0:T(8,128)(2,1)S(1)} %pad_maximum_fusion.1), channel_id=1, source_target_pairs={{0,256},{256,0},{1,257},{257,1},{2,258},{258,2},{3,259},{259,3},{4... | collective-permute-start | bytes 786440 | tf_op jit(solution)/shard_map/ppermute | solution.py:135
  32.7 31.5 %collective-permute-start.4 = (bf16[128,1024]{1,0:T(8,128)(2,1)S(1)}, bf16[128,1024]{1,0:T(8,128)(2,1)S(1)}, u32[]{:S(2)}, u32[]{:S(2)}) collective-permute-start(bf16[128,1024]{1,0:T(8,128)(2,1)S(1)} %copy.25), channel_id=1, source_target_pairs={{0,0},{8,8},{256,16},{264,24},{16,256},{24,264},{272,272},{280,280... | collective-permute-start | bytes 786440 | tf_op jit(solution)/shard_map/ppermute | solution.py:142
  39.7 46.0 %collective-permute-start.5 = (bf16[128,1024]{1,0:T(8,128)(2,1)S(1)}, bf16[128,1024]{1,0:T(8,128)(2,1)S(1)}, u32[]{:S(2)}, u32[]{:S(2)}) collective-permute-start(bf16[128,1024]{1,0:T(8,128)(2,1)S(1)} %copy.25), channel_id=1, source_target_pairs={{8,0},{256,8},{264,16},{0,24},{24,256},{272,264},{280,272},{16,280... | collective-permute-start | bytes 786440 | tf_op jit(solution)/shard_map/ppermute | solution.py:142
  41.6 44.1 %collective-permute-start.6 = (bf16[128,1024]{1,0:T(8,128)(2,1)S(1)}, bf16[128,1024]{1,0:T(8,128)(2,1)S(1)}, u32[]{:S(2)}, u32[]{:S(2)}) collective-permute-start(bf16[128,1024]{1,0:T(8,128)(2,1)S(1)} %copy.25), channel_id=1, source_target_pairs={{256,0},{264,8},{0,16},{8,24},{272,256},{280,264},{16,272},{24,280... | collective-permute-start | bytes 786440 | tf_op jit(solution)/shard_map/ppermute | solution.py:142
  45.0 40.7 %collective-permute-start.7 = (bf16[128,1024]{1,0:T(8,128)(2,1)S(1)}, bf16[128,1024]{1,0:T(8,128)(2,1)S(1)}, u32[]{:S(2)}, u32[]{:S(2)}) collective-permute-start(bf16[128,1024]{1,0:T(8,128)(2,1)S(1)} %copy.25), channel_id=1, source_target_pairs={{264,0},{0,8},{8,16},{256,24},{280,256},{16,264},{24,272},{272,280... | collective-permute-start | bytes 786440 | tf_op jit(solution)/shard_map/ppermute | solution.py:142
  86.0 2.2 %copy-start = (bf16[1,8192,256]{2,1,0:T(8,128)(2,1)S(1)}, bf16[1,8192,256]{2,1,0:T(8,128)(2,1)}, u32[]{:S(2)}) copy-start(bf16[1,8192,256]{2,1,0:T(8,128)(2,1)} %all-gather.3.cloned.1.call-done) | copy-start | bytes 12582916
  137.1 11.6 %collective-permute-start.8 = (bf16[256,256]{1,0:T(8,128)(2,1)S(1)}, bf16[256,256]{1,0:T(8,128)(2,1)S(1)}, u32[]{:S(2)}, u32[]{:S(2)}) collective-permute-start(bf16[256,256]{1,0:T(8,128)(2,1)S(1)} %get-tuple-element.7), channel_id=1, source_target_pairs={{0,8},{1,9},{2,10},{3,11},{4,12},{5,13},{6,14},{7,15},{32,40},{33,... | collective-permute-start | bytes 393224 | tf_op jit(solution)/shard_map/ppermute | solution.py:148
  146.0 7.8 %collective-permute-start.9 = (bf16[256,256]{1,0:T(8,128)(2,1)S(1)}, bf16[256,256]{1,0:T(8,128)(2,1)S(1)}, u32[]{:S(2)}, u32[]{:S(2)}) collective-permute-start(bf16[256,256]{1,0:T(8,128)(2,1)S(1)} %get-tuple-element.8), channel_id=1, source_target_pairs={{0,0},{1,1},{2,2},{3,3},{4,4},{5,5},{6,6},{7,7},{32,32},{33,33},{3... | collective-permute-start | bytes 393224 | tf_op jit(solution)/shard_map/ppermute | solution.py:148
Sparse Core Ops, SparseCore 0:
  9.4 76.5 all-gather.2
  93.9 42.1 reduce-scatter.1

commit v13 on v11

--- a/solution.py
+++ b/solution.py
@@ -82,7 +82,7 @@
         product_kernel,
         grid_spec=grid_spec,
         out_shape=jax.ShapeDtypeStruct((tiles * blocks // 2, 2, tokens, 2 * width), jnp.bfloat16),
-        compiler_params=pltpu.CompilerParams(vmem_limit_bytes=40 * 2**20),
+        compiler_params=pltpu.CompilerParams(vmem_limit_bytes=56 * 2**20),
         cost_estimate=pl.CostEstimate(
             flops=2 * blocks * tokens * right.size,
             bytes_accessed=2 * (left.size + right.size + tiles * blocks * tokens * 2 * width),

time: 137 us -> 138 us (level)
  Pallas kernels: 4.41 us -> 6.76 us
  local copies, waits for them, and re-layouts: 4.35 us -> 2.16 us
  other arithmetic: 3.95 us -> 5.53 us
  waiting for transfers between devices: 82.4 us -> 80.9 us
    pallas_call x1, Pallas kernels: 4.41 us -> 6.76 us  [product(): pl.pallas_call(product_kernel, grid_spec=grid_spec, out_shape=jax.ShapeDt...]
    unnamed x3 -> x1, local copies, waits for them, and re-layouts: 2.89 us -> 0.7 us
  transfers between devices with their start and end apart: 11 -> 11, of which waited for: 7 -> 7; matrix products, arithmetic and copies ran while one was open for 5% -> 6% of each run, Pallas kernels for 0% -> 0%
where the time goes in v13:
time: 138 us; the launch traced here: 137 us
  waiting for transfers between devices  80.9 us (59%)
  starting transfers between devices  26.3 us (19%)
  between operations  13.6 us (10%)
  Pallas kernels  6.76 us (5%)
  other arithmetic  5.53 us (4%)
  local copies, waits for them, and re-layouts  2.16 us (2%)
  matrix products  1.86 us (1%)
    reduce_scatter x1, waiting for transfers between devices, on_device(): tile = lax.psum_scatter(partial, 'kv', scatter_dimension=0)  45.7 us
    ppermute x1, waiting for transfers between devices, on_device(): return lax.ppermute(tile, ALL, to_owner)  16.5 us
    ppermute x4, starting transfers between devices, on_device(): lax.ppermute(heads, ('grp', 'sx'), to_rows[b])  10.1 us
    ppermute x2, starting transfers between devices, fetch_behind(): return lax.ppermute(stacked, ('grp', 'sx', 'sy'), route)  7.98 us
    ppermute x4, waiting for transfers between devices, on_device(): lax.ppermute(heads, ('grp', 'sx'), to_rows[b])  7.69 us
    pallas_call x1, Pallas kernels, product(): pl.pallas_call(product_kernel, grid_spec=grid_spec, out_shape=jax.ShapeDt...  6.76 us
    all_gather x1, waiting for transfers between devices, on_device(): columns = lax.all_gather(weight[0], ('sy', 'grp'), axis=0, tiled=True)  5.34 us
    ppermute x2, waiting for transfers between devices, fetch_behind(): return lax.ppermute(stacked, ('grp', 'sx', 'sy'), route)  3.87 us
  transfers between devices with their start and end apart: 11, of which 7 were waited for; matrix products, arithmetic and copies ran while one was open for 6% of the time, Pallas kernels for 0%

profile of v13, /device:TPU:6, one launch (start us, length us, event | category | flops | bytes accessed | tf_op | source)
XLA Modules:
  0.0 137.1 jit_solution(6906279144382436180)
XLA Ops:
  6.5 0.0 all-gather.3.cloned.1.call-start
  6.5 0.7 all-gather.3.cloned.1.call-update
  7.3 0.0 reduce-scatter.2.cloned.1.call-start
  7.3 0.9 pad_maximum_fusion.3
  8.2 3.5 %collective-permute-start = (bf16[2,256,128]{2,1,0:T(8,128)(2,1)S(1)}, bf16[2,256,128]{2,1,0:T(8,128)(2,1)S(1)}, u32[]{:S(2)}, u32[]{:S(2)}) collective-permute-start(bf16[2,256,128]{2,1,0:T(8,128)(2,1)S(1)} %pad_maximum_fusion.3), channel_id=1, source_target_pairs={{0,1},{1,2},{2,3},{3,4},{4,5},{5,6},{6,7},{7,8},{8,9},{9,10},{10,1... | collective-permute-start | bytes 393224 | tf_op jit(solution)/shard_map/ppermute | solution.py:48
  11.7 4.5 %collective-permute-start.1 = (bf16[2,256,128]{2,1,0:T(8,128)(2,1)S(1)}, bf16[2,256,128]{2,1,0:T(8,128)(2,1)S(1)}, u32[]{:S(2)}, u32[]{:S(2)}) collective-permute-start(bf16[2,256,128]{2,1,0:T(8,128)(2,1)S(1)} %pad_maximum_fusion.3), channel_id=1, source_target_pairs={{0,2},{1,3},{2,4},{3,5},{4,6},{5,7},{6,8},{7,9},{8,10},{9,11},{10,... | collective-permute-start | bytes 393224 | tf_op jit(solution)/shard_map/ppermute | solution.py:48
  16.2 1.0 constant_dynamic-slice_fusion.1
  17.2 0.1 copy.16
  17.3 3.7 %collective-permute-start.3 = (bf16[128,512]{0,1:T(8,128)(2,1)S(1)}, bf16[128,512]{0,1:T(8,128)(2,1)S(1)}, u32[]{:S(2)}, u32[]{:S(2)}) collective-permute-start(bf16[128,512]{0,1:T(8,128)(2,1)S(1)} %bitcast.53), channel_id=1, source_target_pairs={{0,256},{256,0},{1,257},{257,1},{2,258},{258,2},{3,259},{259,3},{4... | collective-permute-start | bytes 393224 | tf_op jit(solution)/shard_map/ppermute | solution.py:134
  21.1 0.1 stack.50
  21.2 0.1 iota_add_fusion
  21.3 0.8 select_reduce_fusion.1
  22.0 0.1 select_reduce_fusion
  22.1 0.2 compare_and_fusion
  22.4 0.1 copy.15
  22.5 0.0 collective-permute-done
  22.5 3.9 %collective-permute-done.1 = bf16[2,256,128]{2,1,0:T(8,128)(2,1)S(1)} collective-permute-done((bf16[2,256,128]{2,1,0:T(8,128)(2,1)S(1)}, bf16[2,256,128]{2,1,0:T(8,128)(2,1)S(1)}, u32[]{:S(2)}, u32[]{:S(2)}) %collective-permute-start.1) | collective-permute-done | bytes 131104 | tf_op jit(solution)/shard_map/ppermute | solution.py:48
  26.4 2.5 %collective-permute-start.2 = (bf16[2,512,128]{2,1,0:T(8,128)(2,1)S(1)}, bf16[2,512,128]{2,1,0:T(8,128)(2,1)S(1)}, u32[]{:S(2)}, u32[]{:S(2)}) collective-permute-start(bf16[2,512,128]{2,1,0:T(8,128)(2,1)S(1)} %pad_maximum_fusion.1), channel_id=1, source_target_pairs={{0,256},{256,0},{1,257},{257,1},{2,258},{258,2},{3,259},{259,3},{4... | collective-permute-start | bytes 786440 | tf_op jit(solution)/shard_map/ppermute | solution.py:135
  28.9 0.0 collective-permute-done.3
  29.0 1.1 collective-permute-done.2
  30.0 0.9 maximum_maximum_fusion
  31.0 0.8 fusion.14
  31.8 0.7 fusion
  32.5 1.0 fusion.11
  33.5 0.1 copy.25
  33.7 0.7 collective-permute-start.4
  34.4 2.2 %collective-permute-start.5 = (bf16[128,1024]{1,0:T(8,128)(2,1)S(1)}, bf16[128,1024]{1,0:T(8,128)(2,1)S(1)}, u32[]{:S(2)}, u32[]{:S(2)}) collective-permute-start(bf16[128,1024]{1,0:T(8,128)(2,1)S(1)} %copy.25), channel_id=1, source_target_pairs={{256,0},{264,8},{272,16},{280,24},{8,256},{16,264},{24,272},{0,280... | collective-permute-start | bytes 786440 | tf_op jit(solution)/shard_map/ppermute | solution.py:142
  36.5 5.4 %collective-permute-start.6 = (bf16[128,1024]{1,0:T(8,128)(2,1)S(1)}, bf16[128,1024]{1,0:T(8,128)(2,1)S(1)}, u32[]{:S(2)}, u32[]{:S(2)}) collective-permute-start(bf16[128,1024]{1,0:T(8,128)(2,1)S(1)} %copy.25), channel_id=1, source_target_pairs={{16,0},{24,8},{0,16},{8,24},{280,256},{256,264},{264,272},{272,280... | collective-permute-start | bytes 786440 | tf_op jit(solution)/shard_map/ppermute | solution.py:142
  41.9 1.9 %collective-permute-start.7 = (bf16[128,1024]{1,0:T(8,128)(2,1)S(1)}, bf16[128,1024]{1,0:T(8,128)(2,1)S(1)}, u32[]{:S(2)}, u32[]{:S(2)}) collective-permute-start(bf16[128,1024]{1,0:T(8,128)(2,1)S(1)} %copy.25), channel_id=1, source_target_pairs={{272,0},{280,8},{256,16},{264,24},{24,256},{0,264},{8,272},{16,280... | collective-permute-start | bytes 786440 | tf_op jit(solution)/shard_map/ppermute | solution.py:142
  43.9 0.7 pad_add_fusion.place_ref
  44.5 0.0 collective-permute-done.4
  44.5 0.0 collective-permute-done.5
  44.5 2.8 %collective-permute-done.6 = bf16[128,1024]{1,0:T(8,128)(2,1)S(1)} collective-permute-done((bf16[128,1024]{1,0:T(8,128)(2,1)S(1)}, bf16[128,1024]{1,0:T(8,128)(2,1)S(1)}, u32[]{:S(2)}, u32[]{:S(2)}) %collective-permute-start.6) | collective-permute-done | bytes 262176 | tf_op jit(solution)/shard_map/ppermute | solution.py:142
  47.3 4.9 %collective-permute-done.7 = bf16[128,1024]{1,0:T(8,128)(2,1)S(1)} collective-permute-done((bf16[128,1024]{1,0:T(8,128)(2,1)S(1)}, bf16[128,1024]{1,0:T(8,128)(2,1)S(1)}, u32[]{:S(2)}, u32[]{:S(2)}) %collective-permute-start.7) | collective-permute-done | bytes 262176 | tf_op jit(solution)/shard_map/ppermute | solution.py:142
  52.2 1.1 pad_maximum_fusion.left_ref
  53.3 5.3 %all-gather.3.cloned.1.call-done = bf16[1,8192,256]{2,1,0:T(8,128)(2,1)} async-done(((bf16[1,512,256]{2,1,0:T(8,128)(2,1)}), bf16[1,8192,256]{2,1,0:T(8,128)(2,1)}) %all-gather.3.cloned.1.call-update) | async-done | bytes 4194320 | tf_op jit(solution)/shard_map/all_gather | solution.py:126
  58.7 6.8 %shard_map.55 = bf16[8,2,128,512]{3,2,1,0:T(8,128)(2,1)} custom-call(s32[2]{0:T(128)} %pad_add_fusion.place_ref, bf16[4,128,1024]{2,1,0:T(8,128)(2,1)} %pad_maximum_fusion.left_ref, bf16[8,2,512,256]{3,2,1,0:T(8,128)(2,1)} %bitcast.55), custom_call_target="tpu_custom_call" | custom-call | flops 2147483648 | bytes 7340032 | tf_op jit(solution)/shard_map/pallas_call | solution.py:81
  65.4 0.0 reduce-scatter.2.cloned.1.call-update
  65.5 45.7 %reduce-scatter.2.cloned.1.call-done = bf16[1,256,512]{2,1,0:T(8,128)(2,1)} async-done(((bf16[8,256,512]{2,1,0:T(8,128)(2,1)}), bf16[1,256,512]{2,1,0:T(8,128)(2,1)}) %reduce-scatter.2.cloned.1.call-update) | async-done | bytes 262160 | tf_op jit(solution)/shard_map/reduce_scatter | solution.py:146
  111.1 1.9 %collective-permute-start.8 = (bf16[256,512]{1,0:T(8,128)(2,1)}, bf16[256,512]{1,0:T(8,128)(2,1)S(1)}, u32[]{:S(2)}, u32[]{:S(2)}) collective-permute-start(bf16[256,512]{1,0:T(8,128)(2,1)} %bitcast.56), channel_id=1, source_target_pairs={{0,32},{1,33},{2,34},{3,35},{4,36},{5,37},{6,38},{7,39},{32,48},{3... | collective-permute-start | bytes 786440 | tf_op jit(solution)/shard_map/ppermute | solution.py:147
  113.1 16.5 %collective-permute-done.8 = bf16[256,512]{1,0:T(8,128)(2,1)S(1)} collective-permute-done((bf16[256,512]{1,0:T(8,128)(2,1)}, bf16[256,512]{1,0:T(8,128)(2,1)S(1)}, u32[]{:S(2)}, u32[]{:S(2)}) %collective-permute-start.8) | collective-permute-done | bytes 262176 | tf_op jit(solution)/shard_map/ppermute | solution.py:147
  129.6 0.7 copy.27
  (6 shorter events, 0.1 us)
Async XLA Ops:
  6.5 52.1 %all-gather.3.cloned.1.call-start = ((), (), s32[]{:S(2)}) async-start(), calls=%async_computation.2 | async-start | bytes 4456448 | tf_op jit(solution)/shard_map/all_gather | solution.py:126
  7.3 103.9 %reduce-scatter.2.cloned.1.call-start = ((), (), s32[]{:S(2)}) async-start(), calls=%async_computation.1 | async-start | bytes 2359296 | tf_op jit(solution)/shard_map/reduce_scatter | solution.py:146
  8.2 14.3 %collective-permute-start = (bf16[2,256,128]{2,1,0:T(8,128)(2,1)S(1)}, bf16[2,256,128]{2,1,0:T(8,128)(2,1)S(1)}, u32[]{:S(2)}, u32[]{:S(2)}) collective-permute-start(bf16[2,256,128]{2,1,0:T(8,128)(2,1)S(1)} %pad_maximum_fusion.3), channel_id=1, source_target_pairs={{0,1},{1,2},{2,3},{3,4},{4,5},{5,6},{6,7},{7,8},{8,9},{9,10},{10,1... | collective-permute-start | bytes 393224 | tf_op jit(solution)/shard_map/ppermute | solution.py:48
  11.7 14.7 %collective-permute-start.1 = (bf16[2,256,128]{2,1,0:T(8,128)(2,1)S(1)}, bf16[2,256,128]{2,1,0:T(8,128)(2,1)S(1)}, u32[]{:S(2)}, u32[]{:S(2)}) collective-permute-start(bf16[2,256,128]{2,1,0:T(8,128)(2,1)S(1)} %pad_maximum_fusion.3), channel_id=1, source_target_pairs={{0,2},{1,3},{2,4},{3,5},{4,6},{5,7},{6,8},{7,9},{8,10},{9,11},{10,... | collective-permute-start | bytes 393224 | tf_op jit(solution)/shard_map/ppermute | solution.py:48
  17.3 11.6 %collective-permute-start.3 = (bf16[128,512]{0,1:T(8,128)(2,1)S(1)}, bf16[128,512]{0,1:T(8,128)(2,1)S(1)}, u32[]{:S(2)}, u32[]{:S(2)}) collective-permute-start(bf16[128,512]{0,1:T(8,128)(2,1)S(1)} %bitcast.53), channel_id=1, source_target_pairs={{0,256},{256,0},{1,257},{257,1},{2,258},{258,2},{3,259},{259,3},{4... | collective-permute-start | bytes 393224 | tf_op jit(solution)/shard_map/ppermute | solution.py:134
  26.4 3.6 %collective-permute-start.2 = (bf16[2,512,128]{2,1,0:T(8,128)(2,1)S(1)}, bf16[2,512,128]{2,1,0:T(8,128)(2,1)S(1)}, u32[]{:S(2)}, u32[]{:S(2)}) collective-permute-start(bf16[2,512,128]{2,1,0:T(8,128)(2,1)S(1)} %pad_maximum_fusion.1), channel_id=1, source_target_pairs={{0,256},{256,0},{1,257},{257,1},{2,258},{258,2},{3,259},{259,3},{4... | collective-permute-start | bytes 786440 | tf_op jit(solution)/shard_map/ppermute | solution.py:135
  33.7 10.8 %collective-permute-start.4 = (bf16[128,1024]{1,0:T(8,128)(2,1)S(1)}, bf16[128,1024]{1,0:T(8,128)(2,1)S(1)}, u32[]{:S(2)}, u32[]{:S(2)}) collective-permute-start(bf16[128,1024]{1,0:T(8,128)(2,1)S(1)} %copy.25), channel_id=1, source_target_pairs={{0,0},{8,8},{16,16},{24,24},{264,256},{272,264},{280,272},{256,280... | collective-permute-start | bytes 786440 | tf_op jit(solution)/shard_map/ppermute | solution.py:142
  34.4 10.1 %collective-permute-start.5 = (bf16[128,1024]{1,0:T(8,128)(2,1)S(1)}, bf16[128,1024]{1,0:T(8,128)(2,1)S(1)}, u32[]{:S(2)}, u32[]{:S(2)}) collective-permute-start(bf16[128,1024]{1,0:T(8,128)(2,1)S(1)} %copy.25), channel_id=1, source_target_pairs={{256,0},{264,8},{272,16},{280,24},{8,256},{16,264},{24,272},{0,280... | collective-permute-start | bytes 786440 | tf_op jit(solution)/shard_map/ppermute | solution.py:142
  36.5 10.7 %collective-permute-start.6 = (bf16[128,1024]{1,0:T(8,128)(2,1)S(1)}, bf16[128,1024]{1,0:T(8,128)(2,1)S(1)}, u32[]{:S(2)}, u32[]{:S(2)}) collective-permute-start(bf16[128,1024]{1,0:T(8,128)(2,1)S(1)} %copy.25), channel_id=1, source_target_pairs={{16,0},{24,8},{0,16},{8,24},{280,256},{256,264},{264,272},{272,280... | collective-permute-start | bytes 786440 | tf_op jit(solution)/shard_map/ppermute | solution.py:142
  41.9 10.3 %collective-permute-start.7 = (bf16[128,1024]{1,0:T(8,128)(2,1)S(1)}, bf16[128,1024]{1,0:T(8,128)(2,1)S(1)}, u32[]{:S(2)}, u32[]{:S(2)}) collective-permute-start(bf16[128,1024]{1,0:T(8,128)(2,1)S(1)} %copy.25), channel_id=1, source_target_pairs={{272,0},{280,8},{256,16},{264,24},{24,256},{0,264},{8,272},{16,280... | collective-permute-start | bytes 786440 | tf_op jit(solution)/shard_map/ppermute | solution.py:142
  111.1 18.4 %collective-permute-start.8 = (bf16[256,512]{1,0:T(8,128)(2,1)}, bf16[256,512]{1,0:T(8,128)(2,1)S(1)}, u32[]{:S(2)}, u32[]{:S(2)}) collective-permute-start(bf16[256,512]{1,0:T(8,128)(2,1)} %bitcast.56), channel_id=1, source_target_pairs={{0,32},{1,33},{2,34},{3,35},{4,36},{5,37},{6,38},{7,39},{32,48},{3... | collective-permute-start | bytes 786440 | tf_op jit(solution)/shard_map/ppermute | solution.py:147
Sparse Core Ops, SparseCore 0:
  9.5 49.1 all-gather.2
  65.6 45.5 reduce-scatter.1
